TPU v7x, 32 devices: a whole 2x2x4 slice. The times are simulated.
32 devices in a mesh: bank: 2 (over x), gal: 16 (over z, y, core).
Axes of the slice: x: 2, y: 2, z: 4, core: 2. Of those that a mesh axis runs over, the one named last changes fastest.
Arguments:
- bank_queries: bfloat16 [256, 768], P(('bank', 'gal'))
- gallery: bfloat16 [65536, 768], P('gal')
- test_queries: bfloat16 [128, 768], P(('bank', 'gal'))
- test_slabs: int32 [128, 8], P('bank'), may hold values from 0 to 15, all different within a row; in each aligned block of 4 rows (0 to 3, 4 to 7, ...) at most 2 rows name the same one
- test_offsets: int32 [128, 8], P('bank'), may hold values from 0 to 31
Outputs:
- pooled: float32 [128, 768], P(('bank', 'gal'))
Inputs may be any that keep to these rules, and one draw needn't show every extreme that they name: `test_slabs`: each row names 8 different slabs; the 4 rows of one device name no slab more than 2 times, and on some devices one slab exactly 2 times.
All inputs are finite; a program needn't handle non-finite values.
Results may differ from a plain program's by a relative error of at most 0.0065.
Values may be sent and summed in bfloat16 or wider, within the bound.
No kernel may reach another device: no remote copies, remote signals or barrier semaphores. Data moves between devices by JAX's collectives and lax.ppermute only.
A program may use at most 64 MiB of HBM per device.

v0:
```python
import jax
import jax.numpy as jnp
from jax import lax
from jax.sharding import PartitionSpec as P

BLOCK = 128


SHARPNESS = 20.0
epsilon = 1e-06


def row_scale(matrix):
    values = matrix.astype(jnp.float32)
    return lax.rsqrt(jnp.sum(values * values, axis=1) + epsilon)


def inner_rows(first_rows, second_rows):
    return lax.dot_general(
        first_rows, second_rows, (((1,), (1,)), ((), ())), preferred_element_type=jnp.float32
    )


def body(bank_queries, gallery, test_queries, test_slabs, test_offsets):
    gallery_rows = gallery.shape[0]
    gallery_scale = row_scale(gallery)
    portion = lax.all_gather(bank_queries, "gal", axis=0, tiled=True)
    scores = (
        SHARPNESS
        * inner_rows(portion, gallery)
        * row_scale(portion)[:, None]
        * gallery_scale[None, :]
    )
    partial_sums = jnp.sum(jnp.exp(scores), axis=0)
    colsum = lax.psum(partial_sums, "bank")
    log_col = jnp.log(colsum)
    own_rows = test_queries.shape[0]
    slab_index = lax.axis_index("gal")
    queries = lax.all_gather(test_queries, "gal", axis=0, tiled=True)
    blocks_here = gallery_rows // BLOCK
    local_blocks = jnp.arange(blocks_here, dtype=jnp.int32)
    block_hits = (test_slabs == slab_index)[:, :, None] & (
        test_offsets[:, :, None] == local_blocks[None, None, :]
    )
    listed = jnp.any(block_hits, axis=1)
    row_mask = jnp.repeat(listed, BLOCK, axis=1)
    logits = (
        SHARPNESS
        * inner_rows(queries, gallery)
        * row_scale(queries)[:, None]
        * gallery_scale[None, :]
        - log_col[None, :]
    )
    weights = jnp.where(row_mask, jnp.exp(logits), jnp.float32(0.0))
    numerator = jnp.dot(weights.astype(jnp.bfloat16), gallery, preferred_element_type=jnp.float32)
    numerator, denominator = (numerator, jnp.sum(weights, axis=1))
    numer_all, denom_all = lax.psum((numerator, denominator), "gal")
    offset = slab_index * own_rows
    numer_own = lax.dynamic_slice_in_dim(numer_all, offset, own_rows, 0)
    denom_own = lax.dynamic_slice_in_dim(denom_all, offset, own_rows, 0)
    return numer_own / denom_own[:, None]


def solution(mesh):
    in_specs = (
        P(("bank", "gal"), None),
        P("gal", None),
        P(("bank", "gal"), None),
        P("bank", None),
        P("bank", None),
    )
    out_specs = P(("bank", "gal"), None)
    return jax.shard_map(body, mesh=mesh, in_specs=in_specs, out_specs=out_specs, check_vma=False)
```

profile of v0, /device:TPU:0, one launch (start us, length us, event | category | flops | bytes accessed | tf_op | source)
XLA Modules:
  0.0 172.6 jit_solution(770654998587153810)
XLA Ops:
  6.5 0.0 copy-start.1
  6.5 0.0 copy-start
  6.5 0.0 all-reduce.2.cloned.1.call-start
  6.5 0.7 broadcast_compare_fusion
  7.3 0.7 fusion.10
  8.0 0.1 copy.10
  8.1 4.1 %multiply_reduce_fusion = f32[4096]{0:T(1024)S(1)} fusion(bf16[4096,768]{1,0:T(8,128)(2,1)} %param.6), kind=kLoop, calls=%fused_computation | loop fusion | flops 9433088 | bytes 6307840 | tf_op jit(solution)/shard_map/reduce_sum | solution.py:15
  12.2 0.0 copy-done.1
  12.2 23.4 %all-gather = bf16[16,4,768]{2,1,0:T(4,128)(2,1)S(1)} all-gather(bf16[1,4,768]{2,1,0:T(4,128)(2,1)S(1)} %bitcast.11), channel_id=1, replica_groups=mesh['bank'=2,'gal'=16] {'gal'}, dimensions={0}, use_global_device_ids=true | all-gather | bytes 104448 | tf_op jit(solution)/shard_map/all_gather | solution.py:39
  35.6 0.1 multiply_reduce_fusion.2
  35.7 0.0 copy-done
  35.7 18.0 %all_gather.7 = bf16[128,768]{1,0:T(8,128)(2,1)S(1)} all-gather(bf16[8,768]{1,0:T(8,128)(2,1)S(1)} %copy-done), channel_id=1, replica_groups=mesh['bank'=2,'gal'=16] {'gal'}, dimensions={0}, use_global_device_ids=true | all-gather | bytes 208896 | tf_op jit(solution)/shard_map/all_gather | solution.py:27
  53.7 0.1 multiply_reduce_fusion.1
  53.8 5.0 %fusion.6 = f32[4096]{0:T(1024)S(1)} fusion(bf16[128,768]{1,0:T(8,128)(2,1)S(1)} %all_gather.7, bf16[4096,768]{1,0:T(8,128)(2,1)} %param.6, f32[4096]{0:T(1024)S(1)} %add_rsqrt_fusion, f32[128]{0:T(128)S(1)} %rsqrt_multiply_fusion), kind=kOutput, calls=%fused_computation.9 | convolution fusion | flops 806875136 | bytes 6521344 | tf_op jit(solution)/shard_map/dot_general | solution.py:19
  58.8 8.2 %psum.21 = f32[4096]{0:T(1024)S(1)} all-reduce(f32[4096]{0:T(1024)S(1)} %fusion.6), channel_id=1, replica_groups=mesh['bank'=2,'gal'=16] {'bank'}, use_global_device_ids=true, to_apply=%region_5.0 | all-reduce | flops 4096 | bytes 32768 | tf_op jit(solution)/shard_map/psum | solution.py:35
  67.0 0.3 broadcast_in_dim.5
  67.3 4.9 %fusion.11 = (f32[64]{0:T(128)S(1)}, bf16[64,4096]{1,0:T(8,128)(2,1)S(1)}) fusion(f32[4096]{0:T(1024)S(1)} %log.3, f32[4096]{0:T(1024)S(1)} %add_rsqrt_fusion, f32[64]{0:T(128)S(1)} %rsqrt_multiply_fusion.1, bf16[64,768]{1,0:T(8,128)(2,1)S(1)} %reshape.21, bf16[4096,768]{1,0:T(8,128)(2,1)} %param.6, pred[8,8,32,128]{3,2,1,0:T(32,128)(4,1)S(1)} %bitcast.10), kind=kOutput, calls=%fused_computation.22 | convolution fusion | flops 404225984 | bytes 7209472 | tf_op jit(solution)/shard_map/dot_general | solution.py:19
  72.3 4.7 %fusion.7 = f32[64,768]{1,0:T(8,128)} fusion(bf16[4096,768]{1,0:T(8,128)(2,1)} %param.6, bf16[64,4096]{1,0:T(8,128)(2,1)S(1)} %get-tuple-element.6), kind=kOutput, calls=%fused_computation.10 | convolution fusion | flops 402653184 | bytes 7012352 | tf_op jit(solution)/shard_map/dot_general | solution.py:55
  77.0 0.0 all-reduce.2.cloned.1.call-update
  77.0 29.5 %psum.23 = f32[64]{0:T(128)S(1)} all-reduce(f32[64]{0:T(128)S(1)} %get-tuple-element.5), channel_id=1, replica_groups=mesh['bank'=2,'gal'=16] {'gal'}, use_global_device_ids=true, to_apply=%region_8.9 | all-reduce | flops 64 | bytes 512 | tf_op jit(solution)/shard_map/psum | solution.py:57
  106.5 0.1 dynamic_slice.7
  106.6 57.8 %all-reduce.2.cloned.1.call-done = f32[64,768]{1,0:T(8,128)} async-done(((f32[64,768]{1,0:T(8,128)}), f32[64,768]{1,0:T(8,128)}) %all-reduce.2.cloned.1.call-update) | async-done | bytes 196624 | tf_op jit(solution)/shard_map/psum | solution.py:57
  164.3 1.4 dynamic-slice_divide_fusion
  (5 shorter events, 0.1 us)
Async XLA Ops:
  6.5 5.7 %copy-start.1 = (bf16[4,768]{1,0:T(4,128)(2,1)S(1)}, bf16[4,768]{1,0:T(4,128)(2,1)}, u32[]{:S(2)}) copy-start(bf16[4,768]{1,0:T(4,128)(2,1)} %param.7) | copy-start | bytes 18436
  6.5 29.2 %copy-start = (bf16[8,768]{1,0:T(8,128)(2,1)S(1)}, bf16[8,768]{1,0:T(8,128)(2,1)}, u32[]{:S(2)}) copy-start(bf16[8,768]{1,0:T(8,128)(2,1)} %param.5) | copy-start | bytes 36868
  6.5 157.8 %all-reduce.2.cloned.1.call-start = ((), (), s32[]{:S(2)}) async-start(), calls=%async_computation | async-start | bytes 393216 | tf_op jit(solution)/shard_map/psum | solution.py:57
Sparse Core Ops, SparseCore 0:
  77.1 87.1 all-reduce.1
where the time goes:
time: 173 us
  blocking collectives  79 us (46%)
  waiting for transfers between devices  57.8 us (33%)
  matrix products  14.6 us (8%)
  between operations  13.4 us (8%)
  other arithmetic  7.2 us (4%)
    psum x1, waiting for transfers between devices, body(): numer_all, denom_all = lax.psum((numerator, denominator), 'gal')  57.8 us
    psum x1, blocking collectives, body(): numer_all, denom_all = lax.psum((numerator, denominator), 'gal')  29.5 us
    all_gather x1, blocking collectives, body(): queries = lax.all_gather(test_queries, 'gal', axis=0, tiled=True)  23.4 us
    all_gather x1, blocking collectives, body(): portion = lax.all_gather(bank_queries, 'gal', axis=0, tiled=True)  18 us
    dot_general x2, matrix products, inner_rows(): lax.dot_general(first_rows, second_rows, (((1,), (1,)), ((), ())), prefer...  9.93 us
    psum x1, blocking collectives, body(): colsum = lax.psum(partial_sums, 'bank')  8.16 us
    dot_general x1, matrix products, body(): jnp.dot(weights.astype(jnp.bfloat16), gallery, preferred_element_type=jnp...  4.67 us
    reduce_sum x3, other arithmetic, row_scale(): return lax.rsqrt(jnp.sum(values * values, axis=1) + epsilon)  4.33 us
  transfers between devices with their start and end apart: 1, of which 1 were waited for; matrix products, arithmetic and copies ran while one was open for 0% of the time, Pallas kernels for 0%

commit v1 on v0

v1 whole, which is shorter than its diff:
```python
import functools

import jax
import jax.numpy as jnp
import numpy as np
from jax import lax
from jax.experimental import pallas as pl
from jax.experimental.pallas import tpu as pltpu
from jax.sharding import PartitionSpec as P

BLOCK = 128
CHUNKS = 8
LANES = 128
SHARPNESS = 20.0
LOG2E = 1.4426950408889634
epsilon = 1e-06

VMEM = pl.BlockSpec(memory_space=pltpu.VMEM)
SMEM = pl.BlockSpec(memory_space=pltpu.SMEM)
PARAMS = pltpu.CompilerParams(vmem_limit_bytes=24 << 20)


def keep(value):
    return pltpu.with_memory_space_constraint(value, pltpu.VMEM)


def load_kernel(gallery_hbm, gallery_ref, scale_ref, sems):
    rows, depth = gallery_hbm.shape
    part = rows // CHUNKS
    copies = [
        pltpu.make_async_copy(
            gallery_hbm.at[pl.ds(c * part, part)], gallery_ref.at[pl.ds(c * part, part)], sems.at[c]
        )
        for c in range(CHUNKS)
    ]
    for copy in copies:
        copy.start()
    for c in range(CHUNKS):
        copies[c].wait()
        values = gallery_ref[pl.ds(c * part, part), :].astype(jnp.float32)
        squares = values * values
        folded = squares[:, :LANES]
        for k in range(1, depth // LANES):
            folded = folded + squares[:, k * LANES : (k + 1) * LANES]
        for b in range(part // BLOCK):
            total = jnp.sum(folded[b * BLOCK : (b + 1) * BLOCK].T, axis=0, keepdims=True)
            scale_ref[c : c + 1, b * BLOCK : (b + 1) * BLOCK] = lax.rsqrt(total + epsilon)


def load(gallery):
    rows, _ = gallery.shape
    return pl.pallas_call(
        load_kernel,
        out_shape=(
            pltpu.VMEM(gallery.shape, gallery.dtype),
            pltpu.VMEM((CHUNKS, rows // CHUNKS), jnp.float32),
        ),
        in_specs=[pl.BlockSpec(memory_space=pl.ANY)],
        out_specs=(VMEM, VMEM),
        scratch_shapes=[pltpu.SemaphoreType.DMA((CHUNKS,))],
        compiler_params=PARAMS,
        name="load",
    )(gallery)


def score_kernel(bank_rows, query_ref, gallery_ref, scale_ref, block_ref, colsum_ref, listed_ref):
    queries = query_ref[...]
    wide = queries.astype(jnp.float32)
    query_scale = lax.rsqrt(jnp.sum(wide * wide, axis=1, keepdims=True) + epsilon) * (SHARPNESS * LOG2E)
    test_rows = queries.shape[0] - bank_rows
    part = gallery_ref.shape[0] // CHUNKS
    block = block_ref[...]
    picked = jnp.zeros((test_rows, BLOCK), jnp.float32)
    for c in range(CHUNKS):
        scores = lax.dot_general(
            queries,
            gallery_ref[pl.ds(c * part, part), :],
            (((1,), (1,)), ((), ())),
            preferred_element_type=jnp.float32,
        )
        scores = scores * scale_ref[c : c + 1, :]
        exps = jnp.exp2(scores[:bank_rows] * query_scale[:bank_rows])
        colsum_ref[c : c + 1, :] = jnp.sum(exps, axis=0, keepdims=True)
        for b in range(part // BLOCK):
            here = scores[bank_rows:, b * BLOCK : (b + 1) * BLOCK]
            picked = jnp.where(block == c * (part // BLOCK) + b, here, picked)
    listed_ref[...] = jnp.exp2(picked * query_scale[bank_rows:])


def score(queries, gallery, scale, block, bank_rows):
    test_rows = queries.shape[0] - bank_rows
    return pl.pallas_call(
        functools.partial(score_kernel, bank_rows),
        out_shape=(pltpu.VMEM(scale.shape, jnp.float32), pltpu.VMEM((test_rows, BLOCK), jnp.float32)),
        in_specs=[VMEM] * 4,
        out_specs=(VMEM, VMEM),
        compiler_params=PARAMS,
        name="score",
    )(queries, keep(gallery), keep(scale), block)


def pool_kernel(order, me_ref, listed_ref, own_ref, other_ref, gallery_ref, block_ref, out_ref, weight_ref):
    block = block_ref[...]
    test_rows = block.shape[0]
    rows, depth = gallery_ref.shape
    each = rows // BLOCK // CHUNKS
    inverse = 1.0 / (own_ref[...] + other_ref[...])
    picked = jnp.zeros((test_rows, BLOCK), jnp.float32)
    for b in range(rows // BLOCK):
        c, at = b // each, (b % each) * BLOCK
        picked = jnp.where(block == b, inverse[c : c + 1, at : at + BLOCK], picked)
    weight = listed_ref[...] * picked
    total = jnp.sum(weight, axis=1, keepdims=True)
    for b in range(rows // BLOCK):
        weight_ref[:, b * BLOCK : (b + 1) * BLOCK] = jnp.where(block == b, weight, 0.0).astype(jnp.bfloat16)
    numerator = jnp.dot(weight_ref[...], gallery_ref[...], preferred_element_type=jnp.float32)
    high = total.astype(jnp.bfloat16).astype(jnp.float32)
    lane = lax.broadcasted_iota(jnp.int32, (test_rows, LANES), 1)
    tail = jnp.where(lane == 0, high, jnp.where(lane == 1, total - high, 0.0))
    own = test_rows // len(order)
    for i, bits in enumerate(order):
        to = me_ref[0] ^ bits
        out_ref[to, :, :depth] = numerator[i * own : (i + 1) * own].astype(jnp.bfloat16)
        out_ref[to, :, depth:] = tail[i * own : (i + 1) * own].astype(jnp.bfloat16)


def pool(order, me, listed, own, other, gallery, block):
    rows, depth = gallery.shape
    test_rows = listed.shape[0]
    return pl.pallas_call(
        functools.partial(pool_kernel, order),
        out_shape=pltpu.VMEM((len(order), test_rows // len(order), depth + LANES), jnp.bfloat16),
        in_specs=[SMEM] + [VMEM] * 5,
        out_specs=VMEM,
        scratch_shapes=[pltpu.VMEM((test_rows, rows), jnp.bfloat16)],
        compiler_params=PARAMS,
        name="pool",
    )(me, keep(listed), keep(own), other, keep(gallery), block)


def swap(value, axis, size, bit):
    return lax.ppermute(value, axis, [(i, i ^ bit) for i in range(size)])


def body(devices, banks, bank_queries, gallery, test_queries, test_slabs, test_offsets):
    me = lax.axis_index("gal")
    bank_own, test_own = bank_queries.shape[0], test_queries.shape[0]

    order = [0]
    bank, test = bank_queries, test_queries
    bit = devices // 2
    while bit:
        packed = jnp.concatenate([bank, test], axis=0)
        other = swap(packed, "gal", devices, bit)
        bank = jnp.concatenate([bank, other[: bank.shape[0]]], axis=0)
        test = jnp.concatenate([test, other[-test.shape[0] :]], axis=0)
        order = order + [o ^ bit for o in order]
        bit //= 2
    queries = jnp.concatenate([bank, test], axis=0)

    place = (me ^ np.array(order, np.int32))[:, None] * test_own + np.arange(test_own, dtype=np.int32)[None, :]
    found = jnp.sum(jnp.where(test_slabs == me, test_offsets + 1, 0), axis=1) - 1
    group = np.arange(devices * test_own, dtype=np.int32)
    block = jnp.sum(jnp.where(place.reshape(-1, 1) == group[None, :], found[None, :], 0), axis=1)
    block = jnp.broadcast_to(block[:, None], (devices * test_own, LANES))

    gallery, scale = load(gallery)
    colsum, listed = score(queries, gallery, scale, block, devices * bank_own)
    bit = banks // 2
    other = jnp.zeros_like(colsum)
    while bit:
        other = swap(colsum, "bank", banks, bit)
        bit //= 2
        if bit:
            colsum = colsum + other
    sums = pool(order, me.reshape(1), listed, colsum, other, gallery, block)
    sums = lax.all_to_all(sums, "gal", 0, 0, tiled=True)
    sums = jnp.sum(sums.astype(jnp.float32), axis=0)
    depth = gallery.shape[1]
    return sums[:, :depth] / (sums[:, depth] + sums[:, depth + 1])[:, None]


def solution(mesh):
    in_specs = (
        P(("bank", "gal"), None),
        P("gal", None),
        P(("bank", "gal"), None),
        P("bank", None),
        P("bank", None),
    )
    out_specs = P(("bank", "gal"), None)
    local = functools.partial(body, mesh.shape["gal"], mesh.shape["bank"])
    return jax.shard_map(local, mesh=mesh, in_specs=in_specs, out_specs=out_specs, check_vma=False)
```

time: 173 us -> 52.6 us (0.30)
  blocking collectives: 79 us -> 13.9 us
  waiting for transfers between devices: 57.8 us -> 6.57 us
  matrix products: 14.6 us -> 0 us
  between operations: 13.4 us -> 0.12 us
  local copies, waits for them, and re-layouts: 0.56 us -> 11.3 us
  starting transfers between devices: 0.01 us -> 10.1 us
  Pallas kernels: 0 us -> 5.82 us
  other arithmetic: 7.2 us -> 4.09 us
    psum x1 -> x0, waiting for transfers between devices: 57.8 us -> none  [body(): numer_all, denom_all = lax.psum((numerator, denominator), 'gal')]
    all_gather x2 -> x0, blocking collectives: 41.3 us -> none  [the longest x1 23.4 us: body(): queries = lax.all_gather(test_queries, 'gal', axis=0, tiled=True)]
    psum x2 -> x0, blocking collectives: 37.7 us -> none  [the longest x1 29.5 us: body(): numer_all, denom_all = lax.psum((numerator, denominator), 'gal')]
    dot_general x3 -> x0, matrix products: 14.6 us -> none  [the longest x2 9.93 us: inner_rows(): lax.dot_general(first_rows, second_rows, (((1,), (1,)), ((), ())), prefer...]
    all_to_all x0 -> x1, blocking collectives: none -> 13.9 us  [body(): sums = lax.all_to_all(sums, 'gal', 0, 0, tiled=True)]
    ppermute x0 -> x5, starting transfers between devices: none -> 10.1 us  [swap(): return lax.ppermute(value, axis, [(i, i ^ bit) for i in range(size)])]
    unnamed x5 -> x10, local copies, waits for them, and re-layouts: 0.04 us -> 8.23 us
    ppermute x0 -> x5, waiting for transfers between devices: none -> 6.57 us  [swap(): return lax.ppermute(value, axis, [(i, i ^ bit) for i in range(size)])]
  transfers between devices with their start and end apart: 1 -> 5, of which waited for: 1 -> 4; matrix products, arithmetic and copies ran while one was open for 0% -> 3% of each run, Pallas kernels for 0% -> 5%
where the time goes in v1:
time: 52.6 us; the launch traced here: 51.9 us
  blocking collectives  13.9 us (26%)
  local copies, waits for them, and re-layouts  11.3 us (21%)
  starting transfers between devices  10.1 us (19%)
  waiting for transfers between devices  6.57 us (12%)
  Pallas kernels  5.82 us (11%)
  other arithmetic  4.09 us (8%)
    all_to_all x1, blocking collectives, body(): sums = lax.all_to_all(sums, 'gal', 0, 0, tiled=True)  13.9 us
    ppermute x5, starting transfers between devices, swap(): return lax.ppermute(value, axis, [(i, i ^ bit) for i in range(size)])  10.1 us
    unnamed x10, local copies, waits for them, and re-layouts  8.23 us
    ppermute x5, waiting for transfers between devices, swap(): return lax.ppermute(value, axis, [(i, i ^ bit) for i in range(size)])  6.57 us
    concatenate x2, local copies, waits for them, and re-layouts, body(): packed = jnp.concatenate([bank, test], axis=0)  2.86 us
    pallas_call x1, Pallas kernels, load(): pl.pallas_call(load_kernel, out_shape=(pltpu.VMEM(gallery.shape, gallery....  2.34 us
    pallas_call x1, Pallas kernels, score(): pl.pallas_call(functools.partial(score_kernel, bank_rows), out_shape=(plt...  2.21 us
    concatenate x2, other arithmetic, body(): packed = jnp.concatenate([bank, test], axis=0)  1.52 us
  transfers between devices with their start and end apart: 5, of which 4 were waited for; matrix products, arithmetic and copies ran while one was open for 3% of the time, Pallas kernels for 5%

profile of v1, /device:TPU:0, one launch (start us, length us, event | category | flops | bytes accessed | tf_op | source)
XLA Modules:
  0.0 51.9 jit_solution(15239756654199204812)
XLA Ops:
  0.0 0.8 %pad_maximum_fusion.1 = bf16[12,768]{1,0:T(8,128)(2,1)S(1)} fusion(bf16[4,768]{1,0:T(4,128)(2,1)} %param.10, bf16[8,768]{1,0:T(8,128)(2,1)} %param.8), kind=kLoop, calls=%fused_computation.4 | loop fusion | flops 36864 | bytes 36864 | tf_op jit(solution)/shard_map/concatenate | solution.py:153
  0.8 4.0 %collective-permute-start = (bf16[12,768]{1,0:T(8,128)(2,1)S(1)}, bf16[12,768]{1,0:T(8,128)(2,1)S(1)}, u32[]{:S(2)}, u32[]{:S(2)}) collective-permute-start(bf16[12,768]{1,0:T(8,128)(2,1)S(1)} %pad_maximum_fusion.1), channel_id=1, source_target_pairs={{0,8},{1,9},{2,10},{3,11},{4,12},{5,13},{6,14},{7,15},{8,0},{9,1},... | collective-permute-start | bytes 55304 | tf_op jit(solution)/shard_map/ppermute | solution.py:142
  4.8 0.7 %xor_multiply_fusion = s32[16]{0:T(128)S(1)} fusion(s32[16]{0:T(128)} %constant.21.clone, s32[]{:T(128)} %axis_index.12), kind=kLoop, calls=%fused_computation.10 | loop fusion | flops 32 | bytes 132 | tf_op jit(solution)/shard_map/mul | solution.py:161
  5.5 1.2 %collective-permute-done = bf16[12,768]{1,0:T(8,128)(2,1)S(1)} collective-permute-done((bf16[12,768]{1,0:T(8,128)(2,1)S(1)}, bf16[12,768]{1,0:T(8,128)(2,1)S(1)}, u32[]{:S(2)}, u32[]{:S(2)}) %collective-permute-start) | collective-permute-done | bytes 18464 | tf_op jit(solution)/shard_map/ppermute | solution.py:142
  6.7 0.7 %pad_maximum_fusion = bf16[24,768]{1,0:T(8,128)(2,1)S(1)} fusion(bf16[4,768]{1,0:T(4,128)(2,1)S(1)} %slice.45, bf16[4,768]{1,0:T(4,128)(2,1)} %param.10, bf16[8,768]{1,0:T(8,128)(2,1)S(1)} %slice.44, bf16[8,768]{1,0:T(8,128)(2,1)} %param.8), kind=kLoop, calls=%fused_computation.1 | loop fusion | flops 147456 | bytes 73728 | tf_op jit(solution)/shard_map/concatenate | solution.py:153
  7.4 2.0 %collective-permute-start.1 = (bf16[24,768]{1,0:T(8,128)(2,1)S(1)}, bf16[24,768]{1,0:T(8,128)(2,1)S(1)}, u32[]{:S(2)}, u32[]{:S(2)}) collective-permute-start(bf16[24,768]{1,0:T(8,128)(2,1)S(1)} %pad_maximum_fusion), channel_id=1, source_target_pairs={{0,4},{1,5},{2,6},{3,7},{4,0},{5,1},{6,2},{7,3},{8,12},{9,13},{10,... | collective-permute-start | bytes 110600 | tf_op jit(solution)/shard_map/ppermute | solution.py:142
  9.4 2.0 %collective-permute-done.1 = bf16[24,768]{1,0:T(8,128)(2,1)S(1)} collective-permute-done((bf16[24,768]{1,0:T(8,128)(2,1)S(1)}, bf16[24,768]{1,0:T(8,128)(2,1)S(1)}, u32[]{:S(2)}, u32[]{:S(2)}) %collective-permute-start.1) | collective-permute-done | bytes 36896 | tf_op jit(solution)/shard_map/ppermute | solution.py:142
  11.4 1.4 %concatenate.31 = bf16[48,768]{1,0:T(8,128)(2,1)S(1)} concatenate(bf16[8,768]{1,0:T(8,128)(2,1)} %param.8, bf16[8,768]{1,0:T(8,128)(2,1)S(1)} %slice.44, bf16[16,768]{1,0:T(8,128)(2,1)S(1)} %slice.46, bf16[4,768]{1,0:T(4,128)(2,1)} %param.10, bf16[4,768]{1,0:T(4,128)(2,1)S(1)} %slice.45, bf16[8,768]{1,0:T(8,128)(2,1)S(1)} %slice.47), dimensions={0} | concatenate | bytes 147456 | tf_op jit(solution)/shard_map/concatenate | solution.py:153
  12.8 2.0 %collective-permute-start.2 = (bf16[48,768]{1,0:T(8,128)(2,1)S(1)}, bf16[48,768]{1,0:T(8,128)(2,1)S(1)}, u32[]{:S(2)}, u32[]{:S(2)}) collective-permute-start(bf16[48,768]{1,0:T(8,128)(2,1)S(1)} %concatenate.31), channel_id=1, source_target_pairs={{0,2},{1,3},{2,0},{3,1},{4,6},{5,7},{6,4},{7,5},{8,10},{9,11},{10,... | collective-permute-start | bytes 221192 | tf_op jit(solution)/shard_map/ppermute | solution.py:142
  14.9 0.7 %select_reduce_fusion.1 = s32[64]{0:T(128)S(1)} fusion(s32[64,8]{0,1:T(8,128)} %param.12, s32[64,8]{0,1:T(8,128)} %param.11, s32[]{:T(128)} %axis_index.12), kind=kLoop, calls=%fused_computation.7 | loop fusion | flops 1984 | bytes 4356 | tf_op jit(solution)/shard_map/reduce_sum | solution.py:162
  15.6 1.6 %collective-permute-done.2 = bf16[48,768]{1,0:T(8,128)(2,1)S(1)} collective-permute-done((bf16[48,768]{1,0:T(8,128)(2,1)S(1)}, bf16[48,768]{1,0:T(8,128)(2,1)S(1)}, u32[]{:S(2)}, u32[]{:S(2)}) %collective-permute-start.2) | collective-permute-done | bytes 73760 | tf_op jit(solution)/shard_map/ppermute | solution.py:142
  17.3 1.4 %concatenate.32 = bf16[96,768]{1,0:T(8,128)(2,1)S(1)} concatenate(bf16[8,768]{1,0:T(8,128)(2,1)} %param.8, bf16[8,768]{1,0:T(8,128)(2,1)S(1)} %slice.44, bf16[16,768]{1,0:T(8,128)(2,1)S(1)} %slice.46, bf16[32,768]{1,0:T(8,128)(2,1)S(1)} %slice.48, bf16[4,768]{1,0:T(4,128)(2,1)} %param.10, bf16[4,768]{1,0:T(4,128)(2,1)S(1)} %slice.45, bf16[8,768]{1,0:T(8,128)(2,1)S(1)} %slice.47, ...), dimensions={0} | concatenate | bytes 294912 | tf_op jit(solution)/shard_map/concatenate | solution.py:153
  18.9 2.8 %copy-done.2 = bf16[4096,768]{1,0:T(8,128)(2,1)S(1)} copy-done((bf16[4096,768]{1,0:T(8,128)(2,1)S(1)}, bf16[4096,768]{1,0:T(8,128)(2,1)}, u32[]{:S(2)}) %copy-start.2) | copy-done | bytes 6291480
  21.7 2.3 %load.1 = (bf16[4096,768]{1,0:T(8,128)(2,1)S(1)}, f32[8,512]{1,0:T(8,128)S(1)}) custom-call(bf16[4096,768]{1,0:T(8,128)(2,1)S(1)} %copy-done.2), custom_call_target="tpu_custom_call" | custom-call | tf_op jit(solution)/shard_map/load/pallas_call | solution.py:52
  24.0 2.6 %copy-done = bf16[4096,768]{1,0:T(8,128)(2,1)} copy-done((bf16[4096,768]{1,0:T(8,128)(2,1)}, bf16[4096,768]{1,0:T(8,128)(2,1)S(1)}, u32[]{:S(2)}) %copy-start) | copy-done | bytes 6291480
  26.7 0.2 select_reduce_fusion
  27.0 2.8 %copy-done.1 = bf16[4096,768]{1,0:T(8,128)(2,1)S(1)} copy-done((bf16[4096,768]{1,0:T(8,128)(2,1)S(1)}, bf16[4096,768]{1,0:T(8,128)(2,1)}, u32[]{:S(2)}) %copy-start.1) | copy-done | bytes 6291480
  29.8 2.2 %score.1 = (f32[8,512]{1,0:T(8,128)S(1)}, f32[64,128]{1,0:T(8,128)S(1)}) custom-call(bf16[192,768]{1,0:T(8,128)(2,1)S(1)} %concatenate.33.query_ref, bf16[4096,768]{1,0:T(8,128)(2,1)S(1)} %copy-done.1, f32[8,512]{1,0:T(8,128)S(1)} %get-tuple-element.10.scale_ref, s32[64,128]{1,0:T(8,128)S(1)} %broadcast_in_dim.28.block_ref), custom_call_target="tpu_custom_call" | custom-call | tf_op jit(solution)/shard_map/score/pallas_call | solution.py:92
  32.0 2.0 %collective-permute-start.4 = (f32[8,512]{1,0:T(8,128)S(1)}, f32[8,512]{1,0:T(8,128)S(1)}, u32[]{:S(2)}, u32[]{:S(2)}) collective-permute-start(f32[8,512]{1,0:T(8,128)S(1)} %get-tuple-element.12.own_ref), channel_id=1, source_target_pairs={{0,16},{16,0},{1,17},{17,1},{2,18},{18,2},{3,19},{19,3},{4,20},{20... | collective-permute-start | bytes 49160 | tf_op jit(solution)/shard_map/ppermute | solution.py:142
  34.1 1.8 %collective-permute-done.4.other_ref = f32[8,512]{1,0:T(8,128)S(1)} collective-permute-done((f32[8,512]{1,0:T(8,128)S(1)}, f32[8,512]{1,0:T(8,128)S(1)}, u32[]{:S(2)}, u32[]{:S(2)}) %collective-permute-start.4) | collective-permute-done | bytes 16416 | tf_op jit(solution)/shard_map/ppermute | solution.py:142
  35.8 1.3 %pool.1 = bf16[16,4,896]{2,1,0:T(4,128)(2,1)S(1)} custom-call(s32[1]{0:T(128)} %bitcast.me_ref, f32[64,128]{1,0:T(8,128)S(1)} %get-tuple-element.11.listed_ref, f32[8,512]{1,0:T(8,128)S(1)} %get-tuple-element.12.own_ref, f32[8,512]{1,0:T(8,128)S(1)} %collective-permute-done.4.other_ref, bf16[4096,768]{1,0:T(8,128)(2,1)S(1)} %copy-done.1, ...), custom_call_target="tpu_custom_call" | custom-call | tf_op jit(solution)/shard_map/pool/pallas_call | solution.py:130
  37.1 13.9 %all_to_all.5 = bf16[16,4,896]{2,1,0:T(4,128)(2,1)S(1)} all-to-all(bf16[16,4,896]{2,1,0:T(4,128)(2,1)S(1)} %pool.1), channel_id=1, replica_groups=mesh['bank'=2,'gal'=16] {'gal'}, dimensions={0} | all-to-all | bytes 229376 | tf_op jit(solution)/shard_map/all_to_all | solution.py:177
  51.0 0.2 fusion
  51.2 0.7 %slice_divide_fusion = f32[4,768]{1,0:T(4,128)} fusion(f32[4,896]{1,0:T(4,128)S(1)} %convert_reduce_fusion, f32[4]{0:T(128)S(1)} %fusion), kind=kLoop, calls=%fused_computation.5 | loop fusion | flops 3072 | bytes 24592 | tf_op jit(solution)/shard_map/div | solution.py:180
  (23 shorter events, 0.5 us)
Async XLA Ops:
  0.0 26.9 %copy-start.4 = (bf16[4,768]{1,0:T(4,128)(2,1)S(1)}, bf16[4,768]{1,0:T(4,128)(2,1)}, u32[]{:S(2)}) copy-start(bf16[4,768]{1,0:T(4,128)(2,1)} %param.10) | copy-start | bytes 18436
  0.0 26.9 %copy-start.3 = (bf16[8,768]{1,0:T(8,128)(2,1)S(1)}, bf16[8,768]{1,0:T(8,128)(2,1)}, u32[]{:S(2)}) copy-start(bf16[8,768]{1,0:T(8,128)(2,1)} %param.8) | copy-start | bytes 36868
  0.8 5.9 %collective-permute-start = (bf16[12,768]{1,0:T(8,128)(2,1)S(1)}, bf16[12,768]{1,0:T(8,128)(2,1)S(1)}, u32[]{:S(2)}, u32[]{:S(2)}) collective-permute-start(bf16[12,768]{1,0:T(8,128)(2,1)S(1)} %pad_maximum_fusion.1), channel_id=1, source_target_pairs={{0,8},{1,9},{2,10},{3,11},{4,12},{5,13},{6,14},{7,15},{8,0},{9,1},... | collective-permute-start | bytes 55304 | tf_op jit(solution)/shard_map/ppermute | solution.py:142
  7.4 4.0 %collective-permute-start.1 = (bf16[24,768]{1,0:T(8,128)(2,1)S(1)}, bf16[24,768]{1,0:T(8,128)(2,1)S(1)}, u32[]{:S(2)}, u32[]{:S(2)}) collective-permute-start(bf16[24,768]{1,0:T(8,128)(2,1)S(1)} %pad_maximum_fusion), channel_id=1, source_target_pairs={{0,4},{1,5},{2,6},{3,7},{4,0},{5,1},{6,2},{7,3},{8,12},{9,13},{10,... | collective-permute-start | bytes 110600 | tf_op jit(solution)/shard_map/ppermute | solution.py:142
  12.8 4.4 %collective-permute-start.2 = (bf16[48,768]{1,0:T(8,128)(2,1)S(1)}, bf16[48,768]{1,0:T(8,128)(2,1)S(1)}, u32[]{:S(2)}, u32[]{:S(2)}) collective-permute-start(bf16[48,768]{1,0:T(8,128)(2,1)S(1)} %concatenate.31), channel_id=1, source_target_pairs={{0,2},{1,3},{2,0},{3,1},{4,6},{5,7},{6,4},{7,5},{8,10},{9,11},{10,... | collective-permute-start | bytes 221192 | tf_op jit(solution)/shard_map/ppermute | solution.py:142
  18.7 8.1 %collective-permute-start.3 = (bf16[96,768]{1,0:T(8,128)(2,1)S(1)}, bf16[96,768]{1,0:T(8,128)(2,1)S(1)}, u32[]{:S(2)}, u32[]{:S(2)}) collective-permute-start(bf16[96,768]{1,0:T(8,128)(2,1)S(1)} %concatenate.32), channel_id=1, source_target_pairs={{0,1},{1,0},{2,3},{3,2},{4,5},{5,4},{6,7},{7,6},{8,9},{9,8},{10,11... | collective-permute-start | bytes 442376 | tf_op jit(solution)/shard_map/ppermute | solution.py:142
  18.9 2.8 %copy-start.2 = (bf16[4096,768]{1,0:T(8,128)(2,1)S(1)}, bf16[4096,768]{1,0:T(8,128)(2,1)}, u32[]{:S(2)}) copy-start(bf16[4096,768]{1,0:T(8,128)(2,1)} %gallery_hbm.1) | copy-start | bytes 18874372
  24.0 2.7 %copy-start = (bf16[4096,768]{1,0:T(8,128)(2,1)}, bf16[4096,768]{1,0:T(8,128)(2,1)S(1)}, u32[]{:S(2)}) copy-start(bf16[4096,768]{1,0:T(8,128)(2,1)S(1)} %get-tuple-element.9.gallery_ref) | copy-start | bytes 18874372
  27.0 2.8 %copy-start.1 = (bf16[4096,768]{1,0:T(8,128)(2,1)S(1)}, bf16[4096,768]{1,0:T(8,128)(2,1)}, u32[]{:S(2)}) copy-start(bf16[4096,768]{1,0:T(8,128)(2,1)} %copy-done) | copy-start | bytes 18874372
  32.0 3.8 %collective-permute-start.4 = (f32[8,512]{1,0:T(8,128)S(1)}, f32[8,512]{1,0:T(8,128)S(1)}, u32[]{:S(2)}, u32[]{:S(2)}) collective-permute-start(f32[8,512]{1,0:T(8,128)S(1)} %get-tuple-element.12.own_ref), channel_id=1, source_target_pairs={{0,16},{16,0},{1,17},{17,1},{2,18},{18,2},{3,19},{19,3},{4,20},{20... | collective-permute-start | bytes 49160 | tf_op jit(solution)/shard_map/ppermute | solution.py:142

commit v2 on v1

v2 whole, which is shorter than its diff:
```python
import functools

import jax
import jax.numpy as jnp
from jax import lax
from jax.experimental import pallas as pl
from jax.experimental.pallas import tpu as pltpu
from jax.sharding import PartitionSpec as P

BLOCK = 128
CHUNKS = 8
LANES = 128
CAP = 2
SHARPNESS = 20.0
LOG2E = 1.4426950408889634
epsilon = 1e-06

VMEM = pl.BlockSpec(memory_space=pltpu.VMEM)
HBM = pl.BlockSpec(memory_space=pltpu.HBM)
PARAMS = pltpu.CompilerParams(vmem_limit_bytes=16 << 20)


def in_hbm(value):
    return pltpu.with_memory_space_constraint(value, pltpu.HBM)


def keep(value):
    return pltpu.with_memory_space_constraint(value, pltpu.VMEM)


def pack_kernel(bank_hbm, test_hbm, packed_ref, bank_ref, test_ref, sems):
    copies = [
        pltpu.make_async_copy(bank_hbm, bank_ref, sems.at[0]),
        pltpu.make_async_copy(test_hbm, test_ref, sems.at[1]),
    ]
    for copy in copies:
        copy.start()
    for copy in copies:
        copy.wait()
    rows = bank_ref.shape[0]
    packed_ref[:rows, :] = bank_ref[...]
    packed_ref[rows:, :] = test_ref[...]


def pack(bank, test):
    return pl.pallas_call(
        pack_kernel,
        out_shape=pltpu.VMEM((bank.shape[0] + test.shape[0], bank.shape[1]), bank.dtype),
        in_specs=[HBM, HBM],
        out_specs=VMEM,
        scratch_shapes=[
            pltpu.VMEM(bank.shape, bank.dtype),
            pltpu.VMEM(test.shape, test.dtype),
            pltpu.SemaphoreType.DMA((2,)),
        ],
        compiler_params=PARAMS,
        name="pack",
    )(in_hbm(bank), in_hbm(test))


def bits_of(index, masks):
    value = jnp.zeros_like(index)
    for k, mask in enumerate(masks):
        value = value ^ jnp.where((index >> k) & 1 == 1, mask, 0)
    return value


def iota(shape, axis):
    return lax.broadcasted_iota(jnp.int32, shape, axis)


def route(masks, bank_own, test_own, slabs, offsets, pick_ref, block_ref, spread_ref):
    me = lax.axis_index("gal")
    devices = 1 << len(masks)
    group = devices * test_own
    own = bank_own + test_own
    bank_rows = devices * bank_own
    slots = devices * CAP

    found = jnp.sum(jnp.where(slabs == me, offsets + 1, 0), axis=0, keepdims=True)
    before = (iota((group, group), 0) // test_own == iota((group, group), 1) // test_own) & (
        iota((group, group), 0) < iota((group, group), 1)
    )
    flags = jnp.broadcast_to(jnp.where(found > 0, 1.0, 0.0), (8, group)).astype(jnp.bfloat16)
    rank = jnp.dot(flags, jnp.where(before, 1.0, 0.0).astype(jnp.bfloat16), preferred_element_type=jnp.float32)
    rank = rank[:1].astype(jnp.int32)
    index = iota((slots, group), 0)
    column = iota((slots, group), 1)
    filled = (column // test_own == me ^ bits_of(index // CAP, masks)) & (found > 0) & (rank == index % CAP)
    block = jnp.sum(jnp.where(filled, found, 0), axis=1, keepdims=True) - 1
    block_ref[...] = jnp.broadcast_to(block, block_ref.shape)
    from_row = jnp.sum(jnp.where(filled, column % test_own + 1, 0), axis=1, keepdims=True)
    index = iota((slots, 1), 0) // CAP
    slot_from = jnp.where(from_row > 0, index * own + bank_own - 1 + from_row, -1)
    index = iota((bank_rows, 1), 0)
    bank_from = index // bank_own * own + index % bank_own
    half = pick_ref.shape[2]
    for h in range(2):
        column = iota((bank_rows, half), 1) + h * half
        pick_ref[h, :bank_rows, :] = jnp.where(column == bank_from, 1.0, 0.0).astype(jnp.bfloat16)
        column = iota((slots, half), 1) + h * half
        pick_ref[h, bank_rows:, :] = jnp.where(column == slot_from, 1.0, 0.0).astype(jnp.bfloat16)

    lane = iota((1, slots), 1)
    filled_before = jnp.zeros((1, slots), jnp.int32)
    mine = iota(slabs.shape, 1)
    for r in range(test_own):
        listed = jnp.sum(jnp.where(mine == me * test_own + r, slabs, 0), axis=1, keepdims=True)
        here = jnp.sum(jnp.where(listed == lane // CAP, 1, 0), axis=0, keepdims=True)
        spread_ref[r : r + 1, :] = jnp.where((here > 0) & (filled_before == lane % CAP), 1.0, 0.0)
        filled_before = filled_before + here


def load_kernel(
    masks, bank_own, test_own, gallery_hbm, packed_ref, slabs_hbm, offsets_hbm,
    gallery_ref, scale_ref, packed_out, pick_ref, block_ref, spread_ref, slabs_ref, offsets_ref, sems, small_sems,
):
    rows, depth = gallery_hbm.shape
    part = rows // CHUNKS
    small = [
        pltpu.make_async_copy(slabs_hbm, slabs_ref, small_sems.at[0]),
        pltpu.make_async_copy(offsets_hbm, offsets_ref, small_sems.at[1]),
    ]
    copies = [
        pltpu.make_async_copy(
            gallery_hbm.at[pl.ds(c * part, part)], gallery_ref.at[pl.ds(c * part, part)], sems.at[c]
        )
        for c in range(CHUNKS)
    ]
    for copy in small + copies:
        copy.start()
    packed_out[...] = packed_ref[...]
    for copy in small:
        copy.wait()
    route(masks, bank_own, test_own, slabs_ref[...], offsets_ref[...], pick_ref, block_ref, spread_ref)
    for c in range(CHUNKS):
        copies[c].wait()
        values = gallery_ref[pl.ds(c * part, part), :].astype(jnp.float32)
        squares = values * values
        folded = squares[:, :LANES]
        for k in range(1, depth // LANES):
            folded = folded + squares[:, k * LANES : (k + 1) * LANES]
        for b in range(part // BLOCK):
            total = jnp.sum(folded[b * BLOCK : (b + 1) * BLOCK].T, axis=0, keepdims=True)
            scale_ref[c : c + 1, b * BLOCK : (b + 1) * BLOCK] = lax.rsqrt(total + epsilon)


def load(masks, bank_own, test_own, gallery, packed, slabs, offsets):
    rows, depth = gallery.shape
    devices = 1 << len(masks)
    slots = devices * CAP
    half = devices * (bank_own + test_own) // 2
    return pl.pallas_call(
        functools.partial(load_kernel, masks, bank_own, test_own),
        out_shape=(
            pltpu.VMEM(gallery.shape, gallery.dtype),
            pltpu.VMEM((CHUNKS, rows // CHUNKS), jnp.float32),
            pltpu.VMEM(packed.shape, packed.dtype),
            pltpu.VMEM((2, devices * bank_own + slots, half), jnp.bfloat16),
            pltpu.VMEM((slots, LANES), jnp.int32),
            pltpu.VMEM((test_own, slots), jnp.float32),
        ),
        in_specs=[HBM, VMEM, HBM, HBM],
        out_specs=(VMEM,) * 6,
        scratch_shapes=[
            pltpu.VMEM(slabs.shape, slabs.dtype),
            pltpu.VMEM(offsets.shape, offsets.dtype),
            pltpu.SemaphoreType.DMA((CHUNKS,)),
            pltpu.SemaphoreType.DMA((2,)),
        ],
        compiler_params=PARAMS,
        name="load",
    )(in_hbm(gallery), packed, in_hbm(slabs), in_hbm(offsets))


def score_kernel(first_ref, second_ref, pick_ref, gallery_ref, scale_ref, block_ref, colsum_ref, listed_ref):
    wide = jnp.dot(pick_ref[0], first_ref[...], preferred_element_type=jnp.float32)
    wide = wide + jnp.dot(pick_ref[1], second_ref[...], preferred_element_type=jnp.float32)
    queries = wide.astype(jnp.bfloat16)
    query_scale = lax.rsqrt(jnp.sum(wide * wide, axis=1, keepdims=True) + epsilon) * (SHARPNESS * LOG2E)
    slots = block_ref.shape[0]
    bank_rows = queries.shape[0] - slots
    part = scale_ref.shape[1]
    block = block_ref[...]
    picked = jnp.zeros((slots, BLOCK), jnp.float32)
    for c in range(CHUNKS):
        scores = lax.dot_general(
            queries,
            gallery_ref[pl.ds(c * part, part), :],
            (((1,), (1,)), ((), ())),
            preferred_element_type=jnp.float32,
        )
        scores = scores * scale_ref[c : c + 1, :]
        exps = jnp.exp2(scores[:bank_rows] * query_scale[:bank_rows])
        colsum_ref[c : c + 1, :] = jnp.sum(exps, axis=0, keepdims=True)
        for b in range(part // BLOCK):
            here = scores[bank_rows:, b * BLOCK : (b + 1) * BLOCK]
            picked = jnp.where(block == c * (part // BLOCK) + b, here, picked)
    listed_ref[...] = jnp.exp2(picked * query_scale[bank_rows:])


def score(first, second, pick, gallery, scale, block):
    return pl.pallas_call(
        score_kernel,
        out_shape=(pltpu.VMEM(scale.shape, jnp.float32), pltpu.VMEM((block.shape[0], BLOCK), jnp.float32)),
        in_specs=[VMEM] * 6,
        out_specs=(VMEM, VMEM),
        compiler_params=PARAMS,
        name="score",
    )(keep(first), second, keep(pick), keep(gallery), keep(scale), keep(block))


def pool_kernel(order, listed_ref, own_ref, other_ref, gallery_ref, block_ref, out_ref, weight_ref):
    block = block_ref[...]
    slots = block.shape[0]
    rows, depth = gallery_ref.shape
    each = rows // BLOCK // CHUNKS
    inverse = 1.0 / (own_ref[...] + other_ref[...])
    picked = jnp.zeros((slots, BLOCK), jnp.float32)
    for b in range(rows // BLOCK):
        c, at = b // each, (b % each) * BLOCK
        picked = jnp.where(block == b, inverse[c : c + 1, at : at + BLOCK], picked)
    weight = listed_ref[...] * picked
    total = jnp.sum(weight, axis=1, keepdims=True)
    for b in range(rows // BLOCK):
        weight_ref[:, b * BLOCK : (b + 1) * BLOCK] = jnp.where(block == b, weight, 0.0).astype(jnp.bfloat16)
    numerator = jnp.dot(weight_ref[...], gallery_ref[...], preferred_element_type=jnp.float32)
    high = total.astype(jnp.bfloat16).astype(jnp.float32)
    lane = iota((slots, LANES), 1)
    tail = jnp.where(lane == 0, high, jnp.where(lane == 1, total - high, 0.0))
    me = lax.axis_index("gal")
    for i, bits in enumerate(order):
        at = slice(i * CAP, (i + 1) * CAP)
        out_ref[me ^ bits, :, :depth] = numerator[at].astype(jnp.bfloat16)
        out_ref[me ^ bits, :, depth:] = tail[at].astype(jnp.bfloat16)


def pool(order, listed, own, other, gallery, block):
    rows, depth = gallery.shape
    slots = listed.shape[0]
    return pl.pallas_call(
        functools.partial(pool_kernel, order),
        out_shape=pltpu.VMEM((len(order), CAP, depth + LANES), jnp.bfloat16),
        in_specs=[VMEM] * 5,
        out_specs=VMEM,
        scratch_shapes=[pltpu.VMEM((slots, rows), jnp.bfloat16)],
        compiler_params=PARAMS,
        name="pool",
    )(keep(listed), keep(own), other, keep(gallery), keep(block))


def finish_kernel(sums_ref, spread_ref, out_ref):
    depth = out_ref.shape[1]
    sums = jnp.concatenate([sums_ref[s].astype(jnp.float32) for s in range(sums_ref.shape[0])], axis=0)
    sums = jnp.dot(
        spread_ref[...].astype(jnp.bfloat16), sums.astype(jnp.bfloat16), preferred_element_type=jnp.float32
    )
    out_ref[...] = sums[:, :depth] / (sums[:, depth : depth + 1] + sums[:, depth + 1 : depth + 2])


def finish(sums, spread):
    return pl.pallas_call(
        finish_kernel,
        out_shape=jax.ShapeDtypeStruct((spread.shape[0], sums.shape[2] - LANES), jnp.float32),
        in_specs=[VMEM, VMEM],
        out_specs=VMEM,
        compiler_params=PARAMS,
        name="finish",
    )(sums, keep(spread))


def swap(value, axis, size, bit):
    return lax.ppermute(value, axis, [(i, i ^ bit) for i in range(size)])


def body(devices, banks, bank_queries, gallery, test_queries, test_slabs, test_offsets):
    bank_own, test_own = bank_queries.shape[0], test_queries.shape[0]

    masks = [devices >> (i + 1) | 1 for i in range(devices.bit_length() - 1)]
    order = [0]
    for mask in masks:
        order = order + [o ^ mask for o in order]

    packed = pack(bank_queries, test_queries)
    other = swap(packed, "gal", devices, masks[0])
    gallery, scale, packed, pick, block, spread = load(
        masks, bank_own, test_own, gallery, packed, test_slabs.T, test_offsets.T
    )
    for mask in masks[1:]:
        packed = jnp.concatenate([packed, other], axis=0)
        other = swap(packed, "gal", devices, mask)

    colsum, listed = score(packed, other, pick, gallery, scale, block)
    bit = banks // 2
    other = jnp.zeros_like(colsum)
    while bit:
        other = swap(colsum, "bank", banks, bit)
        bit //= 2
        if bit:
            colsum = colsum + other
    sums = pool(order, listed, colsum, other, gallery, block)
    sums = lax.all_to_all(sums, "gal", 0, 0, tiled=True)
    return finish(sums, spread)


def solution(mesh):
    in_specs = (
        P(("bank", "gal"), None),
        P("gal", None),
        P(("bank", "gal"), None),
        P("bank", None),
        P("bank", None),
    )
    out_specs = P(("bank", "gal"), None)
    local = functools.partial(body, mesh.shape["gal"], mesh.shape["bank"])
    return jax.shard_map(local, mesh=mesh, in_specs=in_specs, out_specs=out_specs, check_vma=False)
```

time: 52.6 us -> 37.6 us (0.71)
  local copies, waits for them, and re-layouts: 11.3 us -> 0 us
  other arithmetic: 4.09 us -> 0.06 us
  Pallas kernels: 5.82 us -> 9.74 us
  blocking collectives: 13.9 us -> 11 us
  starting transfers between devices: 10.1 us -> 9.37 us
    unnamed x10 -> x0, local copies, waits for them, and re-layouts: 8.23 us -> none
    pallas_call x2 -> x4, Pallas kernels: 4.55 us -> 8.56 us  [the longest x1 4.54 us: load(): pl.pallas_call(functools.partial(load_kernel, masks, bank_own, test_own),...]
    concatenate x3 -> x0, local copies, waits for them, and re-layouts: 2.9 us -> none  [the longest x2 2.86 us: body(): packed = jnp.concatenate([bank, test], axis=0)]
    all_to_all x1, blocking collectives: 13.9 us -> 11 us  [body(): sums = lax.all_to_all(sums, 'gal', 0, 0, tiled=True)]
    concatenate x2 -> x3, other arithmetic: 1.52 us -> 0.06 us  [body(): packed = jnp.concatenate([packed, other], axis=0)]
    reduce_sum x3 -> x0, other arithmetic: 0.97 us -> none  [the longest x1 0.74 us: body(): jnp.sum(jnp.where(test_slabs == me, test_offsets + 1, 0), axis=1) - 1]
    ppermute x5, starting transfers between devices: 10.1 us -> 9.37 us  [swap(): return lax.ppermute(value, axis, [(i, i ^ bit) for i in range(size)])]
    div x1 -> x0, other arithmetic: 0.68 us -> none  [body(): return sums[:, :depth] / (sums[:, depth] + sums[:, depth + 1])[:, None]]
  transfers between devices with their start and end apart: 5 -> 5, of which waited for: 4 -> 4; matrix products, arithmetic and copies ran while one was open for 3% -> 0% of each run, Pallas kernels for 5% -> 12%
where the time goes in v2:
time: 37.6 us; the launch traced here: 37.3 us
  blocking collectives  11 us (29%)
  Pallas kernels  9.74 us (26%)
  starting transfers between devices  9.37 us (25%)
  waiting for transfers between devices  7.08 us (19%)
    all_to_all x1, blocking collectives, body(): sums = lax.all_to_all(sums, 'gal', 0, 0, tiled=True)  11 us
    ppermute x5, starting transfers between devices, swap(): return lax.ppermute(value, axis, [(i, i ^ bit) for i in range(size)])  9.37 us
    ppermute x5, waiting for transfers between devices, swap(): return lax.ppermute(value, axis, [(i, i ^ bit) for i in range(size)])  7.08 us
    pallas_call x1, Pallas kernels, load(): pl.pallas_call(functools.partial(load_kernel, masks, bank_own, test_own),...  4.54 us
    pallas_call x1, Pallas kernels, score(): pl.pallas_call(score_kernel, out_shape=(pltpu.VMEM(scale.shape, jnp.float...  2.42 us
    pallas_call x1, Pallas kernels, pool(): pl.pallas_call(functools.partial(pool_kernel, order), out_shape=pltpu.VME...  1.17 us
    pallas_call x1, Pallas kernels, finish(): pl.pallas_call(finish_kernel, out_shape=jax.ShapeDtypeStruct((spread.shap...  0.88 us
  transfers between devices with their start and end apart: 5, of which 4 were waited for; matrix products, arithmetic and copies ran while one was open for 0% of the time, Pallas kernels for 12%

profile of v2, /device:TPU:0, one launch (start us, length us, event | category | flops | bytes accessed | tf_op | source)
XLA Modules:
  0.0 37.3 jit_solution(11044348865066536666)
XLA Ops:
  0.0 0.7 %pack.1.packed_ref = bf16[12,768]{1,0:T(8,128)(2,1)S(1)} custom-call(bf16[8,768]{1,0:T(8,128)(2,1)} %bank_hbm.1, bf16[4,768]{1,0:T(4,128)(2,1)} %test_hbm.1), custom_call_target="tpu_custom_call" | custom-call | tf_op jit(solution)/shard_map/pack/pallas_call | solution.py:46
  0.7 3.5 %collective-permute-start = (bf16[12,768]{1,0:T(8,128)(2,1)S(1)}, bf16[12,768]{1,0:T(8,128)(2,1)S(1)}, u32[]{:S(2)}, u32[]{:S(2)}) collective-permute-start(bf16[12,768]{1,0:T(8,128)(2,1)S(1)} %pack.1.packed_ref), channel_id=1, source_target_pairs={{0,9},{1,8},{2,11},{3,10},{4,13},{5,12},{6,15},{7,14},{8,1},{9,0},... | collective-permute-start | bytes 55304 | tf_op jit(solution)/shard_map/ppermute | solution.py:273
  4.3 4.5 %load.1 = (bf16[4096,768]{1,0:T(8,128)(2,1)S(1)}, f32[8,512]{1,0:T(8,128)S(1)}, bf16[12,768]{1,0:T(8,128)(2,1)S(1)}, bf16[2,160,96]{2,1,0:T(8,128)(2,1)S(1)}, s3...) custom-call(bf16[4096,768]{1,0:T(8,128)(2,1)} %gallery_hbm.1, bf16[12,768]{1,0:T(8,128)(2,1)S(1)} %pack.1.packed_ref, ...), custom_call_target="tpu_custom_call" | custom-call | tf_op jit(solution)/shard_map/load/pallas_call | solution.py:153
  8.8 0.0 collective-permute-done
  8.9 1.9 %collective-permute-start.1 = (bf16[24,768]{1,0:T(8,128)(2,1)S(1)}, bf16[24,768]{1,0:T(8,128)(2,1)S(1)}, u32[]{:S(2)}, u32[]{:S(2)}) collective-permute-start(bf16[24,768]{1,0:T(8,128)(2,1)S(1)} %pad_maximum_fusion.2), channel_id=1, source_target_pairs={{0,5},{1,4},{2,7},{3,6},{4,1},{5,0},{6,3},{7,2},{8,13},{9,12},{10,... | collective-permute-start | bytes 110600 | tf_op jit(solution)/shard_map/ppermute | solution.py:273
  10.8 1.6 %collective-permute-done.1 = bf16[24,768]{1,0:T(8,128)(2,1)S(1)} collective-permute-done((bf16[24,768]{1,0:T(8,128)(2,1)S(1)}, bf16[24,768]{1,0:T(8,128)(2,1)S(1)}, u32[]{:S(2)}, u32[]{:S(2)}) %collective-permute-start.1) | collective-permute-done | bytes 36896 | tf_op jit(solution)/shard_map/ppermute | solution.py:273
  12.4 1.7 %collective-permute-start.2 = (bf16[48,768]{1,0:T(8,128)(2,1)S(1)}, bf16[48,768]{1,0:T(8,128)(2,1)S(1)}, u32[]{:S(2)}, u32[]{:S(2)}) collective-permute-start(bf16[48,768]{1,0:T(8,128)(2,1)S(1)} %pad_maximum_fusion.1), channel_id=1, source_target_pairs={{0,3},{1,2},{2,1},{3,0},{4,7},{5,6},{6,5},{7,4},{8,11},{9,10},{10,... | collective-permute-start | bytes 221192 | tf_op jit(solution)/shard_map/ppermute | solution.py:273
  14.2 2.2 %collective-permute-done.2 = bf16[48,768]{1,0:T(8,128)(2,1)S(1)} collective-permute-done((bf16[48,768]{1,0:T(8,128)(2,1)S(1)}, bf16[48,768]{1,0:T(8,128)(2,1)S(1)}, u32[]{:S(2)}, u32[]{:S(2)}) %collective-permute-start.2) | collective-permute-done | bytes 73760 | tf_op jit(solution)/shard_map/ppermute | solution.py:273
  16.4 0.6 %collective-permute-start.3 = (bf16[96,768]{1,0:T(8,128)(2,1)S(1)}, bf16[96,768]{1,0:T(8,128)(2,1)S(1)}, u32[]{:S(2)}, u32[]{:S(2)}) collective-permute-start(bf16[96,768]{1,0:T(8,128)(2,1)S(1)} %pad_maximum_fusion.first_ref), channel_id=1, source_target_pairs={{0,1},{1,0},{2,3},{3,2},{4,5},{5,4},{6,7},{7,6},{8,9},{9,8},{10,11... | collective-permute-start | bytes 442376 | tf_op jit(solution)/shard_map/ppermute | solution.py:273
  17.0 1.0 %collective-permute-done.3.second_ref = bf16[96,768]{1,0:T(8,128)(2,1)S(1)} collective-permute-done((bf16[96,768]{1,0:T(8,128)(2,1)S(1)}, bf16[96,768]{1,0:T(8,128)(2,1)S(1)}, u32[]{:S(2)}, u32[]{:S(2)}) %collective-permute-start.3) | collective-permute-done | bytes 147488 | tf_op jit(solution)/shard_map/ppermute | solution.py:273
  18.0 2.4 %score.1 = (f32[8,512]{1,0:T(8,128)S(1)}, f32[32,128]{1,0:T(8,128)S(1)}) custom-call(bf16[96,768]{1,0:T(8,128)(2,1)S(1)} %pad_maximum_fusion.first_ref, bf16[96,768]{1,0:T(8,128)(2,1)S(1)} %collective-permute-done.3.second_ref, bf16[2,160,96]{2,1,0:T(8,128)(2,1)S(1)} %get-tuple-element.14.pick_ref, bf16[4096,768]{1,0:T(8,128)(2,1)S(1)} %get-tuple-element.15.gallery_ref, ...), custom_call_target="tpu_custom_call" | custom-call | tf_op jit(solution)/shard_map/score/pallas_call | solution.py:203
  20.4 1.6 %collective-permute-start.4 = (f32[8,512]{1,0:T(8,128)S(1)}, f32[8,512]{1,0:T(8,128)S(1)}, u32[]{:S(2)}, u32[]{:S(2)}) collective-permute-start(f32[8,512]{1,0:T(8,128)S(1)} %get-tuple-element.19.own_ref), channel_id=1, source_target_pairs={{0,16},{16,0},{1,17},{17,1},{2,18},{18,2},{3,19},{19,3},{4,20},{20... | collective-permute-start | bytes 49160 | tf_op jit(solution)/shard_map/ppermute | solution.py:273
  22.0 2.2 %collective-permute-done.4.other_ref = f32[8,512]{1,0:T(8,128)S(1)} collective-permute-done((f32[8,512]{1,0:T(8,128)S(1)}, f32[8,512]{1,0:T(8,128)S(1)}, u32[]{:S(2)}, u32[]{:S(2)}) %collective-permute-start.4) | collective-permute-done | bytes 16416 | tf_op jit(solution)/shard_map/ppermute | solution.py:273
  24.2 1.2 %pool.1 = bf16[16,2,896]{2,1,0:T(2,128)(2,1)S(1)} custom-call(f32[32,128]{1,0:T(8,128)S(1)} %get-tuple-element.18.listed_ref, f32[8,512]{1,0:T(8,128)S(1)} %get-tuple-element.19.own_ref, f32[8,512]{1,0:T(8,128)S(1)} %collective-permute-done.4.other_ref, bf16[4096,768]{1,0:T(8,128)(2,1)S(1)} %get-tuple-element.15.gallery_ref, ...), custom_call_target="tpu_custom_call" | custom-call | tf_op jit(solution)/shard_map/pool/pallas_call | solution.py:241
  25.4 11.0 %all_to_all.5.sums_ref = bf16[16,2,896]{2,1,0:T(2,128)(2,1)S(1)} all-to-all(bf16[16,2,896]{2,1,0:T(2,128)(2,1)S(1)} %pool.1), channel_id=1, replica_groups=mesh['bank'=2,'gal'=16] {'gal'}, dimensions={0} | all-to-all | bytes 114688 | tf_op jit(solution)/shard_map/all_to_all | solution.py:302
  36.5 0.9 %finish.1 = f32[4,768]{1,0:T(4,128)} custom-call(bf16[16,2,896]{2,1,0:T(2,128)(2,1)S(1)} %all_to_all.5.sums_ref, f32[4,32]{1,0:T(4,128)S(1)} %get-tuple-element.20.spread_ref), custom_call_target="tpu_custom_call" | custom-call | tf_op jit(solution)/shard_map/finish/pallas_call | solution.py:262
  (3 shorter events, 0.1 us)
Async XLA Ops:
  0.7 8.1 %collective-permute-start = (bf16[12,768]{1,0:T(8,128)(2,1)S(1)}, bf16[12,768]{1,0:T(8,128)(2,1)S(1)}, u32[]{:S(2)}, u32[]{:S(2)}) collective-permute-start(bf16[12,768]{1,0:T(8,128)(2,1)S(1)} %pack.1.packed_ref), channel_id=1, source_target_pairs={{0,9},{1,8},{2,11},{3,10},{4,13},{5,12},{6,15},{7,14},{8,1},{9,0},... | collective-permute-start | bytes 55304 | tf_op jit(solution)/shard_map/ppermute | solution.py:273
  8.9 3.6 %collective-permute-start.1 = (bf16[24,768]{1,0:T(8,128)(2,1)S(1)}, bf16[24,768]{1,0:T(8,128)(2,1)S(1)}, u32[]{:S(2)}, u32[]{:S(2)}) collective-permute-start(bf16[24,768]{1,0:T(8,128)(2,1)S(1)} %pad_maximum_fusion.2), channel_id=1, source_target_pairs={{0,5},{1,4},{2,7},{3,6},{4,1},{5,0},{6,3},{7,2},{8,13},{9,12},{10,... | collective-permute-start | bytes 110600 | tf_op jit(solution)/shard_map/ppermute | solution.py:273
  12.4 3.9 %collective-permute-start.2 = (bf16[48,768]{1,0:T(8,128)(2,1)S(1)}, bf16[48,768]{1,0:T(8,128)(2,1)S(1)}, u32[]{:S(2)}, u32[]{:S(2)}) collective-permute-start(bf16[48,768]{1,0:T(8,128)(2,1)S(1)} %pad_maximum_fusion.1), channel_id=1, source_target_pairs={{0,3},{1,2},{2,1},{3,0},{4,7},{5,6},{6,5},{7,4},{8,11},{9,10},{10,... | collective-permute-start | bytes 221192 | tf_op jit(solution)/shard_map/ppermute | solution.py:273
  16.4 1.6 %collective-permute-start.3 = (bf16[96,768]{1,0:T(8,128)(2,1)S(1)}, bf16[96,768]{1,0:T(8,128)(2,1)S(1)}, u32[]{:S(2)}, u32[]{:S(2)}) collective-permute-start(bf16[96,768]{1,0:T(8,128)(2,1)S(1)} %pad_maximum_fusion.first_ref), channel_id=1, source_target_pairs={{0,1},{1,0},{2,3},{3,2},{4,5},{5,4},{6,7},{7,6},{8,9},{9,8},{10,11... | collective-permute-start | bytes 442376 | tf_op jit(solution)/shard_map/ppermute | solution.py:273
  20.4 3.8 %collective-permute-start.4 = (f32[8,512]{1,0:T(8,128)S(1)}, f32[8,512]{1,0:T(8,128)S(1)}, u32[]{:S(2)}, u32[]{:S(2)}) collective-permute-start(f32[8,512]{1,0:T(8,128)S(1)} %get-tuple-element.19.own_ref), channel_id=1, source_target_pairs={{0,16},{16,0},{1,17},{17,1},{2,18},{18,2},{3,19},{19,3},{4,20},{20... | collective-permute-start | bytes 49160 | tf_op jit(solution)/shard_map/ppermute | solution.py:273

commit v3 on v2

--- a/solution.py
+++ b/solution.py
@@ -269,6 +269,26 @@
     )(sums, keep(spread))
 
 
+def join_kernel(*refs):
+    *pieces, out_ref = refs
+    row = 0
+    for piece in pieces:
+        out_ref[row : row + piece.shape[0], :] = piece[...]
+        row += piece.shape[0]
+
+
+def join(pieces):
+    rows = sum(piece.shape[0] for piece in pieces)
+    return pl.pallas_call(
+        join_kernel,
+        out_shape=pltpu.VMEM((rows, pieces[0].shape[1]), pieces[0].dtype),
+        in_specs=[VMEM] * len(pieces),
+        out_specs=VMEM,
+        compiler_params=PARAMS,
+        name="join",
+    )(*pieces)
+
+
 def swap(value, axis, size, bit):
     return lax.ppermute(value, axis, [(i, i ^ bit) for i in range(size)])
 
@@ -276,19 +296,23 @@
 def body(devices, banks, bank_queries, gallery, test_queries, test_slabs, test_offsets):
     bank_own, test_own = bank_queries.shape[0], test_queries.shape[0]
 
-    masks = [devices >> (i + 1) | 1 for i in range(devices.bit_length() - 1)]
+    rounds = [[1 << k | 1] for k in range(devices.bit_length() - 2, 2, -1)] + [[5, 3], [1]]
+    masks = [mask for masks in rounds for mask in masks]
     order = [0]
     for mask in masks:
         order = order + [o ^ mask for o in order]
 
     packed = pack(bank_queries, test_queries)
-    other = swap(packed, "gal", devices, masks[0])
+    other = swap(packed, "gal", devices, rounds[0][0])
     gallery, scale, packed, pick, block, spread = load(
         masks, bank_own, test_own, gallery, packed, test_slabs.T, test_offsets.T
     )
-    for mask in masks[1:]:
-        packed = jnp.concatenate([packed, other], axis=0)
-        other = swap(packed, "gal", devices, mask)
+    others = [other]
+    for near in rounds[1:]:
+        packed = join([packed, *others])
+        toward = near if len(near) == 1 else [near[0], near[1], near[0] ^ near[1]]
+        others = [swap(packed, "gal", devices, mask) for mask in toward]
+    other = others[0]
 
     colsum, listed = score(packed, other, pick, gallery, scale, block)
     bit = banks // 2

time: 37.6 us -> 35.1 us (0.934)
  blocking collectives: 11 us -> 9.53 us
  starting transfers between devices: 9.37 us -> 8.56 us
    all_to_all x1, blocking collectives: 11 us -> 9.53 us  [body(): sums = lax.all_to_all(sums, 'gal', 0, 0, tiled=True)]
    ppermute x5 -> x6, starting transfers between devices: 9.37 us -> 8.56 us  [swap(): return lax.ppermute(value, axis, [(i, i ^ bit) for i in range(size)])]
    ppermute x5 -> x6, waiting for transfers between devices: 7.08 us -> 6.88 us  [swap(): return lax.ppermute(value, axis, [(i, i ^ bit) for i in range(size)])]
  transfers between devices with their start and end apart: 5 -> 6, of which waited for: 4 -> 5; matrix products, arithmetic and copies ran while one was open for 0% -> 0% of each run, Pallas kernels for 12% -> 13%
where the time goes in v3:
time: 35.1 us; the launch traced here: 34.8 us
  Pallas kernels  9.77 us (28%)
  blocking collectives  9.53 us (27%)
  starting transfers between devices  8.56 us (24%)
  waiting for transfers between devices  6.88 us (20%)
    all_to_all x1, blocking collectives, body(): sums = lax.all_to_all(sums, 'gal', 0, 0, tiled=True)  9.53 us
    ppermute x6, starting transfers between devices, swap(): return lax.ppermute(value, axis, [(i, i ^ bit) for i in range(size)])  8.56 us
    ppermute x6, waiting for transfers between devices, swap(): return lax.ppermute(value, axis, [(i, i ^ bit) for i in range(size)])  6.88 us
    pallas_call x1, Pallas kernels, load(): pl.pallas_call(functools.partial(load_kernel, masks, bank_own, test_own),...  4.54 us
    pallas_call x1, Pallas kernels, score(): pl.pallas_call(score_kernel, out_shape=(pltpu.VMEM(scale.shape, jnp.float...  2.43 us
    pallas_call x1, Pallas kernels, pool(): pl.pallas_call(functools.partial(pool_kernel, order), out_shape=pltpu.VME...  1.18 us
    pallas_call x1, Pallas kernels, finish(): pl.pallas_call(finish_kernel, out_shape=jax.ShapeDtypeStruct((spread.shap...  0.88 us
    pallas_call x1, Pallas kernels, pack(): pl.pallas_call(pack_kernel, out_shape=pltpu.VMEM((bank.shape[0] + test.sh...  0.73 us
  transfers between devices with their start and end apart: 6, of which 5 were waited for; matrix products, arithmetic and copies ran while one was open for 0% of the time, Pallas kernels for 13%

profile of v3, /device:TPU:0, one launch (start us, length us, event | category | flops | bytes accessed | tf_op | source)
XLA Modules:
  0.0 34.8 jit_solution(5823290635577383860)
XLA Ops:
  0.0 0.7 %pack.1.packed_ref = bf16[12,768]{1,0:T(8,128)(2,1)S(1)} custom-call(bf16[8,768]{1,0:T(8,128)(2,1)} %bank_hbm.1, bf16[4,768]{1,0:T(4,128)(2,1)} %test_hbm.1), custom_call_target="tpu_custom_call" | custom-call | tf_op jit(solution)/shard_map/pack/pallas_call | solution.py:46
  0.7 3.5 %collective-permute-start = (bf16[12,768]{1,0:T(8,128)(2,1)S(1)}, bf16[12,768]{1,0:T(8,128)(2,1)S(1)}, u32[]{:S(2)}, u32[]{:S(2)}) collective-permute-start(bf16[12,768]{1,0:T(8,128)(2,1)S(1)} %pack.1.packed_ref), channel_id=1, source_target_pairs={{0,9},{1,8},{2,11},{3,10},{4,13},{5,12},{6,15},{7,14},{8,1},{9,0},... | collective-permute-start | bytes 55304 | tf_op jit(solution)/shard_map/ppermute | solution.py:293
  4.3 4.5 %load.1 = (bf16[4096,768]{1,0:T(8,128)(2,1)S(1)}, f32[8,512]{1,0:T(8,128)S(1)}, bf16[12,768]{1,0:T(8,128)(2,1)S(1)}, bf16[2,160,96]{2,1,0:T(8,128)(2,1)S(1)}, s3...) custom-call(bf16[4096,768]{1,0:T(8,128)(2,1)} %gallery_hbm.1, bf16[12,768]{1,0:T(8,128)(2,1)S(1)} %pack.1.packed_ref, ...), custom_call_target="tpu_custom_call" | custom-call | tf_op jit(solution)/shard_map/load/pallas_call | solution.py:153
  8.8 0.0 collective-permute-done.refs_1_
  8.9 2.6 %collective-permute-start.3 = (bf16[24,768]{1,0:T(8,128)(2,1)S(1)}, bf16[24,768]{1,0:T(8,128)(2,1)S(1)}, u32[]{:S(2)}, u32[]{:S(2)}) collective-permute-start(bf16[24,768]{1,0:T(8,128)(2,1)S(1)} %join.2.refs_0_), channel_id=1, source_target_pairs={{0,6},{1,7},{2,4},{3,5},{4,2},{5,3},{6,0},{7,1},{8,14},{9,15},{10,... | collective-permute-start | bytes 110600 | tf_op jit(solution)/shard_map/ppermute | solution.py:293
  11.4 0.5 %collective-permute-start.2 = (bf16[24,768]{1,0:T(8,128)(2,1)S(1)}, bf16[24,768]{1,0:T(8,128)(2,1)S(1)}, u32[]{:S(2)}, u32[]{:S(2)}) collective-permute-start(bf16[24,768]{1,0:T(8,128)(2,1)S(1)} %join.2.refs_0_), channel_id=1, source_target_pairs={{0,3},{1,2},{2,1},{3,0},{4,7},{5,6},{6,5},{7,4},{8,11},{9,10},{10,... | collective-permute-start | bytes 110600 | tf_op jit(solution)/shard_map/ppermute | solution.py:293
  12.0 0.1 collective-permute-start.1
  12.1 1.7 %collective-permute-done.3.refs_3_ = bf16[24,768]{1,0:T(8,128)(2,1)S(1)} collective-permute-done((bf16[24,768]{1,0:T(8,128)(2,1)S(1)}, bf16[24,768]{1,0:T(8,128)(2,1)S(1)}, u32[]{:S(2)}, u32[]{:S(2)}) %collective-permute-start.3) | collective-permute-done | bytes 36896 | tf_op jit(solution)/shard_map/ppermute | solution.py:293
  13.9 1.0 %collective-permute-done.2.refs_2_ = bf16[24,768]{1,0:T(8,128)(2,1)S(1)} collective-permute-done((bf16[24,768]{1,0:T(8,128)(2,1)S(1)}, bf16[24,768]{1,0:T(8,128)(2,1)S(1)}, u32[]{:S(2)}, u32[]{:S(2)}) %collective-permute-start.2) | collective-permute-done | bytes 36896 | tf_op jit(solution)/shard_map/ppermute | solution.py:293
  14.8 0.7 %collective-permute-done.1.refs_1_ = bf16[24,768]{1,0:T(8,128)(2,1)S(1)} collective-permute-done((bf16[24,768]{1,0:T(8,128)(2,1)S(1)}, bf16[24,768]{1,0:T(8,128)(2,1)S(1)}, u32[]{:S(2)}, u32[]{:S(2)}) %collective-permute-start.1) | collective-permute-done | bytes 36896 | tf_op jit(solution)/shard_map/ppermute | solution.py:293
  15.5 0.2 collective-permute-start.4
  15.7 1.3 %collective-permute-done.4.second_ref = bf16[96,768]{1,0:T(8,128)(2,1)S(1)} collective-permute-done((bf16[96,768]{1,0:T(8,128)(2,1)S(1)}, bf16[96,768]{1,0:T(8,128)(2,1)S(1)}, u32[]{:S(2)}, u32[]{:S(2)}) %collective-permute-start.4) | collective-permute-done | bytes 147488 | tf_op jit(solution)/shard_map/ppermute | solution.py:293
  17.0 2.4 %score.1 = (f32[8,512]{1,0:T(8,128)S(1)}, f32[32,128]{1,0:T(8,128)S(1)}) custom-call(bf16[96,768]{1,0:T(8,128)(2,1)S(1)} %join.3.first_ref, bf16[96,768]{1,0:T(8,128)(2,1)S(1)} %collective-permute-done.4.second_ref, bf16[2,160,96]{2,1,0:T(8,128)(2,1)S(1)} %get-tuple-element.14.pick_ref, bf16[4096,768]{1,0:T(8,128)(2,1)S(1)} %get-tuple-element.15.gallery_ref, ...), custom_call_target="tpu_custom_call" | custom-call | tf_op jit(solution)/shard_map/score/pallas_call | solution.py:203
  19.4 1.6 %collective-permute-start.5 = (f32[8,512]{1,0:T(8,128)S(1)}, f32[8,512]{1,0:T(8,128)S(1)}, u32[]{:S(2)}, u32[]{:S(2)}) collective-permute-start(f32[8,512]{1,0:T(8,128)S(1)} %get-tuple-element.19.own_ref), channel_id=1, source_target_pairs={{0,16},{16,0},{1,17},{17,1},{2,18},{18,2},{3,19},{19,3},{4,20},{20... | collective-permute-start | bytes 49160 | tf_op jit(solution)/shard_map/ppermute | solution.py:293
  21.0 2.2 %collective-permute-done.5.other_ref = f32[8,512]{1,0:T(8,128)S(1)} collective-permute-done((f32[8,512]{1,0:T(8,128)S(1)}, f32[8,512]{1,0:T(8,128)S(1)}, u32[]{:S(2)}, u32[]{:S(2)}) %collective-permute-start.5) | collective-permute-done | bytes 16416 | tf_op jit(solution)/shard_map/ppermute | solution.py:293
  23.2 1.2 %pool.1 = bf16[16,2,896]{2,1,0:T(2,128)(2,1)S(1)} custom-call(f32[32,128]{1,0:T(8,128)S(1)} %get-tuple-element.18.listed_ref, f32[8,512]{1,0:T(8,128)S(1)} %get-tuple-element.19.own_ref, f32[8,512]{1,0:T(8,128)S(1)} %collective-permute-done.5.other_ref, bf16[4096,768]{1,0:T(8,128)(2,1)S(1)} %get-tuple-element.15.gallery_ref, ...), custom_call_target="tpu_custom_call" | custom-call | tf_op jit(solution)/shard_map/pool/pallas_call | solution.py:241
  24.4 9.5 %all_to_all.5.sums_ref = bf16[16,2,896]{2,1,0:T(2,128)(2,1)S(1)} all-to-all(bf16[16,2,896]{2,1,0:T(2,128)(2,1)S(1)} %pool.1), channel_id=1, replica_groups=mesh['bank'=2,'gal'=16] {'gal'}, dimensions={0} | all-to-all | bytes 114688 | tf_op jit(solution)/shard_map/all_to_all | solution.py:326
  33.9 0.9 %finish.1 = f32[4,768]{1,0:T(4,128)} custom-call(bf16[16,2,896]{2,1,0:T(2,128)(2,1)S(1)} %all_to_all.5.sums_ref, f32[4,32]{1,0:T(4,128)S(1)} %get-tuple-element.20.spread_ref), custom_call_target="tpu_custom_call" | custom-call | tf_op jit(solution)/shard_map/finish/pallas_call | solution.py:262
  (2 shorter events, 0.0 us)
Async XLA Ops:
  0.7 8.1 %collective-permute-start = (bf16[12,768]{1,0:T(8,128)(2,1)S(1)}, bf16[12,768]{1,0:T(8,128)(2,1)S(1)}, u32[]{:S(2)}, u32[]{:S(2)}) collective-permute-start(bf16[12,768]{1,0:T(8,128)(2,1)S(1)} %pack.1.packed_ref), channel_id=1, source_target_pairs={{0,9},{1,8},{2,11},{3,10},{4,13},{5,12},{6,15},{7,14},{8,1},{9,0},... | collective-permute-start | bytes 55304 | tf_op jit(solution)/shard_map/ppermute | solution.py:293
  8.9 5.0 %collective-permute-start.3 = (bf16[24,768]{1,0:T(8,128)(2,1)S(1)}, bf16[24,768]{1,0:T(8,128)(2,1)S(1)}, u32[]{:S(2)}, u32[]{:S(2)}) collective-permute-start(bf16[24,768]{1,0:T(8,128)(2,1)S(1)} %join.2.refs_0_), channel_id=1, source_target_pairs={{0,6},{1,7},{2,4},{3,5},{4,2},{5,3},{6,0},{7,1},{8,14},{9,15},{10,... | collective-permute-start | bytes 110600 | tf_op jit(solution)/shard_map/ppermute | solution.py:293
  11.4 3.4 %collective-permute-start.2 = (bf16[24,768]{1,0:T(8,128)(2,1)S(1)}, bf16[24,768]{1,0:T(8,128)(2,1)S(1)}, u32[]{:S(2)}, u32[]{:S(2)}) collective-permute-start(bf16[24,768]{1,0:T(8,128)(2,1)S(1)} %join.2.refs_0_), channel_id=1, source_target_pairs={{0,3},{1,2},{2,1},{3,0},{4,7},{5,6},{6,5},{7,4},{8,11},{9,10},{10,... | collective-permute-start | bytes 110600 | tf_op jit(solution)/shard_map/ppermute | solution.py:293
  12.0 3.5 %collective-permute-start.1 = (bf16[24,768]{1,0:T(8,128)(2,1)S(1)}, bf16[24,768]{1,0:T(8,128)(2,1)S(1)}, u32[]{:S(2)}, u32[]{:S(2)}) collective-permute-start(bf16[24,768]{1,0:T(8,128)(2,1)S(1)} %join.2.refs_0_), channel_id=1, source_target_pairs={{0,5},{1,4},{2,7},{3,6},{4,1},{5,0},{6,3},{7,2},{8,13},{9,12},{10,... | collective-permute-start | bytes 110600 | tf_op jit(solution)/shard_map/ppermute | solution.py:293
  15.5 1.4 %collective-permute-start.4 = (bf16[96,768]{1,0:T(8,128)(2,1)S(1)}, bf16[96,768]{1,0:T(8,128)(2,1)S(1)}, u32[]{:S(2)}, u32[]{:S(2)}) collective-permute-start(bf16[96,768]{1,0:T(8,128)(2,1)S(1)} %join.3.first_ref), channel_id=1, source_target_pairs={{0,1},{1,0},{2,3},{3,2},{4,5},{5,4},{6,7},{7,6},{8,9},{9,8},{10,11... | collective-permute-start | bytes 442376 | tf_op jit(solution)/shard_map/ppermute | solution.py:293
  19.4 3.8 %collective-permute-start.5 = (f32[8,512]{1,0:T(8,128)S(1)}, f32[8,512]{1,0:T(8,128)S(1)}, u32[]{:S(2)}, u32[]{:S(2)}) collective-permute-start(f32[8,512]{1,0:T(8,128)S(1)} %get-tuple-element.19.own_ref), channel_id=1, source_target_pairs={{0,16},{16,0},{1,17},{17,1},{2,18},{18,2},{3,19},{19,3},{4,20},{20... | collective-permute-start | bytes 49160 | tf_op jit(solution)/shard_map/ppermute | solution.py:293

commit v4 on v3

--- a/solution.py
+++ b/solution.py
@@ -69,12 +69,10 @@
     return lax.broadcasted_iota(jnp.int32, shape, axis)
 
 
-def route(masks, bank_own, test_own, slabs, offsets, pick_ref, block_ref, spread_ref):
+def route(masks, test_own, slabs, offsets, pick_ref, block_ref, spread_ref):
     me = lax.axis_index("gal")
     devices = 1 << len(masks)
     group = devices * test_own
-    own = bank_own + test_own
-    bank_rows = devices * bank_own
     slots = devices * CAP
 
     found = jnp.sum(jnp.where(slabs == me, offsets + 1, 0), axis=0, keepdims=True)
@@ -91,15 +89,11 @@
     block_ref[...] = jnp.broadcast_to(block, block_ref.shape)
     from_row = jnp.sum(jnp.where(filled, column % test_own + 1, 0), axis=1, keepdims=True)
     index = iota((slots, 1), 0) // CAP
-    slot_from = jnp.where(from_row > 0, index * own + bank_own - 1 + from_row, -1)
-    index = iota((bank_rows, 1), 0)
-    bank_from = index // bank_own * own + index % bank_own
+    slot_from = jnp.where(from_row > 0, index * test_own - 1 + from_row, -1)
     half = pick_ref.shape[2]
     for h in range(2):
-        column = iota((bank_rows, half), 1) + h * half
-        pick_ref[h, :bank_rows, :] = jnp.where(column == bank_from, 1.0, 0.0).astype(jnp.bfloat16)
         column = iota((slots, half), 1) + h * half
-        pick_ref[h, bank_rows:, :] = jnp.where(column == slot_from, 1.0, 0.0).astype(jnp.bfloat16)
+        pick_ref[h] = jnp.where(column == slot_from, 1.0, 0.0).astype(jnp.bfloat16)
 
     lane = iota((1, slots), 1)
     filled_before = jnp.zeros((1, slots), jnp.int32)
@@ -112,8 +106,8 @@
 
 
 def load_kernel(
-    masks, bank_own, test_own, gallery_hbm, packed_ref, slabs_hbm, offsets_hbm,
-    gallery_ref, scale_ref, packed_out, pick_ref, block_ref, spread_ref, slabs_ref, offsets_ref, sems, small_sems,
+    masks, test_own, gallery_hbm, packed_ref, slabs_hbm, offsets_hbm,
+    gallery_ref, turned_ref, scale_ref, packed_out, pick_ref, block_ref, spread_ref, slabs_ref, offsets_ref, sems, small_sems,
 ):
     rows, depth = gallery_hbm.shape
     part = rows // CHUNKS
@@ -130,38 +124,35 @@
     for copy in small + copies:
         copy.start()
     packed_out[...] = packed_ref[...]
-    for copy in small:
-        copy.wait()
-    route(masks, bank_own, test_own, slabs_ref[...], offsets_ref[...], pick_ref, block_ref, spread_ref)
     for c in range(CHUNKS):
         copies[c].wait()
-        values = gallery_ref[pl.ds(c * part, part), :].astype(jnp.float32)
-        squares = values * values
-        folded = squares[:, :LANES]
-        for k in range(1, depth // LANES):
-            folded = folded + squares[:, k * LANES : (k + 1) * LANES]
-        for b in range(part // BLOCK):
-            total = jnp.sum(folded[b * BLOCK : (b + 1) * BLOCK].T, axis=0, keepdims=True)
-            scale_ref[c : c + 1, b * BLOCK : (b + 1) * BLOCK] = lax.rsqrt(total + epsilon)
-
-
-def load(masks, bank_own, test_own, gallery, packed, slabs, offsets):
+        if c == 7:
+            for copy in small:
+                copy.wait()
+            route(masks, test_own, slabs_ref[...], offsets_ref[...], pick_ref, block_ref, spread_ref)
+        turned = gallery_ref[pl.ds(c * part, part), :].T
+        turned_ref[:, c * part : (c + 1) * part] = turned
+        values = turned.astype(jnp.float32)
+        scale_ref[c : c + 1, :] = lax.rsqrt(jnp.sum(values * values, axis=0, keepdims=True) + epsilon)
+
+
+def load(masks, test_own, gallery, packed, slabs, offsets):
     rows, depth = gallery.shape
     devices = 1 << len(masks)
     slots = devices * CAP
-    half = devices * (bank_own + test_own) // 2
-    return pl.pallas_call(
-        functools.partial(load_kernel, masks, bank_own, test_own),
+    return pl.pallas_call(
+        functools.partial(load_kernel, masks, test_own),
         out_shape=(
             pltpu.VMEM(gallery.shape, gallery.dtype),
+            pltpu.VMEM((depth, rows), gallery.dtype),
             pltpu.VMEM((CHUNKS, rows // CHUNKS), jnp.float32),
             pltpu.VMEM(packed.shape, packed.dtype),
-            pltpu.VMEM((2, devices * bank_own + slots, half), jnp.bfloat16),
+            pltpu.VMEM((2, slots, devices * test_own // 2), jnp.bfloat16),
             pltpu.VMEM((slots, LANES), jnp.int32),
             pltpu.VMEM((test_own, slots), jnp.float32),
         ),
         in_specs=[HBM, VMEM, HBM, HBM],
-        out_specs=(VMEM,) * 6,
+        out_specs=(VMEM,) * 7,
         scratch_shapes=[
             pltpu.VMEM(slabs.shape, slabs.dtype),
             pltpu.VMEM(offsets.shape, offsets.dtype),
@@ -173,41 +164,58 @@
     )(in_hbm(gallery), packed, in_hbm(slabs), in_hbm(offsets))
 
 
-def score_kernel(first_ref, second_ref, pick_ref, gallery_ref, scale_ref, block_ref, colsum_ref, listed_ref):
-    wide = jnp.dot(pick_ref[0], first_ref[...], preferred_element_type=jnp.float32)
-    wide = wide + jnp.dot(pick_ref[1], second_ref[...], preferred_element_type=jnp.float32)
+def scales(wide):
+    return lax.rsqrt(jnp.sum(wide * wide, axis=1, keepdims=True) + epsilon) * (SHARPNESS * LOG2E)
+
+
+def bank_kernel(bank_rows, first_ref, second_ref, turned_ref, scale_ref, colsum_ref):
+    queries = jnp.concatenate([first_ref[:bank_rows], second_ref[:bank_rows]], axis=0)
+    query_scale = scales(queries.astype(jnp.float32))
+    part = scale_ref.shape[1]
+    for c in range(CHUNKS):
+        scores = jnp.dot(queries, turned_ref[:, c * part : (c + 1) * part], preferred_element_type=jnp.float32)
+        exps = jnp.exp2(scores * scale_ref[c : c + 1, :] * query_scale)
+        colsum_ref[c : c + 1, :] = jnp.sum(exps, axis=0, keepdims=True)
+
+
+def score_bank(bank_rows, first, second, turned, scale):
+    return pl.pallas_call(
+        functools.partial(bank_kernel, bank_rows),
+        out_shape=pltpu.VMEM(scale.shape, jnp.float32),
+        in_specs=[VMEM] * 4,
+        out_specs=VMEM,
+        compiler_params=PARAMS,
+        name="score_bank",
+    )(keep(first), second, keep(turned), keep(scale))
+
+
+def test_kernel(
+    bank_rows, first_ref, second_ref, pick_ref, turned_ref, scale_ref, block_ref, colsum_ref, listed_ref, colsum_out
+):
+    colsum_out[...] = colsum_ref[...]
+    wide = jnp.dot(pick_ref[0], first_ref[bank_rows:], preferred_element_type=jnp.float32)
+    wide = wide + jnp.dot(pick_ref[1], second_ref[bank_rows:], preferred_element_type=jnp.float32)
     queries = wide.astype(jnp.bfloat16)
-    query_scale = lax.rsqrt(jnp.sum(wide * wide, axis=1, keepdims=True) + epsilon) * (SHARPNESS * LOG2E)
-    slots = block_ref.shape[0]
-    bank_rows = queries.shape[0] - slots
     part = scale_ref.shape[1]
     block = block_ref[...]
-    picked = jnp.zeros((slots, BLOCK), jnp.float32)
+    picked = jnp.zeros(listed_ref.shape, jnp.float32)
     for c in range(CHUNKS):
-        scores = lax.dot_general(
-            queries,
-            gallery_ref[pl.ds(c * part, part), :],
-            (((1,), (1,)), ((), ())),
-            preferred_element_type=jnp.float32,
-        )
+        scores = jnp.dot(queries, turned_ref[:, c * part : (c + 1) * part], preferred_element_type=jnp.float32)
         scores = scores * scale_ref[c : c + 1, :]
-        exps = jnp.exp2(scores[:bank_rows] * query_scale[:bank_rows])
-        colsum_ref[c : c + 1, :] = jnp.sum(exps, axis=0, keepdims=True)
         for b in range(part // BLOCK):
-            here = scores[bank_rows:, b * BLOCK : (b + 1) * BLOCK]
-            picked = jnp.where(block == c * (part // BLOCK) + b, here, picked)
-    listed_ref[...] = jnp.exp2(picked * query_scale[bank_rows:])
-
-
-def score(first, second, pick, gallery, scale, block):
-    return pl.pallas_call(
-        score_kernel,
-        out_shape=(pltpu.VMEM(scale.shape, jnp.float32), pltpu.VMEM((block.shape[0], BLOCK), jnp.float32)),
-        in_specs=[VMEM] * 6,
+            picked = jnp.where(block == c * (part // BLOCK) + b, scores[:, b * BLOCK : (b + 1) * BLOCK], picked)
+    listed_ref[...] = jnp.exp2(picked * scales(wide))
+
+
+def score_tests(bank_rows, first, second, pick, turned, scale, block, colsum):
+    return pl.pallas_call(
+        functools.partial(test_kernel, bank_rows),
+        out_shape=(pltpu.VMEM((block.shape[0], BLOCK), jnp.float32), pltpu.VMEM(colsum.shape, jnp.float32)),
+        in_specs=[VMEM] * 7,
         out_specs=(VMEM, VMEM),
         compiler_params=PARAMS,
-        name="score",
-    )(keep(first), second, keep(pick), keep(gallery), keep(scale), keep(block))
+        name="score_tests",
+    )(keep(first), keep(second), keep(pick), keep(turned), keep(scale), keep(block), keep(colsum))
 
 
 def pool_kernel(order, listed_ref, own_ref, other_ref, gallery_ref, block_ref, out_ref, weight_ref):
@@ -269,18 +277,21 @@
     )(sums, keep(spread))
 
 
-def join_kernel(*refs):
+def join_kernel(bank_own, own, *refs):
     *pieces, out_ref = refs
-    row = 0
+    bank, test = 0, sum(piece.shape[0] for piece in pieces) // own * bank_own
     for piece in pieces:
-        out_ref[row : row + piece.shape[0], :] = piece[...]
-        row += piece.shape[0]
-
-
-def join(pieces):
+        rows = piece.shape[0]
+        split = rows // own * bank_own
+        out_ref[bank : bank + split, :] = piece[:split]
+        out_ref[test : test + rows - split, :] = piece[split:]
+        bank, test = bank + split, test + rows - split
+
+
+def join(bank_own, test_own, pieces):
     rows = sum(piece.shape[0] for piece in pieces)
     return pl.pallas_call(
-        join_kernel,
+        functools.partial(join_kernel, bank_own, bank_own + test_own),
         out_shape=pltpu.VMEM((rows, pieces[0].shape[1]), pieces[0].dtype),
         in_specs=[VMEM] * len(pieces),
         out_specs=VMEM,
@@ -304,17 +315,19 @@
 
     packed = pack(bank_queries, test_queries)
     other = swap(packed, "gal", devices, rounds[0][0])
-    gallery, scale, packed, pick, block, spread = load(
-        masks, bank_own, test_own, gallery, packed, test_slabs.T, test_offsets.T
+    gallery, turned, scale, packed, pick, block, spread = load(
+        masks, test_own, gallery, packed, test_slabs.T, test_offsets.T
     )
     others = [other]
     for near in rounds[1:]:
-        packed = join([packed, *others])
+        packed = join(bank_own, test_own, [packed, *others])
         toward = near if len(near) == 1 else [near[0], near[1], near[0] ^ near[1]]
         others = [swap(packed, "gal", devices, mask) for mask in toward]
     other = others[0]
 
-    colsum, listed = score(packed, other, pick, gallery, scale, block)
+    bank_rows = devices // 2 * bank_own
+    first, second = packed, other
+    colsum = score_bank(bank_rows, first, second, turned, scale)
     bit = banks // 2
     other = jnp.zeros_like(colsum)
     while bit:
@@ -322,6 +335,7 @@
         bit //= 2
         if bit:
             colsum = colsum + other
+    listed, colsum = score_tests(bank_rows, first, second, pick, turned, scale, block, colsum)
     sums = pool(order, listed, colsum, other, gallery, block)
     sums = lax.all_to_all(sums, "gal", 0, 0, tiled=True)
     return finish(sums, spread)

time: 35.1 us -> 33.6 us (0.957)
  waiting for transfers between devices: 6.88 us -> 5.56 us
  Pallas kernels: 9.77 us -> 8.87 us
  blocking collectives: 9.53 us -> 10.3 us
    ppermute x6, waiting for transfers between devices: 6.88 us -> 5.56 us  [swap(): return lax.ppermute(value, axis, [(i, i ^ bit) for i in range(size)])]
    pallas_call x4 -> x5, Pallas kernels: 6.99 us -> 6.08 us  [the longest x1 3.59 us: load(): pl.pallas_call(functools.partial(load_kernel, masks, test_own), out_shape...]
    all_to_all x1, blocking collectives: 9.53 us -> 10.3 us  [body(): sums = lax.all_to_all(sums, 'gal', 0, 0, tiled=True)]
  transfers between devices with their start and end apart: 6 -> 6, of which waited for: 5 -> 5; matrix products, arithmetic and copies ran while one was open for 0% -> 0% of each run, Pallas kernels for 13% -> 15%
where the time goes in v4:
time: 33.6 us; the launch traced here: 33.3 us
  blocking collectives  10.3 us (31%)
  Pallas kernels  8.87 us (26%)
  starting transfers between devices  8.55 us (25%)
  waiting for transfers between devices  5.56 us (17%)
    all_to_all x1, blocking collectives, body(): sums = lax.all_to_all(sums, 'gal', 0, 0, tiled=True)  10.3 us
    ppermute x6, starting transfers between devices, swap(): return lax.ppermute(value, axis, [(i, i ^ bit) for i in range(size)])  8.55 us
    ppermute x6, waiting for transfers between devices, swap(): return lax.ppermute(value, axis, [(i, i ^ bit) for i in range(size)])  5.56 us
    pallas_call x1, Pallas kernels, load(): pl.pallas_call(functools.partial(load_kernel, masks, test_own), out_shape...  3.59 us
    pallas_call x1, Pallas kernels, score_tests(): pl.pallas_call(functools.partial(test_kernel, bank_rows), out_shape=(pltp...  1.31 us
    pallas_call x1, Pallas kernels, pool(): pl.pallas_call(functools.partial(pool_kernel, order), out_shape=pltpu.VME...  1.18 us
    pallas_call x1, Pallas kernels, score_bank(): pl.pallas_call(functools.partial(bank_kernel, bank_rows), out_shape=pltpu...  1.16 us
    pallas_call x1, Pallas kernels, finish(): pl.pallas_call(finish_kernel, out_shape=jax.ShapeDtypeStruct((spread.shap...  0.88 us
  transfers between devices with their start and end apart: 6, of which 5 were waited for; matrix products, arithmetic and copies ran while one was open for 0% of the time, Pallas kernels for 15%

profile of v4, /device:TPU:0, one launch (start us, length us, event | category | flops | bytes accessed | tf_op | source)
XLA Modules:
  0.0 33.3 jit_solution(17259307762389490933)
XLA Ops:
  0.0 0.7 %pack.1.packed_ref = bf16[12,768]{1,0:T(8,128)(2,1)S(1)} custom-call(bf16[8,768]{1,0:T(8,128)(2,1)} %bank_hbm.1, bf16[4,768]{1,0:T(4,128)(2,1)} %test_hbm.1), custom_call_target="tpu_custom_call" | custom-call | tf_op jit(solution)/shard_map/pack/pallas_call | solution.py:46
  0.7 3.5 %collective-permute-start = (bf16[12,768]{1,0:T(8,128)(2,1)S(1)}, bf16[12,768]{1,0:T(8,128)(2,1)S(1)}, u32[]{:S(2)}, u32[]{:S(2)}) collective-permute-start(bf16[12,768]{1,0:T(8,128)(2,1)S(1)} %pack.1.packed_ref), channel_id=1, source_target_pairs={{0,9},{1,8},{2,11},{3,10},{4,13},{5,12},{6,15},{7,14},{8,1},{9,0},... | collective-permute-start | bytes 55304 | tf_op jit(solution)/shard_map/ppermute | solution.py:304
  4.3 3.6 %load.1 = (bf16[4096,768]{1,0:T(8,128)(2,1)S(1)}, bf16[768,4096]{1,0:T(8,128)(2,1)S(1)}, f32[8,512]{1,0:T(8,128)S(1)}, bf16[12,768]{1,0:T(8,128)(2,1)S(1)}, bf16...) custom-call(bf16[4096,768]{1,0:T(8,128)(2,1)} %gallery_hbm.1, ...), custom_call_target="tpu_custom_call" | custom-call | tf_op jit(solution)/shard_map/load/pallas_call | solution.py:143
  7.9 0.0 collective-permute-done.refs_1_
  7.9 2.6 %collective-permute-start.3 = (bf16[24,768]{1,0:T(8,128)(2,1)S(1)}, bf16[24,768]{1,0:T(8,128)(2,1)S(1)}, u32[]{:S(2)}, u32[]{:S(2)}) collective-permute-start(bf16[24,768]{1,0:T(8,128)(2,1)S(1)} %join.2.refs_0_), channel_id=1, source_target_pairs={{0,6},{1,7},{2,4},{3,5},{4,2},{5,3},{6,0},{7,1},{8,14},{9,15},{10,... | collective-permute-start | bytes 110600 | tf_op jit(solution)/shard_map/ppermute | solution.py:304
  10.5 0.5 %collective-permute-start.2 = (bf16[24,768]{1,0:T(8,128)(2,1)S(1)}, bf16[24,768]{1,0:T(8,128)(2,1)S(1)}, u32[]{:S(2)}, u32[]{:S(2)}) collective-permute-start(bf16[24,768]{1,0:T(8,128)(2,1)S(1)} %join.2.refs_0_), channel_id=1, source_target_pairs={{0,3},{1,2},{2,1},{3,0},{4,7},{5,6},{6,5},{7,4},{8,11},{9,10},{10,... | collective-permute-start | bytes 110600 | tf_op jit(solution)/shard_map/ppermute | solution.py:304
  11.0 0.1 collective-permute-start.1
  11.2 1.7 %collective-permute-done.3.refs_3_ = bf16[24,768]{1,0:T(8,128)(2,1)S(1)} collective-permute-done((bf16[24,768]{1,0:T(8,128)(2,1)S(1)}, bf16[24,768]{1,0:T(8,128)(2,1)S(1)}, u32[]{:S(2)}, u32[]{:S(2)}) %collective-permute-start.3) | collective-permute-done | bytes 36896 | tf_op jit(solution)/shard_map/ppermute | solution.py:304
  12.9 1.0 %collective-permute-done.2.refs_2_ = bf16[24,768]{1,0:T(8,128)(2,1)S(1)} collective-permute-done((bf16[24,768]{1,0:T(8,128)(2,1)S(1)}, bf16[24,768]{1,0:T(8,128)(2,1)S(1)}, u32[]{:S(2)}, u32[]{:S(2)}) %collective-permute-start.2) | collective-permute-done | bytes 36896 | tf_op jit(solution)/shard_map/ppermute | solution.py:304
  13.9 0.7 %collective-permute-done.1.refs_1_ = bf16[24,768]{1,0:T(8,128)(2,1)S(1)} collective-permute-done((bf16[24,768]{1,0:T(8,128)(2,1)S(1)}, bf16[24,768]{1,0:T(8,128)(2,1)S(1)}, u32[]{:S(2)}, u32[]{:S(2)}) %collective-permute-start.1) | collective-permute-done | bytes 36896 | tf_op jit(solution)/shard_map/ppermute | solution.py:304
  14.6 0.2 collective-permute-start.4
  14.8 1.3 %collective-permute-done.4.second_ref = bf16[96,768]{1,0:T(8,128)(2,1)S(1)} collective-permute-done((bf16[96,768]{1,0:T(8,128)(2,1)S(1)}, bf16[96,768]{1,0:T(8,128)(2,1)S(1)}, u32[]{:S(2)}, u32[]{:S(2)}) %collective-permute-start.4) | collective-permute-done | bytes 147488 | tf_op jit(solution)/shard_map/ppermute | solution.py:304
  16.0 1.2 %score_bank.1.colsum_ref = f32[8,512]{1,0:T(8,128)S(1)} custom-call(bf16[96,768]{1,0:T(8,128)(2,1)S(1)} %join.3.first_ref, bf16[96,768]{1,0:T(8,128)(2,1)S(1)} %collective-permute-done.4.second_ref, bf16[768,4096]{1,0:T(8,128)(2,1)S(1)} %get-tuple-element.16.turned_ref, f32[8,512]{1,0:T(8,128)S(1)} %get-tuple-element.17.scale_ref), custom_call_target="tpu_custom_call" | custom-call | tf_op jit(solution)/shard_map/score_bank/pallas_call | solution.py:182
  17.2 1.6 %collective-permute-start.5 = (f32[8,512]{1,0:T(8,128)S(1)}, f32[8,512]{1,0:T(8,128)S(1)}, u32[]{:S(2)}, u32[]{:S(2)}) collective-permute-start(f32[8,512]{1,0:T(8,128)S(1)} %score_bank.1.colsum_ref), channel_id=1, source_target_pairs={{0,16},{16,0},{1,17},{17,1},{2,18},{18,2},{3,19},{19,3},{4,20},{20... | collective-permute-start | bytes 49160 | tf_op jit(solution)/shard_map/ppermute | solution.py:304
  18.7 1.3 %score_tests.1 = (f32[32,128]{1,0:T(8,128)S(1)}, f32[8,512]{1,0:T(8,128)S(1)}) custom-call(bf16[96,768]{1,0:T(8,128)(2,1)S(1)} %join.3.first_ref, bf16[96,768]{1,0:T(8,128)(2,1)S(1)} %collective-permute-done.4.second_ref, bf16[2,32,32]{2,1,0:T(8,128)(2,1)S(1)} %get-tuple-element.15.pick_ref, bf16[768,4096]{1,0:T(8,128)(2,1)S(1)} %get-tuple-element.16.turned_ref, ...), custom_call_target="tpu_custom_call" | custom-call | tf_op jit(solution)/shard_map/score_tests/pallas_call | solution.py:211
  20.1 0.9 %collective-permute-done.5.other_ref = f32[8,512]{1,0:T(8,128)S(1)} collective-permute-done((f32[8,512]{1,0:T(8,128)S(1)}, f32[8,512]{1,0:T(8,128)S(1)}, u32[]{:S(2)}, u32[]{:S(2)}) %collective-permute-start.5) | collective-permute-done | bytes 16416 | tf_op jit(solution)/shard_map/ppermute | solution.py:304
  21.0 1.2 %pool.1 = bf16[16,2,896]{2,1,0:T(2,128)(2,1)S(1)} custom-call(f32[32,128]{1,0:T(8,128)S(1)} %get-tuple-element.19.listed_ref, f32[8,512]{1,0:T(8,128)S(1)} %get-tuple-element.20.own_ref, f32[8,512]{1,0:T(8,128)S(1)} %collective-permute-done.5.other_ref, bf16[4096,768]{1,0:T(8,128)(2,1)S(1)} %get-tuple-element.21.gallery_ref, ...), custom_call_target="tpu_custom_call" | custom-call | tf_op jit(solution)/shard_map/pool/pallas_call | solution.py:249
  22.2 10.3 %all_to_all.5.sums_ref = bf16[16,2,896]{2,1,0:T(2,128)(2,1)S(1)} all-to-all(bf16[16,2,896]{2,1,0:T(2,128)(2,1)S(1)} %pool.1), channel_id=1, replica_groups=mesh['bank'=2,'gal'=16] {'gal'}, dimensions={0} | all-to-all | bytes 114688 | tf_op jit(solution)/shard_map/all_to_all | solution.py:340
  32.5 0.9 %finish.1 = f32[4,768]{1,0:T(4,128)} custom-call(bf16[16,2,896]{2,1,0:T(2,128)(2,1)S(1)} %all_to_all.5.sums_ref, f32[4,32]{1,0:T(4,128)S(1)} %get-tuple-element.22.spread_ref), custom_call_target="tpu_custom_call" | custom-call | tf_op jit(solution)/shard_map/finish/pallas_call | solution.py:270
  (2 shorter events, 0.0 us)
Async XLA Ops:
  0.7 7.1 %collective-permute-start = (bf16[12,768]{1,0:T(8,128)(2,1)S(1)}, bf16[12,768]{1,0:T(8,128)(2,1)S(1)}, u32[]{:S(2)}, u32[]{:S(2)}) collective-permute-start(bf16[12,768]{1,0:T(8,128)(2,1)S(1)} %pack.1.packed_ref), channel_id=1, source_target_pairs={{0,9},{1,8},{2,11},{3,10},{4,13},{5,12},{6,15},{7,14},{8,1},{9,0},... | collective-permute-start | bytes 55304 | tf_op jit(solution)/shard_map/ppermute | solution.py:304
  7.9 5.0 %collective-permute-start.3 = (bf16[24,768]{1,0:T(8,128)(2,1)S(1)}, bf16[24,768]{1,0:T(8,128)(2,1)S(1)}, u32[]{:S(2)}, u32[]{:S(2)}) collective-permute-start(bf16[24,768]{1,0:T(8,128)(2,1)S(1)} %join.2.refs_0_), channel_id=1, source_target_pairs={{0,6},{1,7},{2,4},{3,5},{4,2},{5,3},{6,0},{7,1},{8,14},{9,15},{10,... | collective-permute-start | bytes 110600 | tf_op jit(solution)/shard_map/ppermute | solution.py:304
  10.5 3.4 %collective-permute-start.2 = (bf16[24,768]{1,0:T(8,128)(2,1)S(1)}, bf16[24,768]{1,0:T(8,128)(2,1)S(1)}, u32[]{:S(2)}, u32[]{:S(2)}) collective-permute-start(bf16[24,768]{1,0:T(8,128)(2,1)S(1)} %join.2.refs_0_), channel_id=1, source_target_pairs={{0,3},{1,2},{2,1},{3,0},{4,7},{5,6},{6,5},{7,4},{8,11},{9,10},{10,... | collective-permute-start | bytes 110600 | tf_op jit(solution)/shard_map/ppermute | solution.py:304
  11.0 3.5 %collective-permute-start.1 = (bf16[24,768]{1,0:T(8,128)(2,1)S(1)}, bf16[24,768]{1,0:T(8,128)(2,1)S(1)}, u32[]{:S(2)}, u32[]{:S(2)}) collective-permute-start(bf16[24,768]{1,0:T(8,128)(2,1)S(1)} %join.2.refs_0_), channel_id=1, source_target_pairs={{0,5},{1,4},{2,7},{3,6},{4,1},{5,0},{6,3},{7,2},{8,13},{9,12},{10,... | collective-permute-start | bytes 110600 | tf_op jit(solution)/shard_map/ppermute | solution.py:304
  14.6 1.4 %collective-permute-start.4 = (bf16[96,768]{1,0:T(8,128)(2,1)S(1)}, bf16[96,768]{1,0:T(8,128)(2,1)S(1)}, u32[]{:S(2)}, u32[]{:S(2)}) collective-permute-start(bf16[96,768]{1,0:T(8,128)(2,1)S(1)} %join.3.first_ref), channel_id=1, source_target_pairs={{0,1},{1,0},{2,3},{3,2},{4,5},{5,4},{6,7},{7,6},{8,9},{9,8},{10,11... | collective-permute-start | bytes 442376 | tf_op jit(solution)/shard_map/ppermute | solution.py:304
  17.2 3.8 %collective-permute-start.5 = (f32[8,512]{1,0:T(8,128)S(1)}, f32[8,512]{1,0:T(8,128)S(1)}, u32[]{:S(2)}, u32[]{:S(2)}) collective-permute-start(f32[8,512]{1,0:T(8,128)S(1)} %score_bank.1.colsum_ref), channel_id=1, source_target_pairs={{0,16},{16,0},{1,17},{17,1},{2,18},{18,2},{3,19},{19,3},{4,20},{20... | collective-permute-start | bytes 49160 | tf_op jit(solution)/shard_map/ppermute | solution.py:304

commit v5 on v4

v5 whole, which is shorter than its diff:
```python
import functools

import jax
import jax.numpy as jnp
from jax import lax
from jax.experimental import pallas as pl
from jax.experimental.pallas import tpu as pltpu
from jax.sharding import PartitionSpec as P

BLOCK = 128
CHUNKS = 8
EARLY = 5
LANES = 128
CAP = 2
SHARPNESS = 20.0
LOG2E = 1.4426950408889634
epsilon = 1e-06

VMEM = pl.BlockSpec(memory_space=pltpu.VMEM)
HBM = pl.BlockSpec(memory_space=pltpu.HBM)
PARAMS = pltpu.CompilerParams(vmem_limit_bytes=16 << 20)


def in_hbm(value):
    return pltpu.with_memory_space_constraint(value, pltpu.HBM)


def keep(value):
    return pltpu.with_memory_space_constraint(value, pltpu.VMEM)


def bits_of(index, order):
    value = jnp.zeros_like(index)
    for place, mask in enumerate(order):
        value = jnp.where(index == place, mask, value)
    return value


def iota(shape, axis):
    return lax.broadcasted_iota(jnp.int32, shape, axis)


def route(order, test_own, slabs, offsets, pick_ref, block_ref, spread_ref):
    me = lax.axis_index("gal")
    devices = len(order)
    group = devices * test_own
    slots = devices * CAP

    found = jnp.sum(jnp.where(slabs == me, offsets + 1, 0), axis=0, keepdims=True)
    before = (iota((group, group), 0) // test_own == iota((group, group), 1) // test_own) & (
        iota((group, group), 0) < iota((group, group), 1)
    )
    flags = jnp.broadcast_to(jnp.where(found > 0, 1.0, 0.0), (8, group)).astype(jnp.bfloat16)
    rank = jnp.dot(flags, jnp.where(before, 1.0, 0.0).astype(jnp.bfloat16), preferred_element_type=jnp.float32)
    rank = rank[:1].astype(jnp.int32)
    index = iota((slots, group), 0)
    column = iota((slots, group), 1)
    filled = (column // test_own == me ^ bits_of(index // CAP, order)) & (found > 0) & (rank == index % CAP)
    block = jnp.sum(jnp.where(filled, found, 0), axis=1, keepdims=True) - 1
    block_ref[...] = jnp.broadcast_to(block, block_ref.shape)
    from_row = jnp.sum(jnp.where(filled, column % test_own + 1, 0), axis=1, keepdims=True)
    index = iota((slots, 1), 0) // CAP
    slot_from = jnp.where(from_row > 0, index * test_own - 1 + from_row, -1)
    half = pick_ref.shape[2]
    for h in range(2):
        column = iota((slots, half), 1) + h * half
        pick_ref[h] = jnp.where(column == slot_from, 1.0, 0.0).astype(jnp.bfloat16)

    lane = iota((1, slots), 1)
    filled_before = jnp.zeros((1, slots), jnp.int32)
    mine = iota(slabs.shape, 1)
    for r in range(test_own):
        listed = jnp.sum(jnp.where(mine == me * test_own + r, slabs, 0), axis=1, keepdims=True)
        here = jnp.sum(jnp.where(listed == lane // CAP, 1, 0), axis=0, keepdims=True)
        spread_ref[r : r + 1, :] = jnp.where((here > 0) & (filled_before == lane % CAP), 1.0, 0.0)
        filled_before = filled_before + here


def turn(gallery_hbm, first_row, gallery_ref, turned_ref, scale_ref, sems):
    parts, part = scale_ref.shape
    copies = [
        pltpu.make_async_copy(
            gallery_hbm.at[pl.ds(first_row + c * part, part)], gallery_ref.at[pl.ds(c * part, part)], sems.at[c]
        )
        for c in range(parts)
    ]
    for copy in copies:
        copy.start()

    def step(c):
        copies[c].wait()
        turned = gallery_ref[pl.ds(c * part, part), :].T
        turned_ref[:, c * part : (c + 1) * part] = turned
        values = turned.astype(jnp.float32)
        scale_ref[c : c + 1, :] = lax.rsqrt(jnp.sum(values * values, axis=0, keepdims=True) + epsilon)

    return [functools.partial(step, c) for c in range(parts)]


def low_kernel(
    gallery_hbm, bank_hbm, test_hbm, slabs_hbm, offsets_hbm,
    gallery_ref, turned_ref, scale_ref, bank_ref, test_ref, slabs_ref, offsets_ref, sems, small_sems,
):
    pairs = ((bank_hbm, bank_ref), (test_hbm, test_ref), (slabs_hbm, slabs_ref), (offsets_hbm, offsets_ref))
    small = [pltpu.make_async_copy(*pair, small_sems.at[i]) for i, pair in enumerate(pairs)]
    for copy in small:
        copy.start()
    steps = turn(gallery_hbm, 0, gallery_ref, turned_ref, scale_ref, sems)
    for step in steps:
        step()
    for copy in small:
        copy.wait()


def high_kernel(gallery_hbm, packed_ref, gallery_ref, turned_ref, scale_ref, packed_out, sems):
    steps = turn(gallery_hbm, gallery_hbm.shape[0] - gallery_ref.shape[0], gallery_ref, turned_ref, scale_ref, sems)
    packed_out[...] = packed_ref[...]
    for step in steps:
        step()


def part_shapes(gallery, parts):
    rows, depth = gallery.shape
    part = rows // CHUNKS
    return (
        pltpu.VMEM((parts * part, depth), gallery.dtype),
        pltpu.VMEM((depth, parts * part), gallery.dtype),
        pltpu.VMEM((parts, part), jnp.float32),
    )


def load_low(gallery, *small):
    return pl.pallas_call(
        low_kernel,
        out_shape=(*part_shapes(gallery, EARLY), *(pltpu.VMEM(x.shape, x.dtype) for x in small)),
        in_specs=[HBM] * 5,
        out_specs=(VMEM,) * 7,
        scratch_shapes=[pltpu.SemaphoreType.DMA((EARLY,)), pltpu.SemaphoreType.DMA((4,))],
        compiler_params=PARAMS,
        name="load_low",
    )(*map(in_hbm, (gallery, *small)))


def load_high(gallery, packed):
    return pl.pallas_call(
        high_kernel,
        out_shape=(*part_shapes(gallery, CHUNKS - EARLY), pltpu.VMEM(packed.shape, packed.dtype)),
        in_specs=[HBM, VMEM],
        out_specs=(VMEM,) * 4,
        scratch_shapes=[pltpu.SemaphoreType.DMA((CHUNKS - EARLY,))],
        compiler_params=PARAMS,
        name="load_high",
    )(in_hbm(gallery), packed)


def scales(wide):
    return lax.rsqrt(jnp.sum(wide * wide, axis=1, keepdims=True) + epsilon) * (SHARPNESS * LOG2E)


def chunk(c, turned_refs, scale_refs):
    part = scale_refs[0].shape[1]
    late, c = (0, c) if c < EARLY else (1, c - EARLY)
    return turned_refs[late][:, c * part : (c + 1) * part], scale_refs[late][c : c + 1, :]


def bank_kernel(bank_rows, first_ref, second_ref, low_ref, high_ref, low_scale_ref, high_scale_ref, colsum_ref):
    queries = jnp.concatenate([first_ref[:bank_rows], second_ref[:bank_rows]], axis=0)
    query_scale = scales(queries.astype(jnp.float32))
    for c in range(CHUNKS):
        turned, scale = chunk(c, (low_ref, high_ref), (low_scale_ref, high_scale_ref))
        scores = jnp.dot(queries, turned, preferred_element_type=jnp.float32)
        exps = jnp.exp2(scores * scale * query_scale)
        colsum_ref[c : c + 1, :] = jnp.sum(exps, axis=0, keepdims=True)


def score_bank(bank_rows, first, second, turned, scale):
    return pl.pallas_call(
        functools.partial(bank_kernel, bank_rows),
        out_shape=pltpu.VMEM((CHUNKS, scale[0].shape[1]), jnp.float32),
        in_specs=[VMEM] * 6,
        out_specs=VMEM,
        compiler_params=PARAMS,
        name="score_bank",
    )(keep(first), second, *map(keep, turned), *map(keep, scale))


def test_kernel(
    order, bank_rows, first_ref, second_ref, low_ref, high_ref, low_scale_ref, high_scale_ref,
    slabs_ref, offsets_ref, colsum_ref, listed_ref, block_ref, spread_ref, colsum_out, pick_ref,
):
    colsum_out[...] = colsum_ref[...]
    route(order, spread_ref.shape[0], slabs_ref[...], offsets_ref[...], pick_ref, block_ref, spread_ref)
    wide = jnp.dot(pick_ref[0], first_ref[bank_rows:], preferred_element_type=jnp.float32)
    wide = wide + jnp.dot(pick_ref[1], second_ref[bank_rows:], preferred_element_type=jnp.float32)
    queries = wide.astype(jnp.bfloat16)
    part = low_scale_ref.shape[1]
    block = block_ref[...]
    picked = jnp.zeros(listed_ref.shape, jnp.float32)
    for c in range(CHUNKS):
        turned, scale = chunk(c, (low_ref, high_ref), (low_scale_ref, high_scale_ref))
        scores = jnp.dot(queries, turned, preferred_element_type=jnp.float32) * scale
        for b in range(part // BLOCK):
            picked = jnp.where(block == c * (part // BLOCK) + b, scores[:, b * BLOCK : (b + 1) * BLOCK], picked)
    listed_ref[...] = jnp.exp2(picked * scales(wide))


def score_tests(order, bank_rows, first, second, turned, scale, slabs, offsets, colsum):
    slots = len(order) * CAP
    group = slabs.shape[1]
    return pl.pallas_call(
        functools.partial(test_kernel, order, bank_rows),
        out_shape=(
            pltpu.VMEM((slots, BLOCK), jnp.float32),
            pltpu.VMEM((slots, LANES), jnp.int32),
            pltpu.VMEM((group // len(order), slots), jnp.float32),
            pltpu.VMEM(colsum.shape, jnp.float32),
        ),
        in_specs=[VMEM] * 9,
        out_specs=(VMEM,) * 4,
        scratch_shapes=[pltpu.VMEM((2, slots, group // 2), jnp.bfloat16)],
        compiler_params=PARAMS,
        name="score_tests",
    )(*map(keep, (first, second, *turned, *scale, slabs, offsets, colsum)))


def pool_kernel(order, listed_ref, own_ref, other_ref, low_ref, high_ref, block_ref, out_ref, weight_ref):
    block = block_ref[...]
    slots = block.shape[0]
    early, depth = low_ref.shape
    rows = early + high_ref.shape[0]
    each = rows // BLOCK // CHUNKS
    inverse = 1.0 / (own_ref[...] + other_ref[...])
    picked = jnp.zeros((slots, BLOCK), jnp.float32)
    for b in range(rows // BLOCK):
        c, at = b // each, (b % each) * BLOCK
        picked = jnp.where(block == b, inverse[c : c + 1, at : at + BLOCK], picked)
    weight = listed_ref[...] * picked
    total = jnp.sum(weight, axis=1, keepdims=True)
    for b in range(rows // BLOCK):
        weight_ref[:, b * BLOCK : (b + 1) * BLOCK] = jnp.where(block == b, weight, 0.0).astype(jnp.bfloat16)
    numerator = jnp.dot(weight_ref[:, :early], low_ref[...], preferred_element_type=jnp.float32)
    numerator = numerator + jnp.dot(weight_ref[:, early:], high_ref[...], preferred_element_type=jnp.float32)
    high = total.astype(jnp.bfloat16).astype(jnp.float32)
    lane = iota((slots, LANES), 1)
    tail = jnp.where(lane == 0, high, jnp.where(lane == 1, total - high, 0.0))
    me = lax.axis_index("gal")
    for i, bits in enumerate(order):
        at = slice(i * CAP, (i + 1) * CAP)
        out_ref[me ^ bits, :, :depth] = numerator[at].astype(jnp.bfloat16)
        out_ref[me ^ bits, :, depth:] = tail[at].astype(jnp.bfloat16)


def pool(order, listed, own, other, gallery, block):
    depth = gallery[0].shape[1]
    rows = gallery[0].shape[0] + gallery[1].shape[0]
    slots = listed.shape[0]
    return pl.pallas_call(
        functools.partial(pool_kernel, order),
        out_shape=pltpu.VMEM((len(order), CAP, depth + LANES), jnp.bfloat16),
        in_specs=[VMEM] * 6,
        out_specs=VMEM,
        scratch_shapes=[pltpu.VMEM((slots, rows), jnp.bfloat16)],
        compiler_params=PARAMS,
        name="pool",
    )(keep(listed), keep(own), other, *map(keep, gallery), keep(block))


def finish_kernel(sums_ref, spread_ref, out_ref):
    depth = out_ref.shape[1]
    sums = jnp.concatenate([sums_ref[s].astype(jnp.float32) for s in range(sums_ref.shape[0])], axis=0)
    sums = jnp.dot(
        spread_ref[...].astype(jnp.bfloat16), sums.astype(jnp.bfloat16), preferred_element_type=jnp.float32
    )
    out_ref[...] = sums[:, :depth] / (sums[:, depth : depth + 1] + sums[:, depth + 1 : depth + 2])


def finish(sums, spread):
    return pl.pallas_call(
        finish_kernel,
        out_shape=jax.ShapeDtypeStruct((spread.shape[0], sums.shape[2] - LANES), jnp.float32),
        in_specs=[VMEM, VMEM],
        out_specs=VMEM,
        compiler_params=PARAMS,
        name="finish",
    )(sums, keep(spread))


def join_kernel(bank_own, own, *refs):
    *pieces, out_ref = refs
    bank, test = 0, sum(piece.shape[0] for piece in pieces) // own * bank_own
    for piece in pieces:
        rows = piece.shape[0]
        split = rows // own * bank_own
        out_ref[bank : bank + split, :] = piece[:split]
        out_ref[test : test + rows - split, :] = piece[split:]
        bank, test = bank + split, test + rows - split


def join(bank_own, test_own, pieces):
    rows = sum(piece.shape[0] for piece in pieces)
    return pl.pallas_call(
        functools.partial(join_kernel, bank_own, bank_own + test_own),
        out_shape=pltpu.VMEM((rows, pieces[0].shape[1]), pieces[0].dtype),
        in_specs=[VMEM] * len(pieces),
        out_specs=VMEM,
        compiler_params=PARAMS,
        name="join",
    )(*pieces)


def join_first(pieces):
    def kernel(*refs):
        *ins, out_ref = refs
        row = 0
        for piece in ins:
            out_ref[row : row + piece.shape[0], :] = piece[...]
            row += piece.shape[0]

    rows = sum(piece.shape[0] for piece in pieces)
    return pl.pallas_call(
        kernel,
        out_shape=pltpu.VMEM((rows, pieces[0].shape[1]), pieces[0].dtype),
        in_specs=[VMEM] * len(pieces),
        out_specs=VMEM,
        compiler_params=PARAMS,
        name="join",
    )(*pieces)


def swap(value, axis, size, bit):
    return lax.ppermute(value, axis, [(i, i ^ bit) for i in range(size)])


def body(devices, banks, bank_queries, gallery, test_queries, test_slabs, test_offsets):
    bank_own, test_own = bank_queries.shape[0], test_queries.shape[0]

    rounds = [[1 << k | 1] for k in range(devices.bit_length() - 2, 2, -1)] + [[3, 7, 4], [1]]
    order = [0]
    for masks in rounds:
        order = order + [o ^ mask for mask in masks for o in order]

    others = [swap(rows, "gal", devices, rounds[0][0]) for rows in (bank_queries, test_queries)]
    low, low_turned, low_scale, bank, test, slabs, offsets = load_low(
        gallery, bank_queries, test_queries, test_slabs.T, test_offsets.T
    )
    packed = join_first([bank, others[0], test, others[1]])
    for i, near in enumerate(rounds[1:]):
        if i:
            packed = join(bank_own, test_own, [packed, *others])
        others = [swap(packed, "gal", devices, mask) for mask in near]
        if i == 0:
            high, high_turned, high_scale, packed = load_high(gallery, packed)
    other = others[0]
    gallery, turned, scale = (low, high), (low_turned, high_turned), (low_scale, high_scale)

    bank_rows = devices // 2 * bank_own
    first, second = packed, other
    colsum = score_bank(bank_rows, first, second, turned, scale)
    bit = banks // 2
    other = jnp.zeros_like(colsum)
    while bit:
        other = swap(colsum, "bank", banks, bit)
        bit //= 2
        if bit:
            colsum = colsum + other
    listed, block, spread, colsum = score_tests(
        order, bank_rows, first, second, turned, scale, slabs, offsets, colsum
    )
    sums = pool(order, listed, colsum, other, gallery, block)
    sums = lax.all_to_all(sums, "gal", 0, 0, tiled=True)
    return finish(sums, spread)


def solution(mesh):
    in_specs = (
        P(("bank", "gal"), None),
        P("gal", None),
        P(("bank", "gal"), None),
        P("bank", None),
        P("bank", None),
    )
    out_specs = P(("bank", "gal"), None)
    local = functools.partial(body, mesh.shape["gal"], mesh.shape["bank"])
    return jax.shard_map(local, mesh=mesh, in_specs=in_specs, out_specs=out_specs, check_vma=False)
```

time: 33.6 us -> 33.2 us (0.988)
  Pallas kernels: 8.87 us -> 9.27 us
  blocking collectives: 10.3 us -> 9.91 us
    pallas_call x3 -> x4, Pallas kernels: 5.63 us -> 6.17 us  [the longest x1 2.62 us: load_low(): pl.pallas_call(low_kernel, out_shape=(*part_shapes(gallery, EARLY), *(plt...]
    all_to_all x1, blocking collectives: 10.3 us -> 9.91 us  [body(): sums = lax.all_to_all(sums, 'gal', 0, 0, tiled=True)]
    ppermute x6 -> x7, waiting for transfers between devices: 5.56 us -> 5.25 us  [swap(): return lax.ppermute(value, axis, [(i, i ^ bit) for i in range(size)])]
    ppermute x6 -> x7, starting transfers between devices: 8.55 us -> 8.53 us  [swap(): return lax.ppermute(value, axis, [(i, i ^ bit) for i in range(size)])]
  transfers between devices with their start and end apart: 6 -> 7, of which waited for: 5 -> 5; matrix products, arithmetic and copies ran while one was open for 0% -> 0% of each run, Pallas kernels for 15% -> 19%
where the time goes in v5:
time: 33.2 us; the launch traced here: 33 us
  blocking collectives  9.91 us (30%)
  Pallas kernels  9.27 us (28%)
  starting transfers between devices  8.53 us (26%)
  waiting for transfers between devices  5.25 us (16%)
    all_to_all x1, blocking collectives, body(): sums = lax.all_to_all(sums, 'gal', 0, 0, tiled=True)  9.91 us
    ppermute x7, starting transfers between devices, swap(): return lax.ppermute(value, axis, [(i, i ^ bit) for i in range(size)])  8.53 us
    ppermute x7, waiting for transfers between devices, swap(): return lax.ppermute(value, axis, [(i, i ^ bit) for i in range(size)])  5.25 us
    pallas_call x1, Pallas kernels, load_low(): pl.pallas_call(low_kernel, out_shape=(*part_shapes(gallery, EARLY), *(plt...  2.62 us
    pallas_call x1, Pallas kernels, load_high(): pl.pallas_call(high_kernel, out_shape=(*part_shapes(gallery, CHUNKS - EAR...  2 us
    pallas_call x1, Pallas kernels, score_tests(): pl.pallas_call(functools.partial(test_kernel, order, bank_rows), out_shap...  1.54 us
    pallas_call x1, Pallas kernels, pool(): pl.pallas_call(functools.partial(pool_kernel, order), out_shape=pltpu.VME...  1.2 us
    pallas_call x1, Pallas kernels, score_bank(): pl.pallas_call(functools.partial(bank_kernel, bank_rows), out_shape=pltpu...  1.01 us
  transfers between devices with their start and end apart: 7, of which 5 were waited for; matrix products, arithmetic and copies ran while one was open for 0% of the time, Pallas kernels for 19%

profile of v5, /device:TPU:0, one launch (start us, length us, event | category | flops | bytes accessed | tf_op | source)
XLA Modules:
  0.0 33.0 jit_solution(4045402471039196219)
XLA Ops:
  0.0 3.5 %collective-permute-start = (bf16[8,768]{1,0:T(8,128)(2,1)}, bf16[8,768]{1,0:T(8,128)(2,1)S(1)}, u32[]{:S(2)}, u32[]{:S(2)}) collective-permute-start(bf16[8,768]{1,0:T(8,128)(2,1)} %bank_hbm.1), channel_id=1, source_target_pairs={{0,9},{1,8},{2,11},{3,10},{4,13},{5,12},{6,15},{7,14},{8,1},{9,0},... | collective-permute-start | bytes 36872 | tf_op jit(solution)/shard_map/ppermute | solution.py:331
  3.5 0.0 collective-permute-start.1
  3.5 2.6 %load_low.1 = (bf16[2560,768]{1,0:T(8,128)(2,1)S(1)}, bf16[768,2560]{1,0:T(8,128)(2,1)S(1)}, f32[5,512]{1,0:T(8,128)S(1)}, bf16[8,768]{1,0:T(8,128)(2,1)S(1)}, b...) custom-call(bf16[4096,768]{1,0:T(8,128)(2,1)} %gallery_hbm.3, bf16[8,768]{1,0:T(8,128)(2,1)} %bank_hbm.1, ...), custom_call_target="tpu_custom_call" | custom-call | tf_op jit(solution)/shard_map/load_low/pallas_call | solution.py:133
  6.1 1.5 %collective-permute-done.1.refs_3_ = bf16[4,768]{1,0:T(4,128)(2,1)S(1)} collective-permute-done((bf16[4,768]{1,0:T(4,128)(2,1)}, bf16[4,768]{1,0:T(4,128)(2,1)S(1)}, u32[]{:S(2)}, u32[]{:S(2)}) %collective-permute-start.1) | collective-permute-done | bytes 6176 | tf_op jit(solution)/shard_map/ppermute | solution.py:331
  7.6 0.0 collective-permute-done.refs_1_
  7.7 1.6 %collective-permute-start.4 = (bf16[24,768]{1,0:T(8,128)(2,1)S(1)}, bf16[24,768]{1,0:T(8,128)(2,1)S(1)}, u32[]{:S(2)}, u32[]{:S(2)}) collective-permute-start(bf16[24,768]{1,0:T(8,128)(2,1)S(1)} %join.2.packed_ref), channel_id=1, source_target_pairs={{0,4},{1,5},{2,6},{3,7},{4,0},{5,1},{6,2},{7,3},{8,12},{9,13},{10,... | collective-permute-start | bytes 110600 | tf_op jit(solution)/shard_map/ppermute | solution.py:331
  9.3 1.4 %collective-permute-start.3 = (bf16[24,768]{1,0:T(8,128)(2,1)S(1)}, bf16[24,768]{1,0:T(8,128)(2,1)S(1)}, u32[]{:S(2)}, u32[]{:S(2)}) collective-permute-start(bf16[24,768]{1,0:T(8,128)(2,1)S(1)} %join.2.packed_ref), channel_id=1, source_target_pairs={{0,7},{1,6},{2,5},{3,4},{4,3},{5,2},{6,1},{7,0},{8,15},{9,14},{10,... | collective-permute-start | bytes 110600 | tf_op jit(solution)/shard_map/ppermute | solution.py:331
  10.7 0.2 collective-permute-start.2
  10.9 2.0 %load_high.1 = (bf16[1536,768]{1,0:T(8,128)(2,1)S(1)}, bf16[768,1536]{1,0:T(8,128)(2,1)S(1)}, f32[3,512]{1,0:T(4,128)S(1)}, bf16[24,768]{1,0:T(8,128)(2,1)S(1)}) custom-call(bf16[4096,768]{1,0:T(8,128)(2,1)} %gallery_hbm.3, bf16[24,768]{1,0:T(8,128)(2,1)S(1)} %join.2.packed_ref), custom_call_target="tpu_custom_call" | custom-call | tf_op jit(solution)/shard_map/load_high/pallas_call | solution.py:145
  12.9 0.0 collective-permute-done.4.refs_3_
  12.9 0.6 %collective-permute-done.3.refs_2_ = bf16[24,768]{1,0:T(8,128)(2,1)S(1)} collective-permute-done((bf16[24,768]{1,0:T(8,128)(2,1)S(1)}, bf16[24,768]{1,0:T(8,128)(2,1)S(1)}, u32[]{:S(2)}, u32[]{:S(2)}) %collective-permute-start.3) | collective-permute-done | bytes 36896 | tf_op jit(solution)/shard_map/ppermute | solution.py:331
  13.6 1.2 %collective-permute-done.2.refs_1_ = bf16[24,768]{1,0:T(8,128)(2,1)S(1)} collective-permute-done((bf16[24,768]{1,0:T(8,128)(2,1)S(1)}, bf16[24,768]{1,0:T(8,128)(2,1)S(1)}, u32[]{:S(2)}, u32[]{:S(2)}) %collective-permute-start.2) | collective-permute-done | bytes 36896 | tf_op jit(solution)/shard_map/ppermute | solution.py:331
  14.8 0.2 collective-permute-start.5
  14.9 1.3 %collective-permute-done.5.second_ref = bf16[96,768]{1,0:T(8,128)(2,1)S(1)} collective-permute-done((bf16[96,768]{1,0:T(8,128)(2,1)S(1)}, bf16[96,768]{1,0:T(8,128)(2,1)S(1)}, u32[]{:S(2)}, u32[]{:S(2)}) %collective-permute-start.5) | collective-permute-done | bytes 147488 | tf_op jit(solution)/shard_map/ppermute | solution.py:331
  16.2 1.0 %score_bank.1.colsum_ref = f32[8,512]{1,0:T(8,128)S(1)} custom-call(bf16[96,768]{1,0:T(8,128)(2,1)S(1)} %join.3.first_ref, bf16[96,768]{1,0:T(8,128)(2,1)S(1)} %collective-permute-done.5.second_ref, bf16[768,2560]{1,0:T(8,128)(2,1)S(1)} %get-tuple-element.23.low_ref, bf16[768,1536]{1,0:T(8,128)(2,1)S(1)} %get-tuple-element.24.high_ref, ...), custom_call_target="tpu_custom_call" | custom-call | tf_op jit(solution)/shard_map/score_bank/pallas_call | solution.py:177
  17.2 1.6 %collective-permute-start.6 = (f32[8,512]{1,0:T(8,128)S(1)}, f32[8,512]{1,0:T(8,128)S(1)}, u32[]{:S(2)}, u32[]{:S(2)}) collective-permute-start(f32[8,512]{1,0:T(8,128)S(1)} %score_bank.1.colsum_ref), channel_id=1, source_target_pairs={{0,16},{16,0},{1,17},{17,1},{2,18},{18,2},{3,19},{19,3},{4,20},{20... | collective-permute-start | bytes 49160 | tf_op jit(solution)/shard_map/ppermute | solution.py:331
  18.8 1.5 %score_tests.1 = (f32[32,128]{1,0:T(8,128)S(1)}, s32[32,128]{1,0:T(8,128)S(1)}, f32[4,32]{1,0:T(4,128)S(1)}, f32[8,512]{1,0:T(8,128)S(1)}) custom-call(bf16[96,768]{1,0:T(8,128)(2,1)S(1)} %join.3.first_ref, bf16[96,768]{1,0:T(8,128)(2,1)S(1)} %collective-permute-done.5.second_ref, bf16[768,2560]{1,0:T(8,128)(2,1)S(1)} %get-tuple-element.23.low_ref, ...), custom_call_target="tpu_custom_call" | custom-call | tf_op jit(solution)/shard_map/score_tests/pallas_call | solution.py:210
  20.3 0.7 %collective-permute-done.6.other_ref = f32[8,512]{1,0:T(8,128)S(1)} collective-permute-done((f32[8,512]{1,0:T(8,128)S(1)}, f32[8,512]{1,0:T(8,128)S(1)}, u32[]{:S(2)}, u32[]{:S(2)}) %collective-permute-start.6) | collective-permute-done | bytes 16416 | tf_op jit(solution)/shard_map/ppermute | solution.py:331
  21.0 1.2 %pool.1 = bf16[16,2,896]{2,1,0:T(2,128)(2,1)S(1)} custom-call(f32[32,128]{1,0:T(8,128)S(1)} %get-tuple-element.29.listed_ref, f32[8,512]{1,0:T(8,128)S(1)} %get-tuple-element.30.own_ref, f32[8,512]{1,0:T(8,128)S(1)} %collective-permute-done.6.other_ref, bf16[2560,768]{1,0:T(8,128)(2,1)S(1)} %get-tuple-element.31.low_ref, ...), custom_call_target="tpu_custom_call" | custom-call | tf_op jit(solution)/shard_map/pool/pallas_call | solution.py:257
  22.2 9.9 %all_to_all.5.sums_ref = bf16[16,2,896]{2,1,0:T(2,128)(2,1)S(1)} all-to-all(bf16[16,2,896]{2,1,0:T(2,128)(2,1)S(1)} %pool.1), channel_id=1, replica_groups=mesh['bank'=2,'gal'=16] {'gal'}, dimensions={0} | all-to-all | bytes 114688 | tf_op jit(solution)/shard_map/all_to_all | solution.py:370
  32.1 0.9 %finish.1 = f32[4,768]{1,0:T(4,128)} custom-call(bf16[16,2,896]{2,1,0:T(2,128)(2,1)S(1)} %all_to_all.5.sums_ref, f32[4,32]{1,0:T(4,128)S(1)} %get-tuple-element.34.spread_ref), custom_call_target="tpu_custom_call" | custom-call | tf_op jit(solution)/shard_map/finish/pallas_call | solution.py:278
  (2 shorter events, 0.0 us)
Async XLA Ops:
  0.0 7.6 %collective-permute-start = (bf16[8,768]{1,0:T(8,128)(2,1)}, bf16[8,768]{1,0:T(8,128)(2,1)S(1)}, u32[]{:S(2)}, u32[]{:S(2)}) collective-permute-start(bf16[8,768]{1,0:T(8,128)(2,1)} %bank_hbm.1), channel_id=1, source_target_pairs={{0,9},{1,8},{2,11},{3,10},{4,13},{5,12},{6,15},{7,14},{8,1},{9,0},... | collective-permute-start | bytes 36872 | tf_op jit(solution)/shard_map/ppermute | solution.py:331
  3.5 4.2 %collective-permute-start.1 = (bf16[4,768]{1,0:T(4,128)(2,1)}, bf16[4,768]{1,0:T(4,128)(2,1)S(1)}, u32[]{:S(2)}, u32[]{:S(2)}) collective-permute-start(bf16[4,768]{1,0:T(4,128)(2,1)} %test_hbm.1), channel_id=1, source_target_pairs={{0,9},{1,8},{2,11},{3,10},{4,13},{5,12},{6,15},{7,14},{8,1},{9,0},... | collective-permute-start | bytes 18440 | tf_op jit(solution)/shard_map/ppermute | solution.py:331
  7.7 5.3 %collective-permute-start.4 = (bf16[24,768]{1,0:T(8,128)(2,1)S(1)}, bf16[24,768]{1,0:T(8,128)(2,1)S(1)}, u32[]{:S(2)}, u32[]{:S(2)}) collective-permute-start(bf16[24,768]{1,0:T(8,128)(2,1)S(1)} %join.2.packed_ref), channel_id=1, source_target_pairs={{0,4},{1,5},{2,6},{3,7},{4,0},{5,1},{6,2},{7,3},{8,12},{9,13},{10,... | collective-permute-start | bytes 110600 | tf_op jit(solution)/shard_map/ppermute | solution.py:331
  9.3 4.3 %collective-permute-start.3 = (bf16[24,768]{1,0:T(8,128)(2,1)S(1)}, bf16[24,768]{1,0:T(8,128)(2,1)S(1)}, u32[]{:S(2)}, u32[]{:S(2)}) collective-permute-start(bf16[24,768]{1,0:T(8,128)(2,1)S(1)} %join.2.packed_ref), channel_id=1, source_target_pairs={{0,7},{1,6},{2,5},{3,4},{4,3},{5,2},{6,1},{7,0},{8,15},{9,14},{10,... | collective-permute-start | bytes 110600 | tf_op jit(solution)/shard_map/ppermute | solution.py:331
  10.7 4.0 %collective-permute-start.2 = (bf16[24,768]{1,0:T(8,128)(2,1)S(1)}, bf16[24,768]{1,0:T(8,128)(2,1)S(1)}, u32[]{:S(2)}, u32[]{:S(2)}) collective-permute-start(bf16[24,768]{1,0:T(8,128)(2,1)S(1)} %join.2.packed_ref), channel_id=1, source_target_pairs={{0,3},{1,2},{2,1},{3,0},{4,7},{5,6},{6,5},{7,4},{8,11},{9,10},{10,... | collective-permute-start | bytes 110600 | tf_op jit(solution)/shard_map/ppermute | solution.py:331
  14.8 1.4 %collective-permute-start.5 = (bf16[96,768]{1,0:T(8,128)(2,1)S(1)}, bf16[96,768]{1,0:T(8,128)(2,1)S(1)}, u32[]{:S(2)}, u32[]{:S(2)}) collective-permute-start(bf16[96,768]{1,0:T(8,128)(2,1)S(1)} %join.3.first_ref), channel_id=1, source_target_pairs={{0,1},{1,0},{2,3},{3,2},{4,5},{5,4},{6,7},{7,6},{8,9},{9,8},{10,11... | collective-permute-start | bytes 442376 | tf_op jit(solution)/shard_map/ppermute | solution.py:331
  17.2 3.8 %collective-permute-start.6 = (f32[8,512]{1,0:T(8,128)S(1)}, f32[8,512]{1,0:T(8,128)S(1)}, u32[]{:S(2)}, u32[]{:S(2)}) collective-permute-start(f32[8,512]{1,0:T(8,128)S(1)} %score_bank.1.colsum_ref), channel_id=1, source_target_pairs={{0,16},{16,0},{1,17},{17,1},{2,18},{18,2},{3,19},{19,3},{4,20},{20... | collective-permute-start | bytes 49160 | tf_op jit(solution)/shard_map/ppermute | solution.py:331

commit v6 on v5

--- a/solution.py
+++ b/solution.py
@@ -9,7 +9,7 @@
 
 BLOCK = 128
 CHUNKS = 8
-EARLY = 5
+PARTS = (4, 3, 1)
 LANES = 128
 CAP = 2
 SHARPNESS = 20.0
@@ -76,25 +76,25 @@
         filled_before = filled_before + here
 
 
-def turn(gallery_hbm, first_row, gallery_ref, turned_ref, scale_ref, sems):
-    parts, part = scale_ref.shape
+def fetch(gallery_hbm, first_row, gallery_ref, sems):
+    part = gallery_hbm.shape[0] // CHUNKS
     copies = [
         pltpu.make_async_copy(
             gallery_hbm.at[pl.ds(first_row + c * part, part)], gallery_ref.at[pl.ds(c * part, part)], sems.at[c]
         )
-        for c in range(parts)
+        for c in range(gallery_ref.shape[0] // part)
     ]
     for copy in copies:
         copy.start()
-
-    def step(c):
-        copies[c].wait()
-        turned = gallery_ref[pl.ds(c * part, part), :].T
-        turned_ref[:, c * part : (c + 1) * part] = turned
-        values = turned.astype(jnp.float32)
-        scale_ref[c : c + 1, :] = lax.rsqrt(jnp.sum(values * values, axis=0, keepdims=True) + epsilon)
-
-    return [functools.partial(step, c) for c in range(parts)]
+    return copies
+
+
+def turn(c, at, gallery_ref, turned_ref, scale_ref):
+    part = scale_ref.shape[1]
+    turned = gallery_ref[pl.ds(at * part, part), :].T
+    turned_ref[:, c * part : (c + 1) * part] = turned
+    values = turned.astype(jnp.float32)
+    scale_ref[c : c + 1, :] = lax.rsqrt(jnp.sum(values * values, axis=0, keepdims=True) + epsilon)
 
 
 def low_kernel(
@@ -105,69 +105,99 @@
     small = [pltpu.make_async_copy(*pair, small_sems.at[i]) for i, pair in enumerate(pairs)]
     for copy in small:
         copy.start()
-    steps = turn(gallery_hbm, 0, gallery_ref, turned_ref, scale_ref, sems)
-    for step in steps:
-        step()
+    for c, copy in enumerate(fetch(gallery_hbm, 0, gallery_ref, sems)):
+        copy.wait()
+        turn(c, c, gallery_ref, turned_ref, scale_ref)
     for copy in small:
         copy.wait()
 
 
-def high_kernel(gallery_hbm, packed_ref, gallery_ref, turned_ref, scale_ref, packed_out, sems):
-    steps = turn(gallery_hbm, gallery_hbm.shape[0] - gallery_ref.shape[0], gallery_ref, turned_ref, scale_ref, sems)
+def more_kernel(gallery_hbm, packed_ref, gallery_ref, turned_ref, scale_ref, packed_out, sems):
+    copies = fetch(gallery_hbm, gallery_hbm.shape[0] - gallery_ref.shape[0], gallery_ref, sems)
     packed_out[...] = packed_ref[...]
-    for step in steps:
-        step()
+    for c, copy in enumerate(copies):
+        copy.wait()
+        if c < scale_ref.shape[0]:
+            turn(c, c, gallery_ref, turned_ref, scale_ref)
+
+
+def last_kernel(gallery_ref, packed_ref, turned_ref, scale_ref, packed_out):
+    packed_out[...] = packed_ref[...]
+    for c in range(scale_ref.shape[0]):
+        turn(c, PARTS[1] + c, gallery_ref, turned_ref, scale_ref)
 
 
 def part_shapes(gallery, parts):
     rows, depth = gallery.shape
     part = rows // CHUNKS
     return (
-        pltpu.VMEM((parts * part, depth), gallery.dtype),
         pltpu.VMEM((depth, parts * part), gallery.dtype),
         pltpu.VMEM((parts, part), jnp.float32),
     )
 
 
+def rows_shape(gallery, parts):
+    rows, depth = gallery.shape
+    return pltpu.VMEM((rows // CHUNKS * parts, depth), gallery.dtype)
+
+
 def load_low(gallery, *small):
     return pl.pallas_call(
         low_kernel,
-        out_shape=(*part_shapes(gallery, EARLY), *(pltpu.VMEM(x.shape, x.dtype) for x in small)),
+        out_shape=(rows_shape(gallery, PARTS[0]), *part_shapes(gallery, PARTS[0]), *(pltpu.VMEM(x.shape, x.dtype) for x in small)),
         in_specs=[HBM] * 5,
         out_specs=(VMEM,) * 7,
-        scratch_shapes=[pltpu.SemaphoreType.DMA((EARLY,)), pltpu.SemaphoreType.DMA((4,))],
+        scratch_shapes=[pltpu.SemaphoreType.DMA((PARTS[0],)), pltpu.SemaphoreType.DMA((4,))],
         compiler_params=PARAMS,
         name="load_low",
     )(*map(in_hbm, (gallery, *small)))
 
 
-def load_high(gallery, packed):
-    return pl.pallas_call(
-        high_kernel,
-        out_shape=(*part_shapes(gallery, CHUNKS - EARLY), pltpu.VMEM(packed.shape, packed.dtype)),
+def load_more(gallery, packed):
+    parts = CHUNKS - PARTS[0]
+    return pl.pallas_call(
+        more_kernel,
+        out_shape=(
+            rows_shape(gallery, parts),
+            *part_shapes(gallery, PARTS[1]),
+            pltpu.VMEM(packed.shape, packed.dtype),
+        ),
         in_specs=[HBM, VMEM],
         out_specs=(VMEM,) * 4,
-        scratch_shapes=[pltpu.SemaphoreType.DMA((CHUNKS - EARLY,))],
-        compiler_params=PARAMS,
-        name="load_high",
+        scratch_shapes=[pltpu.SemaphoreType.DMA((parts,))],
+        compiler_params=PARAMS,
+        name="load_more",
     )(in_hbm(gallery), packed)
+
+
+def turn_last(gallery, more, packed):
+    return pl.pallas_call(
+        last_kernel,
+        out_shape=(*part_shapes(gallery, PARTS[2]), pltpu.VMEM(packed.shape, packed.dtype)),
+        in_specs=[VMEM, VMEM],
+        out_specs=(VMEM,) * 3,
+        compiler_params=PARAMS,
+        name="turn_last",
+    )(keep(more), packed)
 
 
 def scales(wide):
     return lax.rsqrt(jnp.sum(wide * wide, axis=1, keepdims=True) + epsilon) * (SHARPNESS * LOG2E)
 
 
-def chunk(c, turned_refs, scale_refs):
-    part = scale_refs[0].shape[1]
-    late, c = (0, c) if c < EARLY else (1, c - EARLY)
-    return turned_refs[late][:, c * part : (c + 1) * part], scale_refs[late][c : c + 1, :]
-
-
-def bank_kernel(bank_rows, first_ref, second_ref, low_ref, high_ref, low_scale_ref, high_scale_ref, colsum_ref):
+def chunks(turned_refs, scale_refs):
+    for turned_ref, scale_ref in zip(turned_refs, scale_refs):
+        parts, part = scale_ref.shape
+        for c in range(parts):
+            yield turned_ref[:, c * part : (c + 1) * part], scale_ref[c : c + 1, :]
+
+
+def bank_kernel(bank_rows, first_ref, second_ref, *refs):
+    number = len(PARTS)
+    turned_refs, scale_refs, colsum_ref = refs[:number], refs[number : 2 * number], refs[-1]
     queries = jnp.concatenate([first_ref[:bank_rows], second_ref[:bank_rows]], axis=0)
     query_scale = scales(queries.astype(jnp.float32))
-    for c in range(CHUNKS):
-        turned, scale = chunk(c, (low_ref, high_ref), (low_scale_ref, high_scale_ref))
+    for c, (turned, scale) in enumerate(chunks(turned_refs, scale_refs)):
         scores = jnp.dot(queries, turned, preferred_element_type=jnp.float32)
         exps = jnp.exp2(scores * scale * query_scale)
         colsum_ref[c : c + 1, :] = jnp.sum(exps, axis=0, keepdims=True)
@@ -177,27 +207,26 @@
     return pl.pallas_call(
         functools.partial(bank_kernel, bank_rows),
         out_shape=pltpu.VMEM((CHUNKS, scale[0].shape[1]), jnp.float32),
-        in_specs=[VMEM] * 6,
+        in_specs=[VMEM] * (2 + 2 * len(PARTS)),
         out_specs=VMEM,
         compiler_params=PARAMS,
         name="score_bank",
     )(keep(first), second, *map(keep, turned), *map(keep, scale))
 
 
-def test_kernel(
-    order, bank_rows, first_ref, second_ref, low_ref, high_ref, low_scale_ref, high_scale_ref,
-    slabs_ref, offsets_ref, colsum_ref, listed_ref, block_ref, spread_ref, colsum_out, pick_ref,
-):
+def test_kernel(order, bank_rows, first_ref, second_ref, *refs):
+    number = len(PARTS)
+    turned_refs, scale_refs, refs = refs[:number], refs[number : 2 * number], refs[2 * number :]
+    slabs_ref, offsets_ref, colsum_ref, listed_ref, block_ref, spread_ref, colsum_out, pick_ref = refs
     colsum_out[...] = colsum_ref[...]
     route(order, spread_ref.shape[0], slabs_ref[...], offsets_ref[...], pick_ref, block_ref, spread_ref)
     wide = jnp.dot(pick_ref[0], first_ref[bank_rows:], preferred_element_type=jnp.float32)
     wide = wide + jnp.dot(pick_ref[1], second_ref[bank_rows:], preferred_element_type=jnp.float32)
     queries = wide.astype(jnp.bfloat16)
-    part = low_scale_ref.shape[1]
+    part = scale_refs[0].shape[1]
     block = block_ref[...]
     picked = jnp.zeros(listed_ref.shape, jnp.float32)
-    for c in range(CHUNKS):
-        turned, scale = chunk(c, (low_ref, high_ref), (low_scale_ref, high_scale_ref))
+    for c, (turned, scale) in enumerate(chunks(turned_refs, scale_refs)):
         scores = jnp.dot(queries, turned, preferred_element_type=jnp.float32) * scale
         for b in range(part // BLOCK):
             picked = jnp.where(block == c * (part // BLOCK) + b, scores[:, b * BLOCK : (b + 1) * BLOCK], picked)
@@ -215,7 +244,7 @@
             pltpu.VMEM((group // len(order), slots), jnp.float32),
             pltpu.VMEM(colsum.shape, jnp.float32),
         ),
-        in_specs=[VMEM] * 9,
+        in_specs=[VMEM] * (5 + 2 * len(PARTS)),
         out_specs=(VMEM,) * 4,
         scratch_shapes=[pltpu.VMEM((2, slots, group // 2), jnp.bfloat16)],
         compiler_params=PARAMS,
@@ -223,11 +252,11 @@
     )(*map(keep, (first, second, *turned, *scale, slabs, offsets, colsum)))
 
 
-def pool_kernel(order, listed_ref, own_ref, other_ref, low_ref, high_ref, block_ref, out_ref, weight_ref):
+def pool_kernel(order, listed_ref, own_ref, other_ref, block_ref, *refs):
+    *gallery_refs, out_ref, weight_ref = refs
     block = block_ref[...]
-    slots = block.shape[0]
-    early, depth = low_ref.shape
-    rows = early + high_ref.shape[0]
+    slots, rows = weight_ref.shape
+    depth = gallery_refs[0].shape[1]
     each = rows // BLOCK // CHUNKS
     inverse = 1.0 / (own_ref[...] + other_ref[...])
     picked = jnp.zeros((slots, BLOCK), jnp.float32)
@@ -238,8 +267,11 @@
     total = jnp.sum(weight, axis=1, keepdims=True)
     for b in range(rows // BLOCK):
         weight_ref[:, b * BLOCK : (b + 1) * BLOCK] = jnp.where(block == b, weight, 0.0).astype(jnp.bfloat16)
-    numerator = jnp.dot(weight_ref[:, :early], low_ref[...], preferred_element_type=jnp.float32)
-    numerator = numerator + jnp.dot(weight_ref[:, early:], high_ref[...], preferred_element_type=jnp.float32)
+    numerator, row = jnp.zeros((slots, depth), jnp.float32), 0
+    for gallery_ref in gallery_refs:
+        here = slice(row, row + gallery_ref.shape[0])
+        numerator = numerator + jnp.dot(weight_ref[:, here], gallery_ref[...], preferred_element_type=jnp.float32)
+        row = here.stop
     high = total.astype(jnp.bfloat16).astype(jnp.float32)
     lane = iota((slots, LANES), 1)
     tail = jnp.where(lane == 0, high, jnp.where(lane == 1, total - high, 0.0))
@@ -252,17 +284,17 @@
 
 def pool(order, listed, own, other, gallery, block):
     depth = gallery[0].shape[1]
-    rows = gallery[0].shape[0] + gallery[1].shape[0]
+    rows = sum(part.shape[0] for part in gallery)
     slots = listed.shape[0]
     return pl.pallas_call(
         functools.partial(pool_kernel, order),
         out_shape=pltpu.VMEM((len(order), CAP, depth + LANES), jnp.bfloat16),
-        in_specs=[VMEM] * 6,
+        in_specs=[VMEM] * (4 + len(gallery)),
         out_specs=VMEM,
         scratch_shapes=[pltpu.VMEM((slots, rows), jnp.bfloat16)],
         compiler_params=PARAMS,
         name="pool",
-    )(keep(listed), keep(own), other, *map(keep, gallery), keep(block))
+    )(keep(listed), keep(own), other, keep(block), *map(keep, gallery))
 
 
 def finish_kernel(sums_ref, spread_ref, out_ref):
@@ -349,9 +381,12 @@
             packed = join(bank_own, test_own, [packed, *others])
         others = [swap(packed, "gal", devices, mask) for mask in near]
         if i == 0:
-            high, high_turned, high_scale, packed = load_high(gallery, packed)
+            more, more_turned, more_scale, packed = load_more(gallery, packed)
+        if i == len(rounds) - 2:
+            last_turned, last_scale, packed = turn_last(gallery, more, packed)
     other = others[0]
-    gallery, turned, scale = (low, high), (low_turned, high_turned), (low_scale, high_scale)
+    turned, scale = (low_turned, more_turned, last_turned), (low_scale, more_scale, last_scale)
+    gallery = (low, more)
 
     bank_rows = devices // 2 * bank_own
     first, second = packed, other

time: 33.2 us -> 33 us (level)
    pallas_call x2 -> x3, Pallas kernels: 4.62 us -> 4.63 us  [the longest x1 2.36 us: load_low(): pl.pallas_call(low_kernel, out_shape=(rows_shape(gallery, PARTS[0]), *par...]
where the time goes in v6:
time: 33 us; the launch traced here: 32.8 us
  blocking collectives  9.65 us (29%)
  Pallas kernels  9.33 us (28%)
  starting transfers between devices  8.52 us (26%)
  waiting for transfers between devices  5.23 us (16%)
    all_to_all x1, blocking collectives, body(): sums = lax.all_to_all(sums, 'gal', 0, 0, tiled=True)  9.65 us
    ppermute x7, starting transfers between devices, swap(): return lax.ppermute(value, axis, [(i, i ^ bit) for i in range(size)])  8.52 us
    ppermute x7, waiting for transfers between devices, swap(): return lax.ppermute(value, axis, [(i, i ^ bit) for i in range(size)])  5.23 us
    pallas_call x1, Pallas kernels, load_low(): pl.pallas_call(low_kernel, out_shape=(rows_shape(gallery, PARTS[0]), *par...  2.36 us
    pallas_call x1, Pallas kernels, load_more(): pl.pallas_call(more_kernel, out_shape=(rows_shape(gallery, parts), *part_...  2.01 us
    pallas_call x1, Pallas kernels, score_tests(): pl.pallas_call(functools.partial(test_kernel, order, bank_rows), out_shap...  1.54 us
    pallas_call x1, Pallas kernels, pool(): pl.pallas_call(functools.partial(pool_kernel, order), out_shape=pltpu.VME...  1.19 us
    pallas_call x1, Pallas kernels, score_bank(): pl.pallas_call(functools.partial(bank_kernel, bank_rows), out_shape=pltpu...  1.06 us
  transfers between devices with their start and end apart: 7, of which 5 were waited for; matrix products, arithmetic and copies ran while one was open for 0% of the time, Pallas kernels for 19%

profile of v6, /device:TPU:0, one launch (start us, length us, event | category | flops | bytes accessed | tf_op | source)
XLA Modules:
  0.0 32.8 jit_solution(9379796482158003005)
XLA Ops:
  0.0 3.5 %collective-permute-start = (bf16[8,768]{1,0:T(8,128)(2,1)}, bf16[8,768]{1,0:T(8,128)(2,1)S(1)}, u32[]{:S(2)}, u32[]{:S(2)}) collective-permute-start(bf16[8,768]{1,0:T(8,128)(2,1)} %bank_hbm.1), channel_id=1, source_target_pairs={{0,9},{1,8},{2,11},{3,10},{4,13},{5,12},{6,15},{7,14},{8,1},{9,0},... | collective-permute-start | bytes 36872 | tf_op jit(solution)/shard_map/ppermute | solution.py:363
  3.5 0.0 collective-permute-start.1
  3.5 2.4 %load_low.1 = (bf16[2048,768]{1,0:T(8,128)(2,1)S(1)}, bf16[768,2048]{1,0:T(8,128)(2,1)S(1)}, f32[4,512]{1,0:T(4,128)S(1)}, bf16[8,768]{1,0:T(8,128)(2,1)S(1)}, b...) custom-call(bf16[4096,768]{1,0:T(8,128)(2,1)} %gallery_hbm.3, bf16[8,768]{1,0:T(8,128)(2,1)} %bank_hbm.1, ...), custom_call_target="tpu_custom_call" | custom-call | tf_op jit(solution)/shard_map/load_low/pallas_call | solution.py:145
  5.9 1.8 %collective-permute-done.1.refs_3_ = bf16[4,768]{1,0:T(4,128)(2,1)S(1)} collective-permute-done((bf16[4,768]{1,0:T(4,128)(2,1)}, bf16[4,768]{1,0:T(4,128)(2,1)S(1)}, u32[]{:S(2)}, u32[]{:S(2)}) %collective-permute-start.1) | collective-permute-done | bytes 6176 | tf_op jit(solution)/shard_map/ppermute | solution.py:363
  7.6 0.0 collective-permute-done.refs_1_
  7.7 1.6 %collective-permute-start.4 = (bf16[24,768]{1,0:T(8,128)(2,1)S(1)}, bf16[24,768]{1,0:T(8,128)(2,1)S(1)}, u32[]{:S(2)}, u32[]{:S(2)}) collective-permute-start(bf16[24,768]{1,0:T(8,128)(2,1)S(1)} %join.2.packed_ref), channel_id=1, source_target_pairs={{0,4},{1,5},{2,6},{3,7},{4,0},{5,1},{6,2},{7,3},{8,12},{9,13},{10,... | collective-permute-start | bytes 110600 | tf_op jit(solution)/shard_map/ppermute | solution.py:363
  9.3 1.4 %collective-permute-start.3 = (bf16[24,768]{1,0:T(8,128)(2,1)S(1)}, bf16[24,768]{1,0:T(8,128)(2,1)S(1)}, u32[]{:S(2)}, u32[]{:S(2)}) collective-permute-start(bf16[24,768]{1,0:T(8,128)(2,1)S(1)} %join.2.packed_ref), channel_id=1, source_target_pairs={{0,7},{1,6},{2,5},{3,4},{4,3},{5,2},{6,1},{7,0},{8,15},{9,14},{10,... | collective-permute-start | bytes 110600 | tf_op jit(solution)/shard_map/ppermute | solution.py:363
  10.7 0.2 collective-permute-start.2
  10.9 2.0 %load_more.1 = (bf16[2048,768]{1,0:T(8,128)(2,1)S(1)}, bf16[768,1536]{1,0:T(8,128)(2,1)S(1)}, f32[3,512]{1,0:T(4,128)S(1)}, bf16[24,768]{1,0:T(8,128)(2,1)S(1)}) custom-call(bf16[4096,768]{1,0:T(8,128)(2,1)} %gallery_hbm.3, bf16[24,768]{1,0:T(8,128)(2,1)S(1)} %join.2.packed_ref), custom_call_target="tpu_custom_call" | custom-call | tf_op jit(solution)/shard_map/load_more/pallas_call | solution.py:158
  12.9 0.0 collective-permute-done.4.refs_3_
  13.0 0.6 %collective-permute-done.3.refs_2_ = bf16[24,768]{1,0:T(8,128)(2,1)S(1)} collective-permute-done((bf16[24,768]{1,0:T(8,128)(2,1)S(1)}, bf16[24,768]{1,0:T(8,128)(2,1)S(1)}, u32[]{:S(2)}, u32[]{:S(2)}) %collective-permute-start.3) | collective-permute-done | bytes 36896 | tf_op jit(solution)/shard_map/ppermute | solution.py:363
  13.6 1.2 %collective-permute-done.2.refs_1_ = bf16[24,768]{1,0:T(8,128)(2,1)S(1)} collective-permute-done((bf16[24,768]{1,0:T(8,128)(2,1)S(1)}, bf16[24,768]{1,0:T(8,128)(2,1)S(1)}, u32[]{:S(2)}, u32[]{:S(2)}) %collective-permute-start.2) | collective-permute-done | bytes 36896 | tf_op jit(solution)/shard_map/ppermute | solution.py:363
  14.8 0.2 collective-permute-start.5
  14.9 0.3 turn_last.1
  15.2 1.0 %collective-permute-done.5.second_ref = bf16[96,768]{1,0:T(8,128)(2,1)S(1)} collective-permute-done((bf16[96,768]{1,0:T(8,128)(2,1)S(1)}, bf16[96,768]{1,0:T(8,128)(2,1)S(1)}, u32[]{:S(2)}, u32[]{:S(2)}) %collective-permute-start.5) | collective-permute-done | bytes 147488 | tf_op jit(solution)/shard_map/ppermute | solution.py:363
  16.2 1.1 %score_bank.1.refs_8_ = f32[8,512]{1,0:T(8,128)S(1)} custom-call(bf16[96,768]{1,0:T(8,128)(2,1)S(1)} %get-tuple-element.27.first_ref, bf16[96,768]{1,0:T(8,128)(2,1)S(1)} %collective-permute-done.5.second_ref, bf16[768,2048]{1,0:T(8,128)(2,1)S(1)} %get-tuple-element.28.refs_0_, bf16[768,1536]{1,0:T(8,128)(2,1)S(1)} %get-tuple-element.29.refs_1_, ...), custom_call_target="tpu_custom_call" | custom-call | tf_op jit(solution)/shard_map/score_bank/pallas_call | solution.py:207
  17.3 1.6 %collective-permute-start.6 = (f32[8,512]{1,0:T(8,128)S(1)}, f32[8,512]{1,0:T(8,128)S(1)}, u32[]{:S(2)}, u32[]{:S(2)}) collective-permute-start(f32[8,512]{1,0:T(8,128)S(1)} %score_bank.1.refs_8_), channel_id=1, source_target_pairs={{0,16},{16,0},{1,17},{17,1},{2,18},{18,2},{3,19},{19,3},{4,20},{20... | collective-permute-start | bytes 49160 | tf_op jit(solution)/shard_map/ppermute | solution.py:363
  18.8 1.5 %score_tests.1 = (f32[32,128]{1,0:T(8,128)S(1)}, s32[32,128]{1,0:T(8,128)S(1)}, f32[4,32]{1,0:T(4,128)S(1)}, f32[8,512]{1,0:T(8,128)S(1)}) custom-call(bf16[96,768]{1,0:T(8,128)(2,1)S(1)} %get-tuple-element.27.first_ref, bf16[96,768]{1,0:T(8,128)(2,1)S(1)} %collective-permute-done.5.second_ref, bf16[768,2048]{1,0:T(8,128)(2,1)S(1)} %get-tuple-element.28.refs_0_, ...), custom_call_target="tpu_custom_call" | custom-call | tf_op jit(solution)/shard_map/score_tests/pallas_call | solution.py:239
  20.4 0.7 %collective-permute-done.6.other_ref = f32[8,512]{1,0:T(8,128)S(1)} collective-permute-done((f32[8,512]{1,0:T(8,128)S(1)}, f32[8,512]{1,0:T(8,128)S(1)}, u32[]{:S(2)}, u32[]{:S(2)}) %collective-permute-start.6) | collective-permute-done | bytes 16416 | tf_op jit(solution)/shard_map/ppermute | solution.py:363
  21.1 1.2 %pool.1 = bf16[16,2,896]{2,1,0:T(2,128)(2,1)S(1)} custom-call(f32[32,128]{1,0:T(8,128)S(1)} %get-tuple-element.36.listed_ref, f32[8,512]{1,0:T(8,128)S(1)} %get-tuple-element.37.own_ref, f32[8,512]{1,0:T(8,128)S(1)} %collective-permute-done.6.other_ref, s32[32,128]{1,0:T(8,128)S(1)} %get-tuple-element.38.block_ref, ...), custom_call_target="tpu_custom_call" | custom-call | tf_op jit(solution)/shard_map/pool/pallas_call | solution.py:289
  22.3 9.6 %all_to_all.5.sums_ref = bf16[16,2,896]{2,1,0:T(2,128)(2,1)S(1)} all-to-all(bf16[16,2,896]{2,1,0:T(2,128)(2,1)S(1)} %pool.1), channel_id=1, replica_groups=mesh['bank'=2,'gal'=16] {'gal'}, dimensions={0} | all-to-all | bytes 114688 | tf_op jit(solution)/shard_map/all_to_all | solution.py:405
  31.9 0.9 %finish.1 = f32[4,768]{1,0:T(4,128)} custom-call(bf16[16,2,896]{2,1,0:T(2,128)(2,1)S(1)} %all_to_all.5.sums_ref, f32[4,32]{1,0:T(4,128)S(1)} %get-tuple-element.40.spread_ref), custom_call_target="tpu_custom_call" | custom-call | tf_op jit(solution)/shard_map/finish/pallas_call | solution.py:310
  (2 shorter events, 0.0 us)
Async XLA Ops:
  0.0 7.6 %collective-permute-start = (bf16[8,768]{1,0:T(8,128)(2,1)}, bf16[8,768]{1,0:T(8,128)(2,1)S(1)}, u32[]{:S(2)}, u32[]{:S(2)}) collective-permute-start(bf16[8,768]{1,0:T(8,128)(2,1)} %bank_hbm.1), channel_id=1, source_target_pairs={{0,9},{1,8},{2,11},{3,10},{4,13},{5,12},{6,15},{7,14},{8,1},{9,0},... | collective-permute-start | bytes 36872 | tf_op jit(solution)/shard_map/ppermute | solution.py:363
  3.5 4.2 %collective-permute-start.1 = (bf16[4,768]{1,0:T(4,128)(2,1)}, bf16[4,768]{1,0:T(4,128)(2,1)S(1)}, u32[]{:S(2)}, u32[]{:S(2)}) collective-permute-start(bf16[4,768]{1,0:T(4,128)(2,1)} %test_hbm.1), channel_id=1, source_target_pairs={{0,9},{1,8},{2,11},{3,10},{4,13},{5,12},{6,15},{7,14},{8,1},{9,0},... | collective-permute-start | bytes 18440 | tf_op jit(solution)/shard_map/ppermute | solution.py:363
  7.7 5.3 %collective-permute-start.4 = (bf16[24,768]{1,0:T(8,128)(2,1)S(1)}, bf16[24,768]{1,0:T(8,128)(2,1)S(1)}, u32[]{:S(2)}, u32[]{:S(2)}) collective-permute-start(bf16[24,768]{1,0:T(8,128)(2,1)S(1)} %join.2.packed_ref), channel_id=1, source_target_pairs={{0,4},{1,5},{2,6},{3,7},{4,0},{5,1},{6,2},{7,3},{8,12},{9,13},{10,... | collective-permute-start | bytes 110600 | tf_op jit(solution)/shard_map/ppermute | solution.py:363
  9.3 4.3 %collective-permute-start.3 = (bf16[24,768]{1,0:T(8,128)(2,1)S(1)}, bf16[24,768]{1,0:T(8,128)(2,1)S(1)}, u32[]{:S(2)}, u32[]{:S(2)}) collective-permute-start(bf16[24,768]{1,0:T(8,128)(2,1)S(1)} %join.2.packed_ref), channel_id=1, source_target_pairs={{0,7},{1,6},{2,5},{3,4},{4,3},{5,2},{6,1},{7,0},{8,15},{9,14},{10,... | collective-permute-start | bytes 110600 | tf_op jit(solution)/shard_map/ppermute | solution.py:363
  10.7 4.0 %collective-permute-start.2 = (bf16[24,768]{1,0:T(8,128)(2,1)S(1)}, bf16[24,768]{1,0:T(8,128)(2,1)S(1)}, u32[]{:S(2)}, u32[]{:S(2)}) collective-permute-start(bf16[24,768]{1,0:T(8,128)(2,1)S(1)} %join.2.packed_ref), channel_id=1, source_target_pairs={{0,3},{1,2},{2,1},{3,0},{4,7},{5,6},{6,5},{7,4},{8,11},{9,10},{10,... | collective-permute-start | bytes 110600 | tf_op jit(solution)/shard_map/ppermute | solution.py:363
  14.8 1.4 %collective-permute-start.5 = (bf16[96,768]{1,0:T(8,128)(2,1)S(1)}, bf16[96,768]{1,0:T(8,128)(2,1)S(1)}, u32[]{:S(2)}, u32[]{:S(2)}) collective-permute-start(bf16[96,768]{1,0:T(8,128)(2,1)S(1)} %join.3.packed_ref), channel_id=1, source_target_pairs={{0,1},{1,0},{2,3},{3,2},{4,5},{5,4},{6,7},{7,6},{8,9},{9,8},{10,11... | collective-permute-start | bytes 442376 | tf_op jit(solution)/shard_map/ppermute | solution.py:363
  17.3 3.8 %collective-permute-start.6 = (f32[8,512]{1,0:T(8,128)S(1)}, f32[8,512]{1,0:T(8,128)S(1)}, u32[]{:S(2)}, u32[]{:S(2)}) collective-permute-start(f32[8,512]{1,0:T(8,128)S(1)} %score_bank.1.refs_8_), channel_id=1, source_target_pairs={{0,16},{16,0},{1,17},{17,1},{2,18},{18,2},{3,19},{19,3},{4,20},{20... | collective-permute-start | bytes 49160 | tf_op jit(solution)/shard_map/ppermute | solution.py:363

commit v7 on v6

--- a/solution.py
+++ b/solution.py
@@ -299,10 +299,8 @@
 
 def finish_kernel(sums_ref, spread_ref, out_ref):
     depth = out_ref.shape[1]
-    sums = jnp.concatenate([sums_ref[s].astype(jnp.float32) for s in range(sums_ref.shape[0])], axis=0)
-    sums = jnp.dot(
-        spread_ref[...].astype(jnp.bfloat16), sums.astype(jnp.bfloat16), preferred_element_type=jnp.float32
-    )
+    sums = sums_ref[...].reshape(sums_ref.shape[0] * CAP, sums_ref.shape[2])
+    sums = jnp.dot(spread_ref[...].astype(jnp.bfloat16), sums, preferred_element_type=jnp.float32)
     out_ref[...] = sums[:, :depth] / (sums[:, depth : depth + 1] + sums[:, depth + 1 : depth + 2])
 
 

time: 33 us -> 33 us (level)
  no operation moved by 1% of the time
where the time goes in v7:
time: 33 us; the launch traced here: 32.8 us
  blocking collectives  9.65 us (29%)
  Pallas kernels  9.32 us (28%)
  starting transfers between devices  8.52 us (26%)
  waiting for transfers between devices  5.23 us (16%)
    all_to_all x1, blocking collectives, body(): sums = lax.all_to_all(sums, 'gal', 0, 0, tiled=True)  9.65 us
    ppermute x7, starting transfers between devices, swap(): return lax.ppermute(value, axis, [(i, i ^ bit) for i in range(size)])  8.52 us
    ppermute x7, waiting for transfers between devices, swap(): return lax.ppermute(value, axis, [(i, i ^ bit) for i in range(size)])  5.23 us
    pallas_call x1, Pallas kernels, load_low(): pl.pallas_call(low_kernel, out_shape=(rows_shape(gallery, PARTS[0]), *par...  2.36 us
    pallas_call x1, Pallas kernels, load_more(): pl.pallas_call(more_kernel, out_shape=(rows_shape(gallery, parts), *part_...  2.01 us
    pallas_call x1, Pallas kernels, score_tests(): pl.pallas_call(functools.partial(test_kernel, order, bank_rows), out_shap...  1.54 us
    pallas_call x1, Pallas kernels, pool(): pl.pallas_call(functools.partial(pool_kernel, order), out_shape=pltpu.VME...  1.19 us
    pallas_call x1, Pallas kernels, score_bank(): pl.pallas_call(functools.partial(bank_kernel, bank_rows), out_shape=pltpu...  1.06 us
  transfers between devices with their start and end apart: 7, of which 5 were waited for; matrix products, arithmetic and copies ran while one was open for 0% of the time, Pallas kernels for 19%

profile of v7, /device:TPU:0, one launch (start us, length us, event | category | flops | bytes accessed | tf_op | source)
XLA Modules:
  0.0 32.8 jit_solution(10670607990314661639)
XLA Ops:
  0.0 3.5 %collective-permute-start = (bf16[8,768]{1,0:T(8,128)(2,1)}, bf16[8,768]{1,0:T(8,128)(2,1)S(1)}, u32[]{:S(2)}, u32[]{:S(2)}) collective-permute-start(bf16[8,768]{1,0:T(8,128)(2,1)} %bank_hbm.1), channel_id=1, source_target_pairs={{0,9},{1,8},{2,11},{3,10},{4,13},{5,12},{6,15},{7,14},{8,1},{9,0},... | collective-permute-start | bytes 36872 | tf_op jit(solution)/shard_map/ppermute | solution.py:361
  3.5 0.0 collective-permute-start.1
  3.5 2.4 %load_low.1 = (bf16[2048,768]{1,0:T(8,128)(2,1)S(1)}, bf16[768,2048]{1,0:T(8,128)(2,1)S(1)}, f32[4,512]{1,0:T(4,128)S(1)}, bf16[8,768]{1,0:T(8,128)(2,1)S(1)}, b...) custom-call(bf16[4096,768]{1,0:T(8,128)(2,1)} %gallery_hbm.3, bf16[8,768]{1,0:T(8,128)(2,1)} %bank_hbm.1, ...), custom_call_target="tpu_custom_call" | custom-call | tf_op jit(solution)/shard_map/load_low/pallas_call | solution.py:145
  5.9 1.8 %collective-permute-done.1.refs_3_ = bf16[4,768]{1,0:T(4,128)(2,1)S(1)} collective-permute-done((bf16[4,768]{1,0:T(4,128)(2,1)}, bf16[4,768]{1,0:T(4,128)(2,1)S(1)}, u32[]{:S(2)}, u32[]{:S(2)}) %collective-permute-start.1) | collective-permute-done | bytes 6176 | tf_op jit(solution)/shard_map/ppermute | solution.py:361
  7.6 0.0 collective-permute-done.refs_1_
  7.7 1.6 %collective-permute-start.4 = (bf16[24,768]{1,0:T(8,128)(2,1)S(1)}, bf16[24,768]{1,0:T(8,128)(2,1)S(1)}, u32[]{:S(2)}, u32[]{:S(2)}) collective-permute-start(bf16[24,768]{1,0:T(8,128)(2,1)S(1)} %join.2.packed_ref), channel_id=1, source_target_pairs={{0,4},{1,5},{2,6},{3,7},{4,0},{5,1},{6,2},{7,3},{8,12},{9,13},{10,... | collective-permute-start | bytes 110600 | tf_op jit(solution)/shard_map/ppermute | solution.py:361
  9.3 1.4 %collective-permute-start.3 = (bf16[24,768]{1,0:T(8,128)(2,1)S(1)}, bf16[24,768]{1,0:T(8,128)(2,1)S(1)}, u32[]{:S(2)}, u32[]{:S(2)}) collective-permute-start(bf16[24,768]{1,0:T(8,128)(2,1)S(1)} %join.2.packed_ref), channel_id=1, source_target_pairs={{0,7},{1,6},{2,5},{3,4},{4,3},{5,2},{6,1},{7,0},{8,15},{9,14},{10,... | collective-permute-start | bytes 110600 | tf_op jit(solution)/shard_map/ppermute | solution.py:361
  10.7 0.2 collective-permute-start.2
  10.9 2.0 %load_more.1 = (bf16[2048,768]{1,0:T(8,128)(2,1)S(1)}, bf16[768,1536]{1,0:T(8,128)(2,1)S(1)}, f32[3,512]{1,0:T(4,128)S(1)}, bf16[24,768]{1,0:T(8,128)(2,1)S(1)}) custom-call(bf16[4096,768]{1,0:T(8,128)(2,1)} %gallery_hbm.3, bf16[24,768]{1,0:T(8,128)(2,1)S(1)} %join.2.packed_ref), custom_call_target="tpu_custom_call" | custom-call | tf_op jit(solution)/shard_map/load_more/pallas_call | solution.py:158
  12.9 0.0 collective-permute-done.4.refs_3_
  13.0 0.6 %collective-permute-done.3.refs_2_ = bf16[24,768]{1,0:T(8,128)(2,1)S(1)} collective-permute-done((bf16[24,768]{1,0:T(8,128)(2,1)S(1)}, bf16[24,768]{1,0:T(8,128)(2,1)S(1)}, u32[]{:S(2)}, u32[]{:S(2)}) %collective-permute-start.3) | collective-permute-done | bytes 36896 | tf_op jit(solution)/shard_map/ppermute | solution.py:361
  13.6 1.2 %collective-permute-done.2.refs_1_ = bf16[24,768]{1,0:T(8,128)(2,1)S(1)} collective-permute-done((bf16[24,768]{1,0:T(8,128)(2,1)S(1)}, bf16[24,768]{1,0:T(8,128)(2,1)S(1)}, u32[]{:S(2)}, u32[]{:S(2)}) %collective-permute-start.2) | collective-permute-done | bytes 36896 | tf_op jit(solution)/shard_map/ppermute | solution.py:361
  14.8 0.2 collective-permute-start.5
  14.9 0.3 turn_last.1
  15.2 1.0 %collective-permute-done.5.second_ref = bf16[96,768]{1,0:T(8,128)(2,1)S(1)} collective-permute-done((bf16[96,768]{1,0:T(8,128)(2,1)S(1)}, bf16[96,768]{1,0:T(8,128)(2,1)S(1)}, u32[]{:S(2)}, u32[]{:S(2)}) %collective-permute-start.5) | collective-permute-done | bytes 147488 | tf_op jit(solution)/shard_map/ppermute | solution.py:361
  16.2 1.1 %score_bank.1.refs_8_ = f32[8,512]{1,0:T(8,128)S(1)} custom-call(bf16[96,768]{1,0:T(8,128)(2,1)S(1)} %get-tuple-element.27.first_ref, bf16[96,768]{1,0:T(8,128)(2,1)S(1)} %collective-permute-done.5.second_ref, bf16[768,2048]{1,0:T(8,128)(2,1)S(1)} %get-tuple-element.28.refs_0_, bf16[768,1536]{1,0:T(8,128)(2,1)S(1)} %get-tuple-element.29.refs_1_, ...), custom_call_target="tpu_custom_call" | custom-call | tf_op jit(solution)/shard_map/score_bank/pallas_call | solution.py:207
  17.3 1.6 %collective-permute-start.6 = (f32[8,512]{1,0:T(8,128)S(1)}, f32[8,512]{1,0:T(8,128)S(1)}, u32[]{:S(2)}, u32[]{:S(2)}) collective-permute-start(f32[8,512]{1,0:T(8,128)S(1)} %score_bank.1.refs_8_), channel_id=1, source_target_pairs={{0,16},{16,0},{1,17},{17,1},{2,18},{18,2},{3,19},{19,3},{4,20},{20... | collective-permute-start | bytes 49160 | tf_op jit(solution)/shard_map/ppermute | solution.py:361
  18.8 1.5 %score_tests.1 = (f32[32,128]{1,0:T(8,128)S(1)}, s32[32,128]{1,0:T(8,128)S(1)}, f32[4,32]{1,0:T(4,128)S(1)}, f32[8,512]{1,0:T(8,128)S(1)}) custom-call(bf16[96,768]{1,0:T(8,128)(2,1)S(1)} %get-tuple-element.27.first_ref, bf16[96,768]{1,0:T(8,128)(2,1)S(1)} %collective-permute-done.5.second_ref, bf16[768,2048]{1,0:T(8,128)(2,1)S(1)} %get-tuple-element.28.refs_0_, ...), custom_call_target="tpu_custom_call" | custom-call | tf_op jit(solution)/shard_map/score_tests/pallas_call | solution.py:239
  20.4 0.7 %collective-permute-done.6.other_ref = f32[8,512]{1,0:T(8,128)S(1)} collective-permute-done((f32[8,512]{1,0:T(8,128)S(1)}, f32[8,512]{1,0:T(8,128)S(1)}, u32[]{:S(2)}, u32[]{:S(2)}) %collective-permute-start.6) | collective-permute-done | bytes 16416 | tf_op jit(solution)/shard_map/ppermute | solution.py:361
  21.1 1.2 %pool.1 = bf16[16,2,896]{2,1,0:T(2,128)(2,1)S(1)} custom-call(f32[32,128]{1,0:T(8,128)S(1)} %get-tuple-element.36.listed_ref, f32[8,512]{1,0:T(8,128)S(1)} %get-tuple-element.37.own_ref, f32[8,512]{1,0:T(8,128)S(1)} %collective-permute-done.6.other_ref, s32[32,128]{1,0:T(8,128)S(1)} %get-tuple-element.38.block_ref, ...), custom_call_target="tpu_custom_call" | custom-call | tf_op jit(solution)/shard_map/pool/pallas_call | solution.py:289
  22.3 9.6 %all_to_all.5.sums_ref = bf16[16,2,896]{2,1,0:T(2,128)(2,1)S(1)} all-to-all(bf16[16,2,896]{2,1,0:T(2,128)(2,1)S(1)} %pool.1), channel_id=1, replica_groups=mesh['bank'=2,'gal'=16] {'gal'}, dimensions={0} | all-to-all | bytes 114688 | tf_op jit(solution)/shard_map/all_to_all | solution.py:403
  31.9 0.9 %finish.1 = f32[4,768]{1,0:T(4,128)} custom-call(bf16[16,2,896]{2,1,0:T(2,128)(2,1)S(1)} %all_to_all.5.sums_ref, f32[4,32]{1,0:T(4,128)S(1)} %get-tuple-element.40.spread_ref), custom_call_target="tpu_custom_call" | custom-call | tf_op jit(solution)/shard_map/finish/pallas_call | solution.py:308
  (2 shorter events, 0.0 us)
Async XLA Ops:
  0.0 7.6 %collective-permute-start = (bf16[8,768]{1,0:T(8,128)(2,1)}, bf16[8,768]{1,0:T(8,128)(2,1)S(1)}, u32[]{:S(2)}, u32[]{:S(2)}) collective-permute-start(bf16[8,768]{1,0:T(8,128)(2,1)} %bank_hbm.1), channel_id=1, source_target_pairs={{0,9},{1,8},{2,11},{3,10},{4,13},{5,12},{6,15},{7,14},{8,1},{9,0},... | collective-permute-start | bytes 36872 | tf_op jit(solution)/shard_map/ppermute | solution.py:361
  3.5 4.2 %collective-permute-start.1 = (bf16[4,768]{1,0:T(4,128)(2,1)}, bf16[4,768]{1,0:T(4,128)(2,1)S(1)}, u32[]{:S(2)}, u32[]{:S(2)}) collective-permute-start(bf16[4,768]{1,0:T(4,128)(2,1)} %test_hbm.1), channel_id=1, source_target_pairs={{0,9},{1,8},{2,11},{3,10},{4,13},{5,12},{6,15},{7,14},{8,1},{9,0},... | collective-permute-start | bytes 18440 | tf_op jit(solution)/shard_map/ppermute | solution.py:361
  7.7 5.3 %collective-permute-start.4 = (bf16[24,768]{1,0:T(8,128)(2,1)S(1)}, bf16[24,768]{1,0:T(8,128)(2,1)S(1)}, u32[]{:S(2)}, u32[]{:S(2)}) collective-permute-start(bf16[24,768]{1,0:T(8,128)(2,1)S(1)} %join.2.packed_ref), channel_id=1, source_target_pairs={{0,4},{1,5},{2,6},{3,7},{4,0},{5,1},{6,2},{7,3},{8,12},{9,13},{10,... | collective-permute-start | bytes 110600 | tf_op jit(solution)/shard_map/ppermute | solution.py:361
  9.3 4.3 %collective-permute-start.3 = (bf16[24,768]{1,0:T(8,128)(2,1)S(1)}, bf16[24,768]{1,0:T(8,128)(2,1)S(1)}, u32[]{:S(2)}, u32[]{:S(2)}) collective-permute-start(bf16[24,768]{1,0:T(8,128)(2,1)S(1)} %join.2.packed_ref), channel_id=1, source_target_pairs={{0,7},{1,6},{2,5},{3,4},{4,3},{5,2},{6,1},{7,0},{8,15},{9,14},{10,... | collective-permute-start | bytes 110600 | tf_op jit(solution)/shard_map/ppermute | solution.py:361
  10.7 4.0 %collective-permute-start.2 = (bf16[24,768]{1,0:T(8,128)(2,1)S(1)}, bf16[24,768]{1,0:T(8,128)(2,1)S(1)}, u32[]{:S(2)}, u32[]{:S(2)}) collective-permute-start(bf16[24,768]{1,0:T(8,128)(2,1)S(1)} %join.2.packed_ref), channel_id=1, source_target_pairs={{0,3},{1,2},{2,1},{3,0},{4,7},{5,6},{6,5},{7,4},{8,11},{9,10},{10,... | collective-permute-start | bytes 110600 | tf_op jit(solution)/shard_map/ppermute | solution.py:361
  14.8 1.4 %collective-permute-start.5 = (bf16[96,768]{1,0:T(8,128)(2,1)S(1)}, bf16[96,768]{1,0:T(8,128)(2,1)S(1)}, u32[]{:S(2)}, u32[]{:S(2)}) collective-permute-start(bf16[96,768]{1,0:T(8,128)(2,1)S(1)} %join.3.packed_ref), channel_id=1, source_target_pairs={{0,1},{1,0},{2,3},{3,2},{4,5},{5,4},{6,7},{7,6},{8,9},{9,8},{10,11... | collective-permute-start | bytes 442376 | tf_op jit(solution)/shard_map/ppermute | solution.py:361
  17.3 3.8 %collective-permute-start.6 = (f32[8,512]{1,0:T(8,128)S(1)}, f32[8,512]{1,0:T(8,128)S(1)}, u32[]{:S(2)}, u32[]{:S(2)}) collective-permute-start(f32[8,512]{1,0:T(8,128)S(1)} %score_bank.1.refs_8_), channel_id=1, source_target_pairs={{0,16},{16,0},{1,17},{17,1},{2,18},{18,2},{3,19},{19,3},{4,20},{20... | collective-permute-start | bytes 49160 | tf_op jit(solution)/shard_map/ppermute | solution.py:361

commit v8 on v7

--- a/solution.py
+++ b/solution.py
@@ -103,9 +103,10 @@
 ):
     pairs = ((bank_hbm, bank_ref), (test_hbm, test_ref), (slabs_hbm, slabs_ref), (offsets_hbm, offsets_ref))
     small = [pltpu.make_async_copy(*pair, small_sems.at[i]) for i, pair in enumerate(pairs)]
+    copies = fetch(gallery_hbm, 0, gallery_ref, sems)
     for copy in small:
         copy.start()
-    for c, copy in enumerate(fetch(gallery_hbm, 0, gallery_ref, sems)):
+    for c, copy in enumerate(copies):
         copy.wait()
         turn(c, c, gallery_ref, turned_ref, scale_ref)
     for copy in small:

time: 33 us -> 33 us (level)
  no operation moved by 1% of the time
where the time goes in v8:
time: 33 us; the launch traced here: 32.8 us
  blocking collectives  9.64 us (29%)
  Pallas kernels  9.3 us (28%)
  starting transfers between devices  8.52 us (26%)
  waiting for transfers between devices  5.25 us (16%)
    all_to_all x1, blocking collectives, body(): sums = lax.all_to_all(sums, 'gal', 0, 0, tiled=True)  9.64 us
    ppermute x7, starting transfers between devices, swap(): return lax.ppermute(value, axis, [(i, i ^ bit) for i in range(size)])  8.52 us
    ppermute x7, waiting for transfers between devices, swap(): return lax.ppermute(value, axis, [(i, i ^ bit) for i in range(size)])  5.25 us
    pallas_call x1, Pallas kernels, load_low(): pl.pallas_call(low_kernel, out_shape=(rows_shape(gallery, PARTS[0]), *par...  2.34 us
    pallas_call x1, Pallas kernels, load_more(): pl.pallas_call(more_kernel, out_shape=(rows_shape(gallery, parts), *part_...  2.01 us
    pallas_call x1, Pallas kernels, score_tests(): pl.pallas_call(functools.partial(test_kernel, order, bank_rows), out_shap...  1.54 us
    pallas_call x1, Pallas kernels, pool(): pl.pallas_call(functools.partial(pool_kernel, order), out_shape=pltpu.VME...  1.19 us
    pallas_call x1, Pallas kernels, score_bank(): pl.pallas_call(functools.partial(bank_kernel, bank_rows), out_shape=pltpu...  1.06 us
  transfers between devices with their start and end apart: 7, of which 5 were waited for; matrix products, arithmetic and copies ran while one was open for 0% of the time, Pallas kernels for 19%

profile of v8, /device:TPU:0, one launch (start us, length us, event | category | flops | bytes accessed | tf_op | source)
XLA Modules:
  0.0 32.8 jit_solution(8134081178731675456)
XLA Ops:
  0.0 3.5 %collective-permute-start = (bf16[8,768]{1,0:T(8,128)(2,1)}, bf16[8,768]{1,0:T(8,128)(2,1)S(1)}, u32[]{:S(2)}, u32[]{:S(2)}) collective-permute-start(bf16[8,768]{1,0:T(8,128)(2,1)} %bank_hbm.1), channel_id=1, source_target_pairs={{0,9},{1,8},{2,11},{3,10},{4,13},{5,12},{6,15},{7,14},{8,1},{9,0},... | collective-permute-start | bytes 36872 | tf_op jit(solution)/shard_map/ppermute | solution.py:362
  3.5 0.0 collective-permute-start.1
  3.5 2.3 %load_low.1 = (bf16[2048,768]{1,0:T(8,128)(2,1)S(1)}, bf16[768,2048]{1,0:T(8,128)(2,1)S(1)}, f32[4,512]{1,0:T(4,128)S(1)}, bf16[8,768]{1,0:T(8,128)(2,1)S(1)}, b...) custom-call(bf16[4096,768]{1,0:T(8,128)(2,1)} %gallery_hbm.3, bf16[8,768]{1,0:T(8,128)(2,1)} %bank_hbm.1, ...), custom_call_target="tpu_custom_call" | custom-call | tf_op jit(solution)/shard_map/load_low/pallas_call | solution.py:146
  5.9 1.8 %collective-permute-done.1.refs_3_ = bf16[4,768]{1,0:T(4,128)(2,1)S(1)} collective-permute-done((bf16[4,768]{1,0:T(4,128)(2,1)}, bf16[4,768]{1,0:T(4,128)(2,1)S(1)}, u32[]{:S(2)}, u32[]{:S(2)}) %collective-permute-start.1) | collective-permute-done | bytes 6176 | tf_op jit(solution)/shard_map/ppermute | solution.py:362
  7.6 0.0 collective-permute-done.refs_1_
  7.7 1.6 %collective-permute-start.4 = (bf16[24,768]{1,0:T(8,128)(2,1)S(1)}, bf16[24,768]{1,0:T(8,128)(2,1)S(1)}, u32[]{:S(2)}, u32[]{:S(2)}) collective-permute-start(bf16[24,768]{1,0:T(8,128)(2,1)S(1)} %join.2.packed_ref), channel_id=1, source_target_pairs={{0,4},{1,5},{2,6},{3,7},{4,0},{5,1},{6,2},{7,3},{8,12},{9,13},{10,... | collective-permute-start | bytes 110600 | tf_op jit(solution)/shard_map/ppermute | solution.py:362
  9.3 1.4 %collective-permute-start.3 = (bf16[24,768]{1,0:T(8,128)(2,1)S(1)}, bf16[24,768]{1,0:T(8,128)(2,1)S(1)}, u32[]{:S(2)}, u32[]{:S(2)}) collective-permute-start(bf16[24,768]{1,0:T(8,128)(2,1)S(1)} %join.2.packed_ref), channel_id=1, source_target_pairs={{0,7},{1,6},{2,5},{3,4},{4,3},{5,2},{6,1},{7,0},{8,15},{9,14},{10,... | collective-permute-start | bytes 110600 | tf_op jit(solution)/shard_map/ppermute | solution.py:362
  10.7 0.2 collective-permute-start.2
  10.9 2.0 %load_more.1 = (bf16[2048,768]{1,0:T(8,128)(2,1)S(1)}, bf16[768,1536]{1,0:T(8,128)(2,1)S(1)}, f32[3,512]{1,0:T(4,128)S(1)}, bf16[24,768]{1,0:T(8,128)(2,1)S(1)}) custom-call(bf16[4096,768]{1,0:T(8,128)(2,1)} %gallery_hbm.3, bf16[24,768]{1,0:T(8,128)(2,1)S(1)} %join.2.packed_ref), custom_call_target="tpu_custom_call" | custom-call | tf_op jit(solution)/shard_map/load_more/pallas_call | solution.py:159
  12.9 0.0 collective-permute-done.4.refs_3_
  13.0 0.6 %collective-permute-done.3.refs_2_ = bf16[24,768]{1,0:T(8,128)(2,1)S(1)} collective-permute-done((bf16[24,768]{1,0:T(8,128)(2,1)S(1)}, bf16[24,768]{1,0:T(8,128)(2,1)S(1)}, u32[]{:S(2)}, u32[]{:S(2)}) %collective-permute-start.3) | collective-permute-done | bytes 36896 | tf_op jit(solution)/shard_map/ppermute | solution.py:362
  13.6 1.2 %collective-permute-done.2.refs_1_ = bf16[24,768]{1,0:T(8,128)(2,1)S(1)} collective-permute-done((bf16[24,768]{1,0:T(8,128)(2,1)S(1)}, bf16[24,768]{1,0:T(8,128)(2,1)S(1)}, u32[]{:S(2)}, u32[]{:S(2)}) %collective-permute-start.2) | collective-permute-done | bytes 36896 | tf_op jit(solution)/shard_map/ppermute | solution.py:362
  14.8 0.2 collective-permute-start.5
  14.9 0.3 turn_last.1
  15.2 1.0 %collective-permute-done.5.second_ref = bf16[96,768]{1,0:T(8,128)(2,1)S(1)} collective-permute-done((bf16[96,768]{1,0:T(8,128)(2,1)S(1)}, bf16[96,768]{1,0:T(8,128)(2,1)S(1)}, u32[]{:S(2)}, u32[]{:S(2)}) %collective-permute-start.5) | collective-permute-done | bytes 147488 | tf_op jit(solution)/shard_map/ppermute | solution.py:362
  16.2 1.1 %score_bank.1.refs_8_ = f32[8,512]{1,0:T(8,128)S(1)} custom-call(bf16[96,768]{1,0:T(8,128)(2,1)S(1)} %get-tuple-element.27.first_ref, bf16[96,768]{1,0:T(8,128)(2,1)S(1)} %collective-permute-done.5.second_ref, bf16[768,2048]{1,0:T(8,128)(2,1)S(1)} %get-tuple-element.28.refs_0_, bf16[768,1536]{1,0:T(8,128)(2,1)S(1)} %get-tuple-element.29.refs_1_, ...), custom_call_target="tpu_custom_call" | custom-call | tf_op jit(solution)/shard_map/score_bank/pallas_call | solution.py:208
  17.3 1.6 %collective-permute-start.6 = (f32[8,512]{1,0:T(8,128)S(1)}, f32[8,512]{1,0:T(8,128)S(1)}, u32[]{:S(2)}, u32[]{:S(2)}) collective-permute-start(f32[8,512]{1,0:T(8,128)S(1)} %score_bank.1.refs_8_), channel_id=1, source_target_pairs={{0,16},{16,0},{1,17},{17,1},{2,18},{18,2},{3,19},{19,3},{4,20},{20... | collective-permute-start | bytes 49160 | tf_op jit(solution)/shard_map/ppermute | solution.py:362
  18.8 1.5 %score_tests.1 = (f32[32,128]{1,0:T(8,128)S(1)}, s32[32,128]{1,0:T(8,128)S(1)}, f32[4,32]{1,0:T(4,128)S(1)}, f32[8,512]{1,0:T(8,128)S(1)}) custom-call(bf16[96,768]{1,0:T(8,128)(2,1)S(1)} %get-tuple-element.27.first_ref, bf16[96,768]{1,0:T(8,128)(2,1)S(1)} %collective-permute-done.5.second_ref, bf16[768,2048]{1,0:T(8,128)(2,1)S(1)} %get-tuple-element.28.refs_0_, ...), custom_call_target="tpu_custom_call" | custom-call | tf_op jit(solution)/shard_map/score_tests/pallas_call | solution.py:240
  20.4 0.7 %collective-permute-done.6.other_ref = f32[8,512]{1,0:T(8,128)S(1)} collective-permute-done((f32[8,512]{1,0:T(8,128)S(1)}, f32[8,512]{1,0:T(8,128)S(1)}, u32[]{:S(2)}, u32[]{:S(2)}) %collective-permute-start.6) | collective-permute-done | bytes 16416 | tf_op jit(solution)/shard_map/ppermute | solution.py:362
  21.1 1.2 %pool.1 = bf16[16,2,896]{2,1,0:T(2,128)(2,1)S(1)} custom-call(f32[32,128]{1,0:T(8,128)S(1)} %get-tuple-element.36.listed_ref, f32[8,512]{1,0:T(8,128)S(1)} %get-tuple-element.37.own_ref, f32[8,512]{1,0:T(8,128)S(1)} %collective-permute-done.6.other_ref, s32[32,128]{1,0:T(8,128)S(1)} %get-tuple-element.38.block_ref, ...), custom_call_target="tpu_custom_call" | custom-call | tf_op jit(solution)/shard_map/pool/pallas_call | solution.py:290
  22.3 9.6 %all_to_all.5.sums_ref = bf16[16,2,896]{2,1,0:T(2,128)(2,1)S(1)} all-to-all(bf16[16,2,896]{2,1,0:T(2,128)(2,1)S(1)} %pool.1), channel_id=1, replica_groups=mesh['bank'=2,'gal'=16] {'gal'}, dimensions={0} | all-to-all | bytes 114688 | tf_op jit(solution)/shard_map/all_to_all | solution.py:404
  31.9 0.9 %finish.1 = f32[4,768]{1,0:T(4,128)} custom-call(bf16[16,2,896]{2,1,0:T(2,128)(2,1)S(1)} %all_to_all.5.sums_ref, f32[4,32]{1,0:T(4,128)S(1)} %get-tuple-element.40.spread_ref), custom_call_target="tpu_custom_call" | custom-call | tf_op jit(solution)/shard_map/finish/pallas_call | solution.py:309
  (2 shorter events, 0.0 us)
Async XLA Ops:
  0.0 7.6 %collective-permute-start = (bf16[8,768]{1,0:T(8,128)(2,1)}, bf16[8,768]{1,0:T(8,128)(2,1)S(1)}, u32[]{:S(2)}, u32[]{:S(2)}) collective-permute-start(bf16[8,768]{1,0:T(8,128)(2,1)} %bank_hbm.1), channel_id=1, source_target_pairs={{0,9},{1,8},{2,11},{3,10},{4,13},{5,12},{6,15},{7,14},{8,1},{9,0},... | collective-permute-start | bytes 36872 | tf_op jit(solution)/shard_map/ppermute | solution.py:362
  3.5 4.2 %collective-permute-start.1 = (bf16[4,768]{1,0:T(4,128)(2,1)}, bf16[4,768]{1,0:T(4,128)(2,1)S(1)}, u32[]{:S(2)}, u32[]{:S(2)}) collective-permute-start(bf16[4,768]{1,0:T(4,128)(2,1)} %test_hbm.1), channel_id=1, source_target_pairs={{0,9},{1,8},{2,11},{3,10},{4,13},{5,12},{6,15},{7,14},{8,1},{9,0},... | collective-permute-start | bytes 18440 | tf_op jit(solution)/shard_map/ppermute | solution.py:362
  7.7 5.3 %collective-permute-start.4 = (bf16[24,768]{1,0:T(8,128)(2,1)S(1)}, bf16[24,768]{1,0:T(8,128)(2,1)S(1)}, u32[]{:S(2)}, u32[]{:S(2)}) collective-permute-start(bf16[24,768]{1,0:T(8,128)(2,1)S(1)} %join.2.packed_ref), channel_id=1, source_target_pairs={{0,4},{1,5},{2,6},{3,7},{4,0},{5,1},{6,2},{7,3},{8,12},{9,13},{10,... | collective-permute-start | bytes 110600 | tf_op jit(solution)/shard_map/ppermute | solution.py:362
  9.3 4.3 %collective-permute-start.3 = (bf16[24,768]{1,0:T(8,128)(2,1)S(1)}, bf16[24,768]{1,0:T(8,128)(2,1)S(1)}, u32[]{:S(2)}, u32[]{:S(2)}) collective-permute-start(bf16[24,768]{1,0:T(8,128)(2,1)S(1)} %join.2.packed_ref), channel_id=1, source_target_pairs={{0,7},{1,6},{2,5},{3,4},{4,3},{5,2},{6,1},{7,0},{8,15},{9,14},{10,... | collective-permute-start | bytes 110600 | tf_op jit(solution)/shard_map/ppermute | solution.py:362
  10.7 4.0 %collective-permute-start.2 = (bf16[24,768]{1,0:T(8,128)(2,1)S(1)}, bf16[24,768]{1,0:T(8,128)(2,1)S(1)}, u32[]{:S(2)}, u32[]{:S(2)}) collective-permute-start(bf16[24,768]{1,0:T(8,128)(2,1)S(1)} %join.2.packed_ref), channel_id=1, source_target_pairs={{0,3},{1,2},{2,1},{3,0},{4,7},{5,6},{6,5},{7,4},{8,11},{9,10},{10,... | collective-permute-start | bytes 110600 | tf_op jit(solution)/shard_map/ppermute | solution.py:362
  14.8 1.4 %collective-permute-start.5 = (bf16[96,768]{1,0:T(8,128)(2,1)S(1)}, bf16[96,768]{1,0:T(8,128)(2,1)S(1)}, u32[]{:S(2)}, u32[]{:S(2)}) collective-permute-start(bf16[96,768]{1,0:T(8,128)(2,1)S(1)} %join.3.packed_ref), channel_id=1, source_target_pairs={{0,1},{1,0},{2,3},{3,2},{4,5},{5,4},{6,7},{7,6},{8,9},{9,8},{10,11... | collective-permute-start | bytes 442376 | tf_op jit(solution)/shard_map/ppermute | solution.py:362
  17.3 3.8 %collective-permute-start.6 = (f32[8,512]{1,0:T(8,128)S(1)}, f32[8,512]{1,0:T(8,128)S(1)}, u32[]{:S(2)}, u32[]{:S(2)}) collective-permute-start(f32[8,512]{1,0:T(8,128)S(1)} %score_bank.1.refs_8_), channel_id=1, source_target_pairs={{0,16},{16,0},{1,17},{17,1},{2,18},{18,2},{3,19},{19,3},{4,20},{20... | collective-permute-start | bytes 49160 | tf_op jit(solution)/shard_map/ppermute | solution.py:362
